TPU v7x, 32 devices: a whole 2x2x4 slice. The times are simulated.
32 devices in a mesh: grp: 4 (over z), dev: 8 (over y, x, core).
Axes of the slice: x: 2, y: 2, z: 4, core: 2. Of those that a mesh axis runs over, the one named last changes fastest.
Arguments:
- output_gradient: bfloat16 [4096, 2048], P(('grp', 'dev')), may hold values from -6 to 6
- expert_choice_index: int32 [4096, 8], P(('grp', 'dev')), may hold values from 0 to 31, all different within a row; in each aligned block of 128 rows (0 to 127, 128 to 255, ...) at most 40 rows name the same one
- routing_weight: float32 [4096, 8], P(('grp', 'dev')), may hold values from 0.05 to 0.3
- stored_gate_preact: bfloat16 [32, 1280, 1536], P(('grp', 'dev')), may hold values from -6 to 6
- gate_up_weight: bfloat16 [32, 2048, 1536], P(('grp', 'dev')), may hold values from -0.125 to 0.125
- down_weight: bfloat16 [32, 768, 2048], P(('grp', 'dev')), may hold values from -0.21875 to 0.21875
- down_first_factor: bfloat16 [32, 64, 768], P(('grp', 'dev')), may hold values from -0.21875 to 0.21875
- down_second_factor: bfloat16 [32, 64, 2048], P(('grp', 'dev')), may hold values from -0.75 to 0.75
- rotated_queries: bfloat16 [4096, 4096], P('grp', 'dev'), may hold values from -800 to 800
- rotated_keys: bfloat16 [4096, 512], P('grp'), may hold values from -4 to 4
- stored_values: bfloat16 [4096, 512], P('grp'), may hold values from -6 to 6
- output_weight: bfloat16 [4096, 2048], P('dev'), may hold values from -0.09375 to 0.09375
- output_first_factor: bfloat16 [64, 4096], P(None, 'dev'), may hold values from -0.09375 to 0.09375
- output_second_factor: bfloat16 [64, 2048], replicated, may hold values from -0.75 to 0.75
Outputs:
- first_factor_gradient: float32 [32, 64, 768], P(('grp', 'dev'))
- second_factor_gradient: float32 [32, 64, 2048], P(('grp', 'dev'))
- residual_gradient: bfloat16 [4096, 2048], P(('grp', 'dev'))
- output_first_gradient: float32 [64, 4096], P(None, 'dev')
- output_second_gradient: float32 [64, 2048], replicated
- query_gradient: float32 [4096, 4096], P('grp', 'dev')
- key_gradient: float32 [4096, 512], P(('grp', 'dev'))
- value_gradient: float32 [4096, 512], P(('grp', 'dev'))
Inputs may be any that keep to these rules, and one draw needn't show every extreme that they name: `expert_choice_index`: each row names 8 different experts; within the rows of one device no expert is named more than 40 times, a bound that some block reaches.
All inputs are finite; a program needn't handle non-finite values.
Results may differ from a plain program's by a relative error of at most 0.024.
Values may be sent and summed in bfloat16 or wider, within the bound.
No kernel may reach another device: no remote copies, remote signals or barrier semaphores. Data moves between devices by JAX's collectives and lax.ppermute only.
A program may use at most 192 MiB of HBM per device.

v0:
```python
import jax
import jax.numpy as jnp
from jax import lax
from jax.sharding import PartitionSpec as P

QUERY_HEADS = 32
KVH = 4
HEAD_SIZE = 128


adapter_scale = 2.0
neg_big = -1e30


def contraction(left, right, left_dim, right_dim):
    return lax.dot_general(
        left, right, (((left_dim,), (right_dim,)), ((), ())), preferred_element_type=jnp.float32
    )


def expert_backward(routed_rows, saved_rows, gate_up, down_output, lowrank_first, low_b):
    width_ff = down_output.shape[0]
    pre_gate = saved_rows[:, :width_ff].astype(jnp.float32)
    pre_up = saved_rows[:, width_ff:].astype(jnp.float32)
    sigmoid = jax.nn.sigmoid(pre_gate)
    activated = pre_gate * sigmoid
    slope = sigmoid * (1.0 + pre_gate * (1.0 - sigmoid))
    hidden_activity = (activated * pre_up).astype(jnp.bfloat16)
    lowrank_input = contraction(hidden_activity, lowrank_first, 1, 1).astype(jnp.bfloat16)
    lowrank_gradient = contraction(routed_rows, low_b, 1, 1).astype(jnp.bfloat16)
    gradient_second = adapter_scale * contraction(lowrank_input, routed_rows, 0, 0)
    gradient_first = adapter_scale * contraction(lowrank_gradient, hidden_activity, 0, 0)
    hidden_gradient = contraction(routed_rows, down_output, 1, 1) + adapter_scale * jnp.dot(
        lowrank_gradient, lowrank_first, preferred_element_type=jnp.float32
    )
    grad_pre = jnp.concatenate(
        [hidden_gradient * pre_up * slope, hidden_gradient * activated], axis=1
    ).astype(jnp.bfloat16)
    return (
        contraction(grad_pre, gate_up, 1, 1).astype(jnp.bfloat16),
        gradient_first,
        gradient_second,
    )


def on_device(
    output_gradient,
    expert_choice_index,
    routing_weight,
    stored_gate_preact,
    gate_up_weight,
    down_weight,
    down_first_factor,
    down_second_factor,
    rotated_queries,
    rotated_keys,
    stored_values,
    output_weight,
    output_first_factor,
    output_second_factor,
):
    tok_rows, model_width = output_gradient.shape
    top_count = expert_choice_index.shape[1]
    grp_count = lax.axis_size("grp")
    dev_count = lax.axis_size("dev")
    experts = grp_count * dev_count
    slot_count = stored_gate_preact.shape[1]
    capacity = slot_count // experts
    assign = tok_rows * top_count
    flat_ids = expert_choice_index.reshape(assign)
    onehot = (flat_ids[:, None] == jnp.arange(experts, dtype=jnp.int32)[None, :]).astype(jnp.int32)
    before = jnp.cumsum(onehot, axis=0) - onehot
    slot_rank = jnp.sum(before * onehot, axis=1)
    cells = flat_ids * capacity + slot_rank
    scaled = (
        (routing_weight[:, :, None] * output_gradient[:, None, :].astype(jnp.float32))
        .astype(jnp.bfloat16)
        .reshape(assign, model_width)
    )
    outgoing = jnp.zeros((experts * capacity, model_width), jnp.bfloat16).at[cells].set(scaled)
    outgoing = outgoing.reshape(experts, capacity, model_width)
    incoming = lax.all_to_all(outgoing, ("grp", "dev"), split_axis=0, concat_axis=0, tiled=True)
    routed_rows = incoming.reshape(slot_count, model_width)
    grad_rows, gradient_first, gradient_second = expert_backward(
        routed_rows,
        stored_gate_preact[0],
        gate_up_weight[0],
        down_weight[0],
        down_first_factor[0],
        down_second_factor[0],
    )
    returned = lax.all_to_all(
        grad_rows.reshape(experts, capacity, model_width),
        ("grp", "dev"),
        split_axis=0,
        concat_axis=0,
        tiled=True,
    )
    picked = returned.reshape(experts * capacity, model_width)[cells]
    merged_result = jnp.sum(
        picked.reshape(tok_rows, top_count, model_width).astype(jnp.float32), axis=1
    )
    residual_gradient = (output_gradient.astype(jnp.float32) + merged_result).astype(jnp.bfloat16)
    segment_gradient = lax.all_gather(residual_gradient, "dev", axis=0, tiled=True)
    piece_len = segment_gradient.shape[0]
    device_share = rotated_queries.shape[1] // HEAD_SIZE
    group_size = QUERY_HEADS // KVH
    rank_total = output_second_factor.shape[0]
    kv_index = lax.axis_index("dev") * device_share // group_size
    key_rows = lax.dynamic_slice_in_dim(rotated_keys, kv_index * HEAD_SIZE, HEAD_SIZE, 1)
    value_rows = lax.dynamic_slice_in_dim(stored_values, kv_index * HEAD_SIZE, HEAD_SIZE, 1)
    lowrank_token = contraction(segment_gradient, output_second_factor, 1, 1).astype(jnp.bfloat16)
    head_gradient = (
        contraction(segment_gradient, output_weight, 1, 1)
        + adapter_scale
        * jnp.dot(lowrank_token, output_first_factor, preferred_element_type=jnp.float32)
    ).astype(jnp.bfloat16)
    lowrank_heads = output_first_factor.reshape(rank_total, device_share, HEAD_SIZE)
    att_scale = HEAD_SIZE ** (-0.5)
    block_rows = min(512, piece_len)
    grad_key_sum = jnp.zeros((piece_len, HEAD_SIZE), jnp.float32)
    grad_value_sum = jnp.zeros((piece_len, HEAD_SIZE), jnp.float32)
    row_contrib = jnp.zeros((rank_total, device_share * HEAD_SIZE), jnp.float32)
    column_contrib = jnp.zeros((rank_total, model_width), jnp.float32)
    query_parts = []
    for number in range(piece_len // block_rows):
        first_row = number * block_rows
        last_row = first_row + block_rows
        query_block = rotated_queries[first_row:last_row].reshape(
            block_rows, device_share, HEAD_SIZE
        )
        grad_block = head_gradient[first_row:last_row].reshape(block_rows, device_share, HEAD_SIZE)
        key_part = key_rows[:last_row]
        value_part = value_rows[:last_row]
        scores = (
            jnp.einsum("qhd,kd->hqk", query_block, key_part, preferred_element_type=jnp.float32)
            * att_scale
        )
        positions = first_row + jnp.arange(block_rows, dtype=jnp.int32)
        causal = positions[:, None] >= jnp.arange(last_row, dtype=jnp.int32)[None, :]
        scores = jnp.where(causal[None, :, :], scores, neg_big)
        probs_full = jnp.exp(scores - jnp.max(scores, axis=2, keepdims=True))
        probs_full = probs_full / jnp.sum(probs_full, axis=2, keepdims=True)
        probs_low = probs_full.astype(jnp.bfloat16)
        attended = jnp.einsum(
            "hqk,kd->qhd", probs_low, value_part, preferred_element_type=jnp.float32
        ).astype(jnp.bfloat16)
        grad_probs = jnp.einsum(
            "qhd,kd->hqk", grad_block, value_part, preferred_element_type=jnp.float32
        )
        row_delta = jnp.sum(grad_block.astype(jnp.float32) * attended.astype(jnp.float32), axis=2)
        grad_scores = (probs_full * (grad_probs - row_delta.T[:, :, None])).astype(jnp.bfloat16)
        query_parts.append(
            att_scale
            * jnp.einsum("hqk,kd->qhd", grad_scores, key_part, preferred_element_type=jnp.float32)
        )
        grad_key_sum = grad_key_sum.at[:last_row].add(
            att_scale
            * jnp.einsum(
                "hqk,qhd->kd", grad_scores, query_block, preferred_element_type=jnp.float32
            )
        )
        grad_value_sum = grad_value_sum.at[:last_row].add(
            jnp.einsum("hqk,qhd->kd", probs_low, grad_block, preferred_element_type=jnp.float32)
        )
        row_contrib = row_contrib + contraction(
            lowrank_token[first_row:last_row],
            attended.reshape(block_rows, device_share * HEAD_SIZE),
            0,
            0,
        )
        flattened = jnp.einsum(
            "qhd,rhd->qhr", attended, lowrank_heads, preferred_element_type=jnp.float32
        ).astype(jnp.bfloat16)
        column_contrib = column_contrib + jnp.einsum(
            "qhr,qc->rc",
            flattened,
            segment_gradient[first_row:last_row],
            preferred_element_type=jnp.float32,
        )
    query_gradient = jnp.concatenate(query_parts, axis=0).reshape(
        piece_len, device_share * HEAD_SIZE
    )
    output_first_gradient = lax.psum(
        (adapter_scale * row_contrib).astype(jnp.bfloat16), "grp"
    ).astype(jnp.float32)
    output_second_gradient = lax.psum(adapter_scale * column_contrib, ("grp", "dev"))
    token_block = piece_len // dev_count
    got_keys, got_values = (
        lax.all_to_all(
            grad_key_sum.reshape(dev_count, token_block, HEAD_SIZE).astype(jnp.bfloat16),
            "dev",
            split_axis=0,
            concat_axis=0,
            tiled=True,
        ).astype(jnp.float32),
        lax.all_to_all(
            grad_value_sum.reshape(dev_count, token_block, HEAD_SIZE).astype(jnp.bfloat16),
            "dev",
            split_axis=0,
            concat_axis=0,
            tiled=True,
        ).astype(jnp.float32),
    )
    sharing = dev_count // KVH
    key_gradient = (
        got_keys.reshape(KVH, sharing, token_block, HEAD_SIZE)
        .sum(axis=1)
        .transpose(1, 0, 2)
        .reshape(token_block, KVH * HEAD_SIZE)
    )
    value_gradient = (
        got_values.reshape(KVH, sharing, token_block, HEAD_SIZE)
        .sum(axis=1)
        .transpose(1, 0, 2)
        .reshape(token_block, KVH * HEAD_SIZE)
    )
    return (
        gradient_first[None],
        gradient_second[None],
        residual_gradient,
        output_first_gradient,
        output_second_gradient,
        query_gradient,
        key_gradient,
        value_gradient,
    )


def solution(mesh):
    in_specs = (
        P(("grp", "dev"), None),
        P(("grp", "dev"), None),
        P(("grp", "dev"), None),
        P(("grp", "dev"), None, None),
        P(("grp", "dev"), None, None),
        P(("grp", "dev"), None, None),
        P(("grp", "dev"), None, None),
        P(("grp", "dev"), None, None),
        P("grp", "dev"),
        P("grp", None),
        P("grp", None),
        P("dev", None),
        P(None, "dev"),
        P(),
    )
    out_specs = (
        P(("grp", "dev"), None, None),
        P(("grp", "dev"), None, None),
        P(("grp", "dev"), None),
        P(None, "dev"),
        P(),
        P("grp", "dev"),
        P(("grp", "dev"), None),
        P(("grp", "dev"), None),
    )
    return jax.shard_map(
        on_device, mesh=mesh, in_specs=in_specs, out_specs=out_specs, check_vma=False
    )
```

profile of v0, /device:TPU:0, one launch (start us, length us, event | category | flops | bytes accessed | tf_op | source)
XLA Modules:
  0.0 544.8 jit_solution(2716416181937897674)
XLA Ops:
  9.3 9.0 %reduce-window.6 = s32[32,8,128]{2,1,0:T(8,128)S(1)} reduce-window(s32[32,8,128]{2,1,0:T(8,128)S(1)} %fusion.82, s32[]{:T(128)} %constant.159.clone.1), window={size=1x1x128 pad=0_0x0_0x127_0}, to_apply=%region_0.0 | reduce-window | flops 4161536 | bytes 262148 | tf_op jit(solution)/shard_map/reduce-window
  21.9 10.4 %scatter_custom_fusion = bf16[1280,2048]{1,0:T(8,128)(2,1)} fusion(s32[1024]{0:T(1024)S(1)} %bitcast.258, f32[128,2048]{1,0:T(8,128)} %convert_element_type.124, f32[1024]{0:T(1024)S(1)} %mul.153, bf16[]{:T(256)} %constant.157.clone.1), kind=kCustom, calls=%fused_computation.20 | custom fusion | flops 4194304 | bytes 6295554 | tf_op jit(solution)/shard_map/scatter | solution.py:80
  32.3 7.6 %all-to-all-start = ((bf16[32,40,2048]{2,1,0:T(8,128)(2,1)}), bf16[32,40,2048]{2,1,0:T(8,128)(2,1)}, u32[]{:S(2)}, u32[]{:S(2)}) async-start(bf16[32,40,2048]{2,1,0:T(8,128)(2,1)} %bitcast.236), calls=%async_computation | async-start | bytes 10485760 | tf_op jit(solution)/shard_map/all_to_all | solution.py:82
  39.9 6.3 %copy.132 = bf16[1,1280,1536]{1,2,0:T(8,128)(2,1)} copy(bf16[1,1280,1536]{2,1,0:T(8,128)(2,1)} %param.29) | data formatting | bytes 7864320 | tf_op args[3]
  46.2 110.4 %all-to-all-done = bf16[32,40,2048]{2,1,0:T(8,128)(2,1)} async-done(((bf16[32,40,2048]{2,1,0:T(8,128)(2,1)}), bf16[32,40,2048]{2,1,0:T(8,128)(2,1)}, u32[]{:S(2)}, u32[]{:S(2)}) %all-to-all-start) | async-done | bytes 5242912 | tf_op jit(solution)/shard_map/all_to_all | solution.py:82
  156.6 4.2 convolution_convert_fusion.2
  160.9 6.9 %fusion.30 = f32[1280,768]{0,1:T(8,128)S(1)} fusion(bf16[1280,2048]{1,0:T(8,128)(2,1)} %bitcast.6, bf16[1,768,2048]{2,1,0:T(8,128)(2,1)S(1)} %copy-done), kind=kOutput, calls=%fused_computation.48 | convolution fusion | flops 4026531840 | bytes 12320768 | tf_op jit(solution)/shard_map/dot_general | solution.py:16
  167.8 3.7 fusion.19
  171.5 10.2 %convolution_convert_fusion = bf16[1280,2048]{1,0:T(8,128)(2,1)} fusion(bf16[1,2048,1536]{2,1,0:T(8,128)(2,1)S(1)} %bitcast.261, bf16[1280,768]{0,1:T(8,128)(2,1)S(1)} %get-tuple-element.115, bf16[1280,768]{0,1:T(8,128)(2,1)S(1)} %get-tuple-element.114), kind=kOutput, calls=%fused_computation.12 | convolution fusion | flops 8063549440 | bytes 15466496 | tf_op jit(solution)/shard_map/dot_general | solution.py:16
  181.8 3.7 all-to-all-start.1
  185.5 116.7 %all-to-all-done.1 = bf16[32,40,2048]{2,1,0:T(8,128)(2,1)} async-done(((bf16[32,40,2048]{2,1,0:T(8,128)(2,1)}), bf16[32,40,2048]{2,1,0:T(8,128)(2,1)}, u32[]{:S(2)}, u32[]{:S(2)}) %all-to-all-start.1) | async-done | bytes 5242912 | tf_op jit(solution)/shard_map/all_to_all | solution.py:92
  302.2 12.0 %gather_fusion = bf16[1024,2048]{1,0:T(8,128)(2,1)} fusion(bf16[1280,2048]{1,0:T(8,128)(2,1)} %bitcast.15, s32[1024]{0:T(1024)S(1)} %broadcast_clamp_fusion), kind=kCustom, calls=%fused_computation | custom fusion | bytes 8392704 | tf_op jit(solution)/shard_map/gather | solution.py:99
  314.2 5.1 convert_reduce_fusion
  323.7 7.3 %fusion.112 = (f32[4,512]{1,0:T(4,128)S(1)}, f32[4,512,1024]{1,2,0:T(8,128)}) fusion(pred[512,1024]{0,1:T(8,128)(4,1)S(1)} %iota_compare_fusion, bf16[512,4,128]{0,2,1:T(8,128)(2,1)S(1)} %bitcast.250, bf16[1024,512]{1,0:T(8,128)(2,1)} %param.35, s32[]{:T(128)S(6)} %select_n.30), kind=kOutput, calls=%fused_computation.154 | convolution fusion | flops 545260544 | bytes 9707524 | tf_op jit(solution)/shard_map/sub | solution.py:142
  331.0 4.6 fusion.28
  338.6 4.6 fusion.111
  347.6 5.4 fusion.33
  352.9 3.1 all-gather.2.cloned.1.call-done
  356.1 5.4 fusion.117
  367.8 4.8 fusion.3
  380.7 3.5 all-to-all-start.2
  384.3 4.3 fusion.50
  391.9 4.1 all-to-all-start.3
  409.8 126.4 %all-reduce.7.cloned.1.call-done = f32[64,2048]{1,0:T(8,128)} async-done(((f32[64,2048]{1,0:T(8,128)}), f32[64,2048]{1,0:T(8,128)}) %all-reduce.7.cloned.1.call-update) | async-done | bytes 524304 | tf_op jit(solution)/shard_map/psum | solution.py:187
  (128 shorter events, 50.6 us)
Async XLA Ops:
  7.2 153.6 %copy-start = (bf16[1,768,2048]{2,1,0:T(8,128)(2,1)S(1)}, bf16[1,768,2048]{2,1,0:T(8,128)(2,1)}, u32[]{:S(2)}) copy-start(bf16[1,768,2048]{2,1,0:T(8,128)(2,1)} %param.31) | copy-start | bytes 9437188
  32.3 124.3 %all-to-all-start = ((bf16[32,40,2048]{2,1,0:T(8,128)(2,1)}), bf16[32,40,2048]{2,1,0:T(8,128)(2,1)}, u32[]{:S(2)}, u32[]{:S(2)}) async-start(bf16[32,40,2048]{2,1,0:T(8,128)(2,1)} %bitcast.236), calls=%async_computation | async-start | bytes 10485760 | tf_op jit(solution)/shard_map/all_to_all | solution.py:82
  39.9 116.7 %copy-start.19 = (bf16[1,64,2048]{2,1,0:T(8,128)(2,1)S(1)}, bf16[1,64,2048]{2,1,0:T(8,128)(2,1)}, u32[]{:S(2)}) copy-start(bf16[1,64,2048]{2,1,0:T(8,128)(2,1)} %param.33) | copy-start | bytes 786436
  160.8 6.9 %copy-start.13 = (bf16[1280,64]{0,1:T(8,128)(2,1)}, bf16[1280,64]{0,1:T(8,128)(2,1)S(1)}, u32[]{:S(2)}) copy-start(bf16[1280,64]{0,1:T(8,128)(2,1)S(1)} %convolution_convert_fusion.2) | copy-start | bytes 491524
  160.8 6.9 %copy-start.7 = (bf16[1,1280,1536]{1,2,0:T(8,128)(2,1)S(1)}, bf16[1,1280,1536]{1,2,0:T(8,128)(2,1)}, u32[]{:S(2)}) copy-start(bf16[1,1280,1536]{1,2,0:T(8,128)(2,1)} %copy.132) | copy-start | bytes 11796484
  160.8 6.9 %copy-start.25 = (bf16[1,64,768]{2,1,0:T(8,128)(2,1)S(1)}, bf16[1,64,768]{2,1,0:T(8,128)(2,1)}, u32[]{:S(2)}) copy-start(bf16[1,64,768]{2,1,0:T(8,128)(2,1)} %param.32) | copy-start | bytes 294916
  160.8 10.7 %slice-start = ((s8[6291456]{0:T(1024)(128)(4,1)}), s8[4194304]{0:T(1024)(128)(4,1)S(1)}, s32[]{:S(2)}) async-start(s8[6291456]{0:T(1024)(128)(4,1)} %bitcast.260), calls=%async_computation.7 | async-start | bytes 8388608
  181.8 120.4 %all-to-all-start.1 = ((bf16[32,40,2048]{2,1,0:T(8,128)(2,1)}), bf16[32,40,2048]{2,1,0:T(8,128)(2,1)}, u32[]{:S(2)}, u32[]{:S(2)}) async-start(bf16[32,40,2048]{2,1,0:T(8,128)(2,1)} %bitcast.238), calls=%async_computation.1 | async-start | bytes 10485760 | tf_op jit(solution)/shard_map/all_to_all | solution.py:92
  185.4 170.6 %all-gather.2.cloned.1.call-start = ((), (), s32[]{:S(2)}) async-start(), calls=%async_computation.4 | async-start | bytes 4718592 | tf_op jit(solution)/shard_map/all_gather | solution.py:104
  314.2 5.2 copy-start.8
  314.2 6.5 %copy-start.12 = (bf16[1024,512]{1,0:T(8,128)(2,1)S(1)}, bf16[1024,512]{1,0:T(8,128)(2,1)}, u32[]{:S(2)}) copy-start(bf16[1024,512]{1,0:T(8,128)(2,1)} %param.34) | copy-start | bytes 3145732
  320.3 81.7 %all-reduce.5.cloned.1.call-start = ((), (), s32[]{:S(2)}) async-start(), calls=%async_computation.5 | async-start | bytes 131072 | tf_op jit(solution)/shard_map/psum | solution.py:184
  321.0 10.0 %copy-start.16 = (bf16[512,512]{0,1:T(8,128)(2,1)}, bf16[512,512]{0,1:T(8,128)(2,1)S(1)}, u32[]{:S(2)}) copy-start(bf16[512,512]{0,1:T(8,128)(2,1)S(1)} %copy.181) | copy-start | bytes 1572868
  321.3 17.4 %copy-start.9 = (bf16[512,512]{0,1:T(8,128)(2,1)}, bf16[512,512]{0,1:T(8,128)(2,1)S(1)}, u32[]{:S(2)}) copy-start(bf16[512,512]{0,1:T(8,128)(2,1)S(1)} %copy.180) | copy-start | bytes 1572868
  343.2 4.4 copy-start.26
  352.9 8.5 %copy-start.20 = (bf16[64,2048]{1,0:T(8,128)(2,1)S(1)}, bf16[64,2048]{1,0:T(8,128)(2,1)}, u32[]{:S(2)}) copy-start(bf16[64,2048]{1,0:T(8,128)(2,1)} %param.39) | copy-start | bytes 786436
  356.1 5.4 copy-start.2
  378.7 5.6 %copy-start.18 = (bf16[512,512]{0,1:T(8,128)(2,1)S(1)}, bf16[512,512]{0,1:T(8,128)(2,1)}, u32[]{:S(2)}) copy-start(bf16[512,512]{0,1:T(8,128)(2,1)} %get-tuple-element.118) | copy-start | bytes 1572868
  378.7 5.6 %copy-start.21 = (f32[512,128]{1,0:T(8,128)S(1)}, f32[512,128]{1,0:T(8,128)}, u32[]{:S(2)}) copy-start(f32[512,128]{1,0:T(8,128)} %convolution_bitcast_fusion.2) | copy-start | bytes 786436
  380.7 7.9 %copy-start.22 = (bf16[512,64]{0,1:T(8,128)(2,1)S(1)}, bf16[512,64]{0,1:T(8,128)(2,1)}, u32[]{:S(2)}) copy-start(bf16[512,64]{0,1:T(8,128)(2,1)} %fusion.51) | copy-start | bytes 196612
  380.7 11.2 %all-to-all-start.2 = ((bf16[8,128,128]{2,1,0:T(8,128)(2,1)}), bf16[8,128,128]{2,1,0:T(8,128)(2,1)S(1)}, u32[]{:S(2)}, u32[]{:S(2)}) async-start(bf16[8,128,128]{2,1,0:T(8,128)(2,1)} %bitcast.44), calls=%async_computation.2 | async-start | bytes 524288 | tf_op jit(solution)/shard_map/all_to_all | solution.py:190
  384.3 152.0 %all-reduce.7.cloned.1.call-start = ((), (), s32[]{:S(2)}) async-start(), calls=%async_computation.6 | async-start | bytes 1048576 | tf_op jit(solution)/shard_map/psum | solution.py:187
  391.9 14.3 %all-to-all-start.3 = ((bf16[8,128,128]{2,1,0:T(8,128)(2,1)}), bf16[8,128,128]{2,1,0:T(8,128)(2,1)}, u32[]{:S(2)}, u32[]{:S(2)}) async-start(bf16[8,128,128]{2,1,0:T(8,128)(2,1)} %bitcast.255), calls=%async_computation.3 | async-start | bytes 524288 | tf_op jit(solution)/shard_map/all_to_all | solution.py:197
  398.7 139.3 %copy-start.1 = (bf16[1,768,2048]{2,1,0:T(8,128)(2,1)S(1)}, bf16[1,768,2048]{2,1,0:T(8,128)(2,1)}, u32[]{:S(2)}) copy-start(bf16[1,768,2048]{2,1,0:T(8,128)(2,1)} %param.31) | copy-start | bytes 9437188
  (13 other events, 38.4 us)
Sparse Core Ops, SparseCore 0:
  320.4 35.6 all-gather.1
  367.9 33.9 all-reduce.4
  408.7 127.4 all-reduce.6
where the time goes:
time: 551 us; the launch traced here: 545 us
  waiting for transfers between devices  357 us (65%)
  matrix products  75.2 us (14%)
  other arithmetic  42.6 us (8%)
  local copies, waits for them, and re-layouts  36.2 us (7%)
  starting transfers between devices  19.4 us (4%)
  between operations  14.5 us (3%)
    psum x1, waiting for transfers between devices, on_device(): lax.psum(adapter_scale * column_contrib, ('grp', 'dev'))  126 us
    all_to_all x1, waiting for transfers between devices, on_device(): lax.all_to_all(grad_rows.reshape(experts, capacity, model_width), ('grp',...  117 us
    all_to_all x1, waiting for transfers between devices, on_device(): lax.all_to_all(outgoing, ('grp', 'dev'), split_axis=0, concat_axis=0, til...  110 us
    dot_general x9, matrix products, contraction(): lax.dot_general(left, right, (((left_dim,), (right_dim,)), ((), ())), pre...  36.2 us
    unnamed x70, local copies, waits for them, and re-layouts  19.2 us
    gather x1, local copies, waits for them, and re-layouts, on_device(): picked = returned.reshape(experts * capacity, model_width)[cells]  12 us
    sub x2, matrix products, on_device(): probs_full = jnp.exp(scores - jnp.max(scores, axis=2, keepdims=True))  11.9 us
  transfers between devices with their start and end apart: 7, of which 5 were waited for; matrix products, arithmetic and copies ran while one was open for 13% of the time, Pallas kernels for 0%

commit v1 on v0

v1 whole, which is shorter than its diff:
```python
import functools

import jax
import jax.numpy as jnp
from jax import lax
from jax.experimental import pallas as pl
from jax.experimental.pallas import tpu as pltpu
from jax.sharding import PartitionSpec as P

QUERY_HEADS = 32
KVH = 4
HEAD_SIZE = 128

adapter_scale = 2.0
neg_big = -1e30
att_scale = HEAD_SIZE ** (-0.5)
VMEM_BYTES = 56 * 1024 * 1024


def contraction(left, right, left_dim, right_dim):
    return lax.dot_general(
        left, right, (((left_dim,), (right_dim,)), ((), ())), preferred_element_type=jnp.float32
    )


def across(value, step):
    count = lax.axis_size("dev")
    return lax.ppermute(value, "dev", [(i, i ^ step) for i in range(count)])


def shift(value, step):
    count = lax.axis_size("grp")
    return lax.ppermute(value, "grp", [(i, (i + step) % count) for i in range(count)])


def forward_kernel(place, q_ref, k_ref, v_ref, a_ref, probs_ref, att_ref, even_ref, odd_ref, folded):
    head = pl.program_id(0)
    rows = q_ref.shape[0]
    token_block = folded.shape[2]
    block = min(256, rows)

    @pl.when(head == 0)
    def _():
        folded[...] = jnp.zeros_like(folded)

    for first in range(0, rows, block):
        last = first + block
        scores = contraction(q_ref[first:last, :], k_ref[:last, :], 1, 1) * att_scale
        row = first + lax.broadcasted_iota(jnp.int32, scores.shape, 0)
        column = lax.broadcasted_iota(jnp.int32, scores.shape, 1)
        scores = jnp.where(row >= column, scores, neg_big)
        weights = jnp.exp(scores - jnp.max(scores, axis=1, keepdims=True))
        weights = weights * (1.0 / jnp.sum(weights, axis=1, keepdims=True))
        low = weights.astype(jnp.bfloat16)
        probs_ref[0, first:last, :last] = low
        attended = jnp.dot(low, v_ref[:last, :], preferred_element_type=jnp.float32).astype(
            jnp.bfloat16
        )
        att_ref[first:last, :] = attended
        part = contraction(a_ref[...], attended, 1, 1).astype(jnp.bfloat16).astype(jnp.float32)
        for inner in range(0, block, token_block):
            number = (first + inner) // token_block
            folded[number] = folded[number] + part[:, inner : inner + token_block]

    @pl.when(head == pl.num_programs(0) - 1)
    def _():
        for j in range(even_ref.shape[0]):
            even_ref[j] = folded[place[0] ^ (2 * j)].astype(even_ref.dtype)
            odd_ref[j] = folded[place[0] ^ (2 * j + 1)].astype(odd_ref.dtype)


def attention_forward(place, queries, keys, values, first_factor, token_block):
    rows, width = queries.shape
    heads = width // HEAD_SIZE
    rank = first_factor.shape[0]
    pairs = rows // token_block // 2
    of_head = pl.BlockSpec((rows, HEAD_SIZE), lambda h, place: (0, h))
    of_group = pl.BlockSpec((rows, HEAD_SIZE), lambda h, place: (0, place[1]))
    part = pl.BlockSpec((pairs, rank, token_block), lambda h, place: (0, 0, 0))
    part_shape = jax.ShapeDtypeStruct((pairs, rank, token_block), jnp.bfloat16)
    return pl.pallas_call(
        forward_kernel,
        grid_spec=pltpu.PrefetchScalarGridSpec(
            num_scalar_prefetch=1,
            grid=(heads,),
            in_specs=[
                of_head,
                of_group,
                of_group,
                pl.BlockSpec((rank, HEAD_SIZE), lambda h, place: (0, h)),
            ],
            out_specs=[
                pl.BlockSpec((1, rows, rows), lambda h, place: (h, 0, 0)),
                of_head,
                part,
                part,
            ],
            scratch_shapes=[pltpu.VMEM((2 * pairs, rank, token_block), jnp.float32)],
        ),
        out_shape=[
            jax.ShapeDtypeStruct((heads, rows, rows), jnp.bfloat16),
            jax.ShapeDtypeStruct((rows, width), jnp.bfloat16),
            part_shape,
            part_shape,
        ],
        compiler_params=pltpu.CompilerParams(
            dimension_semantics=("arbitrary",), vmem_limit_bytes=VMEM_BYTES
        ),
        name="attention_forward",
    )(place, queries, keys, values, first_factor)


def head_kernel(place, *refs):
    count = len(refs) - 5
    blocks = refs[:count]
    weight_ref, first_ref, second_ref, grad_ref, low_ref = refs[count:]
    rows = blocks[0].shape[0]
    pairs = count // 2
    for j in range(pairs):
        gradient = jnp.concatenate([blocks[j][...], blocks[pairs + j][...]], axis=0)
        low = contraction(gradient, second_ref[...], 1, 1).astype(jnp.bfloat16)
        result = contraction(gradient, weight_ref[...], 1, 1)
        result = result + adapter_scale * jnp.dot(
            low, first_ref[...], preferred_element_type=jnp.float32
        )
        result = result.astype(jnp.bfloat16)
        for half in range(2):
            at = pl.ds(pl.multiple_of((place[0] ^ (2 * j + half)) * rows, rows), rows)
            grad_ref[at, :] = result[half * rows : (half + 1) * rows]
            low_ref[at, :] = low[half * rows : (half + 1) * rows]


def head_gradients(place, blocks, weight, first_factor, second_factor):
    rows = blocks[0].shape[0] * len(blocks)
    whole = lambda a: pl.BlockSpec(a.shape, lambda i, place: (0,) * a.ndim)
    operands = [*blocks, weight, first_factor, second_factor]
    outs = [
        jax.ShapeDtypeStruct((rows, weight.shape[0]), jnp.bfloat16),
        jax.ShapeDtypeStruct((rows, second_factor.shape[0]), jnp.bfloat16),
    ]
    return pl.pallas_call(
        head_kernel,
        grid_spec=pltpu.PrefetchScalarGridSpec(
            num_scalar_prefetch=1,
            grid=(1,),
            in_specs=[whole(a) for a in operands],
            out_specs=[whole(a) for a in outs],
        ),
        out_shape=outs,
        compiler_params=pltpu.CompilerParams(
            dimension_semantics=("arbitrary",), vmem_limit_bytes=VMEM_BYTES
        ),
        name="head_gradients",
    )(place, *operands)


def backward_kernel(
    place, q_ref, k_ref, v_ref, g_ref, att_ref, probs_ref, dq_ref, even_ref, odd_ref, dk, dv
):
    head = pl.program_id(0)
    rows = q_ref.shape[0]
    block = min(256, rows)
    token_block = even_ref.shape[1]

    @pl.when(head == 0)
    def _():
        dk[...] = jnp.zeros_like(dk)
        dv[...] = jnp.zeros_like(dv)

    for first in range(0, rows, block):
        last = first + block
        gradient = g_ref[first:last, :]
        query = q_ref[first:last, :]
        probs = probs_ref[0, first:last, :last]
        grad_probs = contraction(gradient, v_ref[:last, :], 1, 1)
        delta = jnp.sum(
            gradient.astype(jnp.float32) * att_ref[first:last, :].astype(jnp.float32),
            axis=1,
            keepdims=True,
        )
        grad_scores = (probs.astype(jnp.float32) * (grad_probs - delta)).astype(jnp.bfloat16)
        dq_ref[first:last, :] = att_scale * jnp.dot(
            grad_scores, k_ref[:last, :], preferred_element_type=jnp.float32
        )
        dk[:last, :] += contraction(grad_scores, query, 0, 0)
        dv[:last, :] += contraction(probs, gradient, 0, 0)

    @pl.when(head == pl.num_programs(0) - 1)
    def _():
        for j in range(even_ref.shape[0]):
            for half, ref in enumerate((even_ref, odd_ref)):
                number = place[0] ^ (2 * j + half)
                at = pl.ds(pl.multiple_of(number * token_block, token_block), token_block)
                ref[j, :, :HEAD_SIZE] = (dk[at, :] * att_scale).astype(ref.dtype)
                ref[j, :, HEAD_SIZE:] = dv[at, :].astype(ref.dtype)


def attention_backward(place, queries, keys, values, gradient, attended, probs, token_block):
    rows, width = queries.shape
    heads = width // HEAD_SIZE
    pairs = rows // token_block // 2
    of_head = pl.BlockSpec((rows, HEAD_SIZE), lambda h, place: (0, h))
    of_group = pl.BlockSpec((rows, HEAD_SIZE), lambda h, place: (0, place[1]))
    part = pl.BlockSpec((pairs, token_block, 2 * HEAD_SIZE), lambda h, place: (0, 0, 0))
    part_shape = (pairs, token_block, 2 * HEAD_SIZE)
    return pl.pallas_call(
        backward_kernel,
        grid_spec=pltpu.PrefetchScalarGridSpec(
            num_scalar_prefetch=1,
            grid=(heads,),
            in_specs=[
                of_head,
                of_group,
                of_group,
                of_head,
                of_head,
                pl.BlockSpec((1, rows, rows), lambda h, place: (h, 0, 0)),
            ],
            out_specs=[of_head, part, part],
            scratch_shapes=[
                pltpu.VMEM((rows, HEAD_SIZE), jnp.float32),
                pltpu.VMEM((rows, HEAD_SIZE), jnp.float32),
            ],
        ),
        out_shape=[
            jax.ShapeDtypeStruct((rows, width), jnp.float32),
            jax.ShapeDtypeStruct(part_shape, jnp.float32),
            jax.ShapeDtypeStruct(part_shape, jnp.bfloat16),
        ],
        compiler_params=pltpu.CompilerParams(
            dimension_semantics=("arbitrary",), vmem_limit_bytes=VMEM_BYTES
        ),
        name="attention_backward",
    )(place, queries, keys, values, gradient, attended, probs)


def planes_sum(parts, grp_index):
    count = len(parts)
    total = None
    for plane in range(count):
        term = parts[0].astype(jnp.float32)
        for step in range(1, count):
            here = (grp_index - step) % count == plane
            term = jnp.where(here, parts[step].astype(jnp.float32), term)
        total = term if total is None else total + term
    return total


def on_device(
    output_gradient,
    expert_choice_index,
    routing_weight,
    stored_gate_preact,
    gate_up_weight,
    down_weight,
    down_first_factor,
    down_second_factor,
    rotated_queries,
    rotated_keys,
    stored_values,
    output_weight,
    output_first_factor,
    output_second_factor,
):
    tok_rows, model_width = output_gradient.shape
    grp_count = lax.axis_size("grp")
    dev_count = lax.axis_size("dev")
    pairs = dev_count // 2
    experts = grp_count * dev_count
    slot_count = stored_gate_preact.shape[1]
    capacity = slot_count // experts
    chunk = dev_count * capacity
    width_ff = down_weight.shape[1]
    grp_index = lax.axis_index("grp")
    dev_index = lax.axis_index("dev")
    device_share = rotated_queries.shape[1] // HEAD_SIZE
    piece_len = rotated_queries.shape[0]
    kv_index = dev_index * device_share // (QUERY_HEADS // KVH)
    place = jnp.stack([dev_index, kv_index]).astype(jnp.int32)

    order = [2 * j for j in range(pairs)] + [2 * j + 1 for j in range(pairs)]

    ordinal = jnp.arange(experts, dtype=jnp.int32)
    in_plane = ordinal % dev_count
    distance = jnp.where(in_plane < pairs, 2 * in_plane, 2 * (in_plane - pairs) + 1)
    expert_of = ((grp_index + ordinal // dev_count) % grp_count) * dev_count + (
        dev_index ^ distance
    )
    named = expert_choice_index.T[:, None, :] == expert_of[None, :, None]
    chosen = jnp.any(named, axis=0)
    weight_of = jnp.sum(jnp.where(named, routing_weight.T[:, None, :], 0.0), axis=0)
    token = jnp.arange(tok_rows, dtype=jnp.int32)
    earlier = (token[:, None] < token[None, :]).astype(jnp.bfloat16)
    rank_of = jnp.dot(
        chosen.astype(jnp.bfloat16), earlier, preferred_element_type=jnp.float32
    )
    table = jnp.stack([jnp.where(chosen, rank_of, -1.0), weight_of]).reshape(
        2, grp_count, dev_count, tok_rows
    )

    tokens_at = [output_gradient] + [shift(output_gradient, s) for s in range(1, grp_count)]
    tables_at = [table[:, 0]] + [shift(table[:, s], s) for s in range(1, grp_count)]

    line = jnp.arange(chunk, dtype=jnp.int32)
    source = line // capacity
    source_distance = jnp.where(source < pairs, 2 * source, 2 * (source - pairs) + 1)
    saved_line = (dev_index ^ source_distance) * capacity + line % capacity
    reorder = (saved_line[:, None] == line[None, :]).astype(jnp.bfloat16)

    slot = jnp.arange(capacity, dtype=jnp.float32)

    def placement(step):
        ranks, weights = tables_at[step]
        filled = ranks[:, None, :] == slot[None, :, None]
        row_weight = jnp.sum(jnp.where(filled, weights[:, None, :], 0.0), axis=2)
        return filled.astype(jnp.bfloat16), row_weight

    placements = [placement(s) for s in range(grp_count)]

    def message_rows(step, j):
        filled = placements[step][0]
        return jnp.concatenate([filled[j], filled[pairs + j]], axis=0)

    def dispatched(step):
        weights = placements[step][1]
        messages = []
        for j in range(pairs):
            scale = jnp.concatenate([weights[j], weights[pairs + j]])
            rows = jnp.dot(
                message_rows(step, j), tokens_at[step], preferred_element_type=jnp.float32
            )
            messages.append((rows * scale[:, None]).astype(jnp.bfloat16))
        got = [messages[0]] + [across(messages[j], 2 * j) for j in range(1, pairs)]
        passed = across(jnp.concatenate([part[capacity:] for part in got], axis=0), 1)
        return jnp.concatenate([part[:capacity] for part in got] + [passed], axis=0)

    first_factor = down_first_factor[0]
    second_factor = down_second_factor[0]

    def saved_of(step):
        plane = (grp_index - step) % grp_count
        rows = lax.dynamic_slice_in_dim(stored_gate_preact[0], plane * chunk, chunk, 0)
        rows = jnp.dot(reorder, rows, preferred_element_type=jnp.float32).astype(jnp.bfloat16)
        gate = rows[:, :width_ff].astype(jnp.float32)
        hidden = (gate * jax.nn.sigmoid(gate) * rows[:, width_ff:].astype(jnp.float32)).astype(
            jnp.bfloat16
        )
        return rows, hidden, contraction(hidden, first_factor, 1, 1).astype(jnp.bfloat16)

    saved = [saved_of(s) for s in range(grp_count)]

    probs, attended, fold_even, fold_odd = attention_forward(
        place, rotated_queries, rotated_keys, stored_values, output_first_factor, tok_rows
    )

    def plane_scatter(even, odd):
        both = (even.astype(jnp.float32) + across(odd, 1).astype(jnp.float32)).astype(
            jnp.bfloat16
        )
        return [both[0]] + [across(both[j], 2 * j) for j in range(1, pairs)]

    folded = sum(part.astype(jnp.float32) for part in plane_scatter(fold_even, fold_odd)).astype(
        jnp.bfloat16
    )

    routed = [dispatched(s) for s in range(grp_count)]

    grad_first = jnp.zeros(first_factor.shape, jnp.float32)
    grad_second = jnp.zeros(second_factor.shape, jnp.float32)

    def returned(step):
        rows, hidden, low_in = saved[step]
        gate = rows[:, :width_ff].astype(jnp.float32)
        up = rows[:, width_ff:].astype(jnp.float32)
        sigmoid = jax.nn.sigmoid(gate)
        slope = sigmoid * (1.0 + gate * (1.0 - sigmoid))
        low_grad = contraction(routed[step], second_factor, 1, 1).astype(jnp.bfloat16)
        grad_hidden = contraction(
            routed[step], down_weight[0], 1, 1
        ) + adapter_scale * jnp.dot(low_grad, first_factor, preferred_element_type=jnp.float32)
        grad_pre = jnp.concatenate(
            [grad_hidden * up * slope, grad_hidden * (gate * sigmoid)], axis=1
        ).astype(jnp.bfloat16)
        half = pairs * capacity
        odd = contraction(grad_pre[half:], gate_up_weight[0], 1, 1).astype(jnp.bfloat16)
        even = contraction(grad_pre[:half], gate_up_weight[0], 1, 1).astype(jnp.bfloat16)
        passed = across(odd, 1)
        parts = []
        for j in range(pairs):
            here = slice(j * capacity, (j + 1) * capacity)
            message = jnp.concatenate([even[here], passed[here]], axis=0)
            parts.append(message if j == 0 else across(message, 2 * j))
        rows_in = jnp.concatenate(parts, axis=0)
        spread = jnp.concatenate([message_rows(step, j) for j in range(pairs)], axis=0)
        total = contraction(spread, rows_in, 0, 0)
        first = contraction(low_grad, hidden, 0, 0)
        second = contraction(low_in, routed[step], 0, 0)
        if step:
            total = shift(total.astype(jnp.bfloat16), -step).astype(jnp.float32)
        return total, first, second

    steps = list(range(1, grp_count)) + [0]
    merged = output_gradient.astype(jnp.float32)
    for step in steps:
        total, first, second = returned(step)
        merged = merged + total
        grad_first = grad_first + first
        grad_second = grad_second + second
    residual = merged.astype(jnp.bfloat16)

    near = [residual] + [across(residual, 2 * j) for j in range(1, pairs)]
    blocks = near + [across(part, 1) for part in near]
    head_gradient, low_tokens = head_gradients(
        place, blocks, output_weight, output_first_factor, output_second_factor
    )

    column_term = adapter_scale * jnp.dot(folded, residual, preferred_element_type=jnp.float32)
    share = model_width // dev_count
    pieces = [
        lax.dynamic_slice_in_dim(column_term, (dev_index ^ k) * share, share, 1) for k in order
    ]
    even = jnp.stack(pieces[:pairs])
    odd = jnp.stack(pieces[pairs:]).astype(jnp.bfloat16)
    own = sum(part.astype(jnp.float32) for part in plane_scatter(even, odd))
    own = planes_sum([own] + [shift(own, s) for s in range(1, grp_count)], grp_index)
    output_second_gradient = lax.all_gather(own, "dev", axis=1, tiled=True)

    row_term = (adapter_scale * contraction(low_tokens, attended, 0, 0)).astype(jnp.bfloat16)
    output_first_gradient = planes_sum(
        [row_term] + [shift(row_term, s) for s in range(1, grp_count)], grp_index
    )

    query_gradient, pair_even, pair_odd = attention_backward(
        place,
        rotated_queries,
        rotated_keys,
        stored_values,
        head_gradient,
        attended,
        probs,
        tok_rows,
    )
    arrived = plane_scatter(pair_even, pair_odd)
    grads = []
    for group in range(KVH):
        grad = jnp.zeros(arrived[0].shape, jnp.float32)
        for j in range(pairs):
            of_part = (dev_index ^ (2 * j)) * device_share // (QUERY_HEADS // KVH)
            grad = grad + jnp.where(of_part == group, arrived[j].astype(jnp.float32), 0.0)
        grads.append(grad)
    key_gradient = jnp.concatenate([grad[:, :HEAD_SIZE] for grad in grads], axis=1)
    value_gradient = jnp.concatenate([grad[:, HEAD_SIZE:] for grad in grads], axis=1)
    return (
        adapter_scale * grad_first[None],
        adapter_scale * grad_second[None],
        residual,
        output_first_gradient,
        output_second_gradient,
        query_gradient,
        key_gradient,
        value_gradient,
    )


def solution(mesh):
    in_specs = (
        P(("grp", "dev"), None),
        P(("grp", "dev"), None),
        P(("grp", "dev"), None),
        P(("grp", "dev"), None, None),
        P(("grp", "dev"), None, None),
        P(("grp", "dev"), None, None),
        P(("grp", "dev"), None, None),
        P(("grp", "dev"), None, None),
        P("grp", "dev"),
        P("grp", None),
        P("grp", None),
        P("dev", None),
        P(None, "dev"),
        P(),
    )
    out_specs = (
        P(("grp", "dev"), None, None),
        P(("grp", "dev"), None, None),
        P(("grp", "dev"), None),
        P(None, "dev"),
        P(),
        P("grp", "dev"),
        P(("grp", "dev"), None),
        P(("grp", "dev"), None),
    )
    return jax.shard_map(
        on_device, mesh=mesh, in_specs=in_specs, out_specs=out_specs, check_vma=False
    )
```

time: 551 us -> 399 us (0.72)
  waiting for transfers between devices: 357 us -> 138 us
  starting transfers between devices: 19.4 us -> 76.7 us
  Pallas kernels: 0 us -> 36 us
  other arithmetic: 42.6 us -> 14.1 us
  matrix products: 75.2 us -> 88.1 us
  between operations: 14.5 us -> 2.63 us
  blocking collectives: 0 us -> 9.35 us
  local copies, waits for them, and re-layouts: 36.2 us -> 28.1 us
    all_to_all x4 -> x0, waiting for transfers between devices: 227 us -> none  [the longest x1 117 us: on_device(): lax.all_to_all(grad_rows.reshape(experts, capacity, model_width), ('grp',...]
    ppermute x0 -> x66, waiting for transfers between devices: none -> 138 us  [the longest x51 105 us: across(): return lax.ppermute(value, 'dev', [(i, i ^ step) for i in range(count)])]
    psum x2 -> x0, waiting for transfers between devices: 127 us -> none  [the longest x1 126 us: on_device(): lax.psum(adapter_scale * column_contrib, ('grp', 'dev'))]
    ppermute x0 -> x66, starting transfers between devices: none -> 76.7 us  [the longest x51 42.4 us: across(): return lax.ppermute(value, 'dev', [(i, i ^ step) for i in range(count)])]
    pallas_call x0 -> x3, Pallas kernels: none -> 36 us  [the longest x1 14.6 us: attention_forward(): pl.pallas_call(forward_kernel, grid_spec=pltpu.PrefetchScalarGridSpec(num...]
    all_to_all x4 -> x0, starting transfers between devices: 18.9 us -> none  [the longest x1 7.59 us: on_device(): lax.all_to_all(outgoing, ('grp', 'dev'), split_axis=0, concat_axis=0, til...]
    dot_general x9 -> x29, matrix products: 36.2 us -> 53.5 us  [contraction(): lax.dot_general(left, right, (((left_dim,), (right_dim,)), ((), ())), pre...]
    gather x1 -> x0, local copies, waits for them, and re-layouts: 12 us -> none  [on_device(): picked = returned.reshape(experts * capacity, model_width)[cells]]
  transfers between devices with their start and end apart: 7 -> 66, of which waited for: 5 -> 20; matrix products, arithmetic and copies ran while one was open for 13% -> 30% of each run, Pallas kernels for 0% -> 4%
where the time goes in v1:
time: 399 us; the launch traced here: 393 us
  waiting for transfers between devices  138 us (35%)
  matrix products  88.1 us (22%)
  starting transfers between devices  76.7 us (19%)
  Pallas kernels  36 us (9%)
  local copies, waits for them, and re-layouts  28.1 us (7%)
  other arithmetic  14.1 us (4%)
  blocking collectives  9.35 us (2%)
    ppermute x51, waiting for transfers between devices, across(): return lax.ppermute(value, 'dev', [(i, i ^ step) for i in range(count)])  105 us
    dot_general x29, matrix products, contraction(): lax.dot_general(left, right, (((left_dim,), (right_dim,)), ((), ())), pre...  53.5 us
    ppermute x51, starting transfers between devices, across(): return lax.ppermute(value, 'dev', [(i, i ^ step) for i in range(count)])  42.4 us
    ppermute x15, starting transfers between devices, shift(): lax.ppermute(value, 'grp', [(i, (i + step) % count) for i in range(count)])  34.2 us
    ppermute x15, waiting for transfers between devices, shift(): lax.ppermute(value, 'grp', [(i, (i + step) % count) for i in range(count)])  33 us
    dot_general x16, matrix products, dispatched(): jnp.dot(message_rows(step, j), tokens_at[step], preferred_element_type=jn...  20.7 us
    pallas_call x1, Pallas kernels, attention_forward(): pl.pallas_call(forward_kernel, grid_spec=pltpu.PrefetchScalarGridSpec(num...  14.6 us
    pallas_call x1, Pallas kernels, attention_backward(): pl.pallas_call(backward_kernel, grid_spec=pltpu.PrefetchScalarGridSpec(nu...  11.9 us
  transfers between devices with their start and end apart: 66, of which 20 were waited for; matrix products, arithmetic and copies ran while one was open for 30% of the time, Pallas kernels for 4%

profile of v1, /device:TPU:0, one launch (start us, length us, event | category | flops | bytes accessed | tf_op | source)
XLA Modules:
  0.0 392.8 jit_solution(16897232348460092322)
XLA Ops:
  10.7 3.1 collective-permute-start.12
  35.5 14.6 %attention_forward.1 = (bf16[4,1024,1024]{2,1,0:T(8,128)(2,1)}, bf16[1024,512]{1,0:T(8,128)(2,1)}, bf16[4,64,128]{2,1,0:T(8,128)(2,1)}, bf16[4,64,128]{2,1,0:T(8,128)(2,1)}) custom-call(s32[2]{0:T(128)} %pad_add_fusion.place, bf16[1024,512]{1,0:T(8,128)(2,1)} %q_ref.3, bf16[1024,512]{1,0:T(8,128)(2,1)} %k_ref.3, bf16[1024,512]{1,0:T(8,128)(2,1)} %v_ref.3, ...), custom_call_target="tpu_custom_call" | custom-call | tf_op jit(solution)/shard_map/attention_forward/pallas_call | solution.py:81
  61.8 8.2 %collective-permute-done.18 = bf16[80,2048]{1,0:T(8,128)(2,1)S(1)} collective-permute-done((bf16[80,2048]{1,0:T(8,128)(2,1)S(1)}, bf16[80,2048]{1,0:T(8,128)(2,1)S(1)}, u32[]{:S(2)}, u32[]{:S(2)}) %collective-permute-start.18) | collective-permute-done | bytes 327712 | tf_op jit(solution)/shard_map/ppermute | solution.py:28
  70.5 8.9 %collective-permute-done.19 = bf16[80,2048]{1,0:T(8,128)(2,1)S(1)} collective-permute-done((bf16[80,2048]{1,0:T(8,128)(2,1)S(1)}, bf16[80,2048]{1,0:T(8,128)(2,1)S(1)}, u32[]{:S(2)}, u32[]{:S(2)}) %collective-permute-start.19) | collective-permute-done | bytes 327712 | tf_op jit(solution)/shard_map/ppermute | solution.py:28
  103.5 9.1 %collective-permute-done.8 = bf16[80,2048]{1,0:T(8,128)(2,1)S(1)} collective-permute-done((bf16[80,2048]{1,0:T(8,128)(2,1)S(1)}, bf16[80,2048]{1,0:T(8,128)(2,1)S(1)}, u32[]{:S(2)}, u32[]{:S(2)}) %collective-permute-start.8) | collective-permute-done | bytes 327712 | tf_op jit(solution)/shard_map/ppermute | solution.py:28
  116.9 9.4 %collective-permute-done.14 = bf16[80,2048]{1,0:T(8,128)(2,1)S(1)} collective-permute-done((bf16[80,2048]{1,0:T(8,128)(2,1)S(1)}, bf16[80,2048]{1,0:T(8,128)(2,1)S(1)}, u32[]{:S(2)}, u32[]{:S(2)}) %collective-permute-start.14) | collective-permute-done | bytes 327712 | tf_op jit(solution)/shard_map/ppermute | solution.py:28
  139.1 3.1 fusion.85
  179.4 3.1 fusion.84
  195.4 14.1 %collective-permute-done.33 = bf16[80,2048]{1,0:T(8,128)(2,1)S(1)} collective-permute-done((bf16[80,2048]{1,0:T(8,128)(2,1)S(1)}, bf16[80,2048]{1,0:T(8,128)(2,1)S(1)}, u32[]{:S(2)}, u32[]{:S(2)}) %collective-permute-start.33) | collective-permute-done | bytes 327712 | tf_op jit(solution)/shard_map/ppermute | solution.py:28
  212.0 9.0 %collective-permute-done.35 = bf16[80,2048]{1,0:T(8,128)(2,1)S(1)} collective-permute-done((bf16[80,2048]{1,0:T(8,128)(2,1)S(1)}, bf16[80,2048]{1,0:T(8,128)(2,1)S(1)}, u32[]{:S(2)}, u32[]{:S(2)}) %collective-permute-start.35) | collective-permute-done | bytes 327712 | tf_op jit(solution)/shard_map/ppermute | solution.py:28
  222.0 4.0 %collective-permute-done.28 = bf16[80,2048]{1,0:T(8,128)(2,1)S(1)} collective-permute-done((bf16[80,2048]{1,0:T(8,128)(2,1)S(1)}, bf16[80,2048]{1,0:T(8,128)(2,1)S(1)}, u32[]{:S(2)}, u32[]{:S(2)}) %collective-permute-start.28) | collective-permute-done | bytes 327712 | tf_op jit(solution)/shard_map/ppermute | solution.py:28
  228.8 8.7 %collective-permute-done.30 = bf16[80,2048]{1,0:T(8,128)(2,1)S(1)} collective-permute-done((bf16[80,2048]{1,0:T(8,128)(2,1)S(1)}, bf16[80,2048]{1,0:T(8,128)(2,1)S(1)}, u32[]{:S(2)}, u32[]{:S(2)}) %collective-permute-start.30) | collective-permute-done | bytes 327712 | tf_op jit(solution)/shard_map/ppermute | solution.py:28
  243.3 8.3 %collective-permute-done.24 = bf16[80,2048]{1,0:T(8,128)(2,1)S(1)} collective-permute-done((bf16[80,2048]{1,0:T(8,128)(2,1)S(1)}, bf16[80,2048]{1,0:T(8,128)(2,1)S(1)}, u32[]{:S(2)}, u32[]{:S(2)}) %collective-permute-start.24) | collective-permute-done | bytes 327712 | tf_op jit(solution)/shard_map/ppermute | solution.py:28
  260.4 7.9 %collective-permute-done.36 = bf16[128,2048]{1,0:T(8,128)(2,1)S(1)} collective-permute-done((bf16[128,2048]{1,0:T(8,128)(2,1)S(1)}, bf16[128,2048]{1,0:T(8,128)(2,1)S(1)}, u32[]{:S(2)}, u32[]{:S(2)}) %collective-permute-start.36) | collective-permute-done | bytes 524320 | tf_op jit(solution)/shard_map/ppermute | solution.py:33
  269.1 12.0 %collective-permute-done.31 = bf16[128,2048]{1,0:T(8,128)(2,1)S(1)} collective-permute-done((bf16[128,2048]{1,0:T(8,128)(2,1)S(1)}, bf16[128,2048]{1,0:T(8,128)(2,1)S(1)}, u32[]{:S(2)}, u32[]{:S(2)}) %collective-permute-start.31) | collective-permute-done | bytes 524320 | tf_op jit(solution)/shard_map/ppermute | solution.py:33
  284.3 3.1 fusion.83
  290.9 3.6 fusion.51
  301.9 20.1 %collective-permute-done.57 = bf16[64,256]{1,0:T(8,128)(2,1)S(1)} collective-permute-done((bf16[64,256]{1,0:T(8,128)(2,1)}, bf16[64,256]{1,0:T(8,128)(2,1)S(1)}, u32[]{:S(2)}, u32[]{:S(2)}) %collective-permute-start.57) | collective-permute-done | bytes 32800 | tf_op jit(solution)/shard_map/ppermute | solution.py:28
  322.0 11.2 %collective-permute-start.59 = (f32[64,256]{1,0:T(8,128)S(1)}, f32[64,256]{1,0:T(8,128)S(1)}, u32[]{:S(2)}, u32[]{:S(2)}) collective-permute-start(f32[64,256]{1,0:T(8,128)S(1)} %fusion.185), channel_id=1, source_target_pairs={{0,24},{8,0},{16,8},{24,16},{1,25},{9,1},{17,9},{25,17},{2,26},{10... | collective-permute-start | bytes 196616 | tf_op jit(solution)/shard_map/ppermute | solution.py:33
  336.8 3.4 collective-permute-done.60
  342.9 3.8 collective-permute-done.61
  348.7 9.6 %head_gradients.1 = (bf16[1024,512]{1,0:T(8,128)(2,1)}, bf16[1024,64]{1,0:T(8,128)(2,1)}) custom-call(s32[2]{0:T(128)} %pad_add_fusion.place, bf16[128,2048]{1,0:T(8,128)(2,1)} %copy-done.16, bf16[128,2048]{1,0:T(8,128)(2,1)} %copy-done.39, bf16[128,2048]{1,0:T(8,128)(2,1)} %copy-done.40, bf16[128,2048]{1,0:T(8,128)(2,1)} %copy-done.41, ...), custom_call_target="tpu_custom_call" | custom-call | tf_op jit(solution)/shard_map/head_gradients/pallas_call | solution.py:141
  358.3 11.9 %attention_backward.1 = (f32[1024,512]{1,0:T(8,128)}, f32[4,128,256]{2,1,0:T(8,128)}, bf16[4,128,256]{2,1,0:T(8,128)(2,1)}) custom-call(s32[2]{0:T(128)} %pad_add_fusion.place, bf16[1024,512]{1,0:T(8,128)(2,1)} %q_ref.3, bf16[1024,512]{1,0:T(8,128)(2,1)} %k_ref.3, bf16[1024,512]{1,0:T(8,128)(2,1)} %v_ref.3, bf16[1024,512]{1,0:T(8,128)(2,1)} %get-tuple-element.21.g_ref, ...), custom_call_target="tpu_custom_call" | custom-call | tf_op jit(solution)/shard_map/attention_backward/pallas_call | solution.py:206
  370.3 9.3 %all_gather.3 = f32[64,2048]{1,0:T(8,128)S(1)} all-gather(f32[64,256]{1,0:T(8,128)S(1)} %select_add_fusion), channel_id=1, replica_groups=mesh['grp'=4,'dev'=8] {'dev'}, dimensions={1}, use_global_device_ids=true | all-gather | bytes 589824 | tf_op jit(solution)/shard_map/all_gather | solution.py:426
  (464 shorter events, 190.6 us)
Async XLA Ops:
  0.6 79.0 %collective-permute-start.1 = (bf16[128,2048]{1,0:T(8,128)(2,1)}, bf16[128,2048]{1,0:T(8,128)(2,1)}, u32[]{:S(2)}, u32[]{:S(2)}) collective-permute-start(bf16[128,2048]{1,0:T(8,128)(2,1)} %param.14), channel_id=1, source_target_pairs={{0,8},{8,16},{16,24},{24,0},{1,9},{9,17},{17,25},{25,1},{2,10},{10... | collective-permute-start | bytes 1572872 | tf_op jit(solution)/shard_map/ppermute | solution.py:33
  3.7 83.4 %collective-permute-start.7 = (bf16[128,2048]{1,0:T(8,128)(2,1)}, bf16[128,2048]{1,0:T(8,128)(2,1)}, u32[]{:S(2)}, u32[]{:S(2)}) collective-permute-start(bf16[128,2048]{1,0:T(8,128)(2,1)} %param.14), channel_id=1, source_target_pairs={{0,16},{8,24},{16,0},{24,8},{1,17},{9,25},{17,1},{25,9},{2,18},{10... | collective-permute-start | bytes 1572872 | tf_op jit(solution)/shard_map/ppermute | solution.py:33
  6.3 84.8 %collective-permute-start.13 = (bf16[128,2048]{1,0:T(8,128)(2,1)}, bf16[128,2048]{1,0:T(8,128)(2,1)}, u32[]{:S(2)}, u32[]{:S(2)}) collective-permute-start(bf16[128,2048]{1,0:T(8,128)(2,1)} %param.14), channel_id=1, source_target_pairs={{0,24},{8,0},{16,8},{24,16},{1,25},{9,1},{17,9},{25,17},{2,26},{10... | collective-permute-start | bytes 1572872 | tf_op jit(solution)/shard_map/ppermute | solution.py:33
  10.0 47.2 %collective-permute-start = (f32[2,8,128]{2,1,0:T(8,128)}, f32[2,8,128]{2,1,0:T(8,128)}, u32[]{:S(2)}, u32[]{:S(2)}) collective-permute-start(f32[2,8,128]{2,1,0:T(8,128)} %get-tuple-element.164), channel_id=1, source_target_pairs={{0,8},{8,16},{16,24},{24,0},{1,9},{9,17},{17,25},{25,1},{2,10},{10... | collective-permute-start | bytes 24584 | tf_op jit(solution)/shard_map/ppermute | solution.py:33
  10.7 39.4 %collective-permute-start.12 = (f32[2,8,128]{2,1,0:T(8,128)}, f32[2,8,128]{2,1,0:T(8,128)}, u32[]{:S(2)}, u32[]{:S(2)}) collective-permute-start(f32[2,8,128]{2,1,0:T(8,128)} %get-tuple-element.162), channel_id=1, source_target_pairs={{0,24},{8,0},{16,8},{24,16},{1,25},{9,1},{17,9},{25,17},{2,26},{10... | collective-permute-start | bytes 24584 | tf_op jit(solution)/shard_map/ppermute | solution.py:33
  54.7 24.7 %collective-permute-start.20 = (bf16[80,2048]{1,0:T(8,128)(2,1)S(1)}, bf16[80,2048]{1,0:T(8,128)(2,1)S(1)}, u32[]{:S(2)}, u32[]{:S(2)}) collective-permute-start(bf16[80,2048]{1,0:T(8,128)(2,1)S(1)} %copy-done.51), channel_id=1, source_target_pairs={{0,6},{1,7},{2,4},{3,5},{4,2},{5,3},{6,0},{7,1},{8,14},{9,15},{10,... | collective-permute-start | bytes 983048 | tf_op jit(solution)/shard_map/ppermute | solution.py:28
  79.5 48.6 %collective-permute-start.21 = (bf16[160,2048]{1,0:T(8,128)(2,1)S(1)}, bf16[160,2048]{1,0:T(8,128)(2,1)S(1)}, u32[]{:S(2)}, u32[]{:S(2)}) collective-permute-start(bf16[160,2048]{1,0:T(8,128)(2,1)S(1)} %pad_maximum_fusion.3), channel_id=1, source_target_pairs={{0,1},{1,0},{2,3},{3,2},{4,5},{5,4},{6,7},{7,6},{8,9},{9,8},{10,11... | collective-permute-start | bytes 1966088 | tf_op jit(solution)/shard_map/ppermute | solution.py:28
  91.1 24.8 %collective-permute-start.10 = (bf16[80,2048]{1,0:T(8,128)(2,1)S(1)}, bf16[80,2048]{1,0:T(8,128)(2,1)S(1)}, u32[]{:S(2)}, u32[]{:S(2)}) collective-permute-start(bf16[80,2048]{1,0:T(8,128)(2,1)S(1)} %fusion.59), channel_id=1, source_target_pairs={{0,6},{1,7},{2,4},{3,5},{4,2},{5,3},{6,0},{7,1},{8,14},{9,15},{10,... | collective-permute-start | bytes 983048 | tf_op jit(solution)/shard_map/ppermute | solution.py:28
  102.7 24.6 %collective-permute-start.16 = (bf16[80,2048]{1,0:T(8,128)(2,1)S(1)}, bf16[80,2048]{1,0:T(8,128)(2,1)S(1)}, u32[]{:S(2)}, u32[]{:S(2)}) collective-permute-start(bf16[80,2048]{1,0:T(8,128)(2,1)S(1)} %fusion.63), channel_id=1, source_target_pairs={{0,6},{1,7},{2,4},{3,5},{4,2},{5,3},{6,0},{7,1},{8,14},{9,15},{10,... | collective-permute-start | bytes 983048 | tf_op jit(solution)/shard_map/ppermute | solution.py:28
  115.9 49.8 %collective-permute-start.5 = (bf16[160,2048]{1,0:T(8,128)(2,1)}, bf16[160,2048]{1,0:T(8,128)(2,1)}, u32[]{:S(2)}, u32[]{:S(2)}) collective-permute-start(bf16[160,2048]{1,0:T(8,128)(2,1)} %pad_maximum_fusion), channel_id=1, source_target_pairs={{0,1},{1,0},{2,3},{3,2},{4,5},{5,4},{6,7},{7,6},{8,9},{9,8},{10,11... | collective-permute-start | bytes 1966088 | tf_op jit(solution)/shard_map/ppermute | solution.py:28
  126.3 28.9 %collective-permute-start.11 = (bf16[160,2048]{1,0:T(8,128)(2,1)}, bf16[160,2048]{1,0:T(8,128)(2,1)}, u32[]{:S(2)}, u32[]{:S(2)}) collective-permute-start(bf16[160,2048]{1,0:T(8,128)(2,1)} %pad_maximum_fusion.1), channel_id=1, source_target_pairs={{0,1},{1,0},{2,3},{3,2},{4,5},{5,4},{6,7},{7,6},{8,9},{9,8},{10,11... | collective-permute-start | bytes 1966088 | tf_op jit(solution)/shard_map/ppermute | solution.py:28
  138.8 45.0 %collective-permute-start.37 = (bf16[160,2048]{1,0:T(8,128)(2,1)}, bf16[160,2048]{1,0:T(8,128)(2,1)}, u32[]{:S(2)}, u32[]{:S(2)}) collective-permute-start(bf16[160,2048]{1,0:T(8,128)(2,1)} %fusion.45), channel_id=1, source_target_pairs={{0,1},{1,0},{2,3},{3,2},{4,5},{5,4},{6,7},{7,6},{8,9},{9,8},{10,11... | collective-permute-start | bytes 1966088 | tf_op jit(solution)/shard_map/ppermute | solution.py:28
  185.5 70.7 %collective-permute-start.38 = (bf16[80,2048]{1,0:T(8,128)(2,1)S(1)}, bf16[80,2048]{1,0:T(8,128)(2,1)S(1)}, u32[]{:S(2)}, u32[]{:S(2)}) collective-permute-start(bf16[80,2048]{1,0:T(8,128)(2,1)S(1)} %pad_maximum_fusion.21), channel_id=1, source_target_pairs={{0,2},{1,3},{2,0},{3,1},{4,6},{5,7},{6,4},{7,5},{8,10},{9,11},{10,... | collective-permute-start | bytes 983048 | tf_op jit(solution)/shard_map/ppermute | solution.py:28
  186.3 72.1 %collective-permute-start.39 = (bf16[80,2048]{1,0:T(8,128)(2,1)S(1)}, bf16[80,2048]{1,0:T(8,128)(2,1)S(1)}, u32[]{:S(2)}, u32[]{:S(2)}) collective-permute-start(bf16[80,2048]{1,0:T(8,128)(2,1)S(1)} %pad_maximum_fusion.22), channel_id=1, source_target_pairs={{0,4},{1,5},{2,6},{3,7},{4,0},{5,1},{6,2},{7,3},{8,12},{9,13},{10,... | collective-permute-start | bytes 983048 | tf_op jit(solution)/shard_map/ppermute | solution.py:28
  187.3 72.0 %collective-permute-start.40 = (bf16[80,2048]{1,0:T(8,128)(2,1)S(1)}, bf16[80,2048]{1,0:T(8,128)(2,1)S(1)}, u32[]{:S(2)}, u32[]{:S(2)}) collective-permute-start(bf16[80,2048]{1,0:T(8,128)(2,1)S(1)} %pad_maximum_fusion.23), channel_id=1, source_target_pairs={{0,6},{1,7},{2,4},{3,5},{4,2},{5,3},{6,0},{7,1},{8,14},{9,15},{10,... | collective-permute-start | bytes 983048 | tf_op jit(solution)/shard_map/ppermute | solution.py:28
  255.3 25.7 %collective-permute-start.31 = (bf16[128,2048]{1,0:T(8,128)(2,1)S(1)}, bf16[128,2048]{1,0:T(8,128)(2,1)S(1)}, u32[]{:S(2)}, u32[]{:S(2)}) collective-permute-start(bf16[128,2048]{1,0:T(8,128)(2,1)S(1)} %convolution_convert_fusion.5), channel_id=1, source_target_pairs={{0,16},{8,24},{16,0},{24,8},{1,17},{9,25},{17,1},{25,9},{2,18},{10... | collective-permute-start | bytes 1572872 | tf_op jit(solution)/shard_map/ppermute | solution.py:33
  256.2 24.8 %collective-permute-start.26 = (bf16[128,2048]{1,0:T(8,128)(2,1)S(1)}, bf16[128,2048]{1,0:T(8,128)(2,1)S(1)}, u32[]{:S(2)}, u32[]{:S(2)}) collective-permute-start(bf16[128,2048]{1,0:T(8,128)(2,1)S(1)} %convolution_convert_fusion.6), channel_id=1, source_target_pairs={{0,24},{8,0},{16,8},{24,16},{1,25},{9,1},{17,9},{25,17},{2,26},{10... | collective-permute-start | bytes 1572872 | tf_op jit(solution)/shard_map/ppermute | solution.py:33
  258.4 23.2 %collective-permute-start.54 = (bf16[64,128]{1,0:T(8,128)(2,1)S(1)}, bf16[64,128]{1,0:T(8,128)(2,1)S(1)}, u32[]{:S(2)}, u32[]{:S(2)}) collective-permute-start(bf16[64,128]{1,0:T(8,128)(2,1)S(1)} %copy-done.66), channel_id=1, source_target_pairs={{0,6},{1,7},{2,4},{3,5},{4,2},{5,3},{6,0},{7,1},{8,14},{9,15},{10,... | collective-permute-start | bytes 49160 | tf_op jit(solution)/shard_map/ppermute | solution.py:28
  259.3 22.4 %collective-permute-start.53 = (bf16[64,128]{1,0:T(8,128)(2,1)S(1)}, bf16[64,128]{1,0:T(8,128)(2,1)S(1)}, u32[]{:S(2)}, u32[]{:S(2)}) collective-permute-start(bf16[64,128]{1,0:T(8,128)(2,1)S(1)} %copy-done.65), channel_id=1, source_target_pairs={{0,4},{1,5},{2,6},{3,7},{4,0},{5,1},{6,2},{7,3},{8,12},{9,13},{10,... | collective-permute-start | bytes 49160 | tf_op jit(solution)/shard_map/ppermute | solution.py:28
  294.5 41.4 %collective-permute-start.41 = (bf16[128,2048]{1,0:T(8,128)(2,1)}, bf16[128,2048]{1,0:T(8,128)(2,1)S(1)}, u32[]{:S(2)}, u32[]{:S(2)}) collective-permute-start(bf16[128,2048]{1,0:T(8,128)(2,1)} %copy-done.16), channel_id=1, source_target_pairs={{0,2},{1,3},{2,0},{3,1},{4,6},{5,7},{6,4},{7,5},{8,10},{9,11},{10,... | collective-permute-start | bytes 1572872 | tf_op jit(solution)/shard_map/ppermute | solution.py:28
  296.0 39.9 %collective-permute-start.42 = (bf16[128,2048]{1,0:T(8,128)(2,1)}, bf16[128,2048]{1,0:T(8,128)(2,1)S(1)}, u32[]{:S(2)}, u32[]{:S(2)}) collective-permute-start(bf16[128,2048]{1,0:T(8,128)(2,1)} %copy-done.16), channel_id=1, source_target_pairs={{0,4},{1,5},{2,6},{3,7},{4,0},{5,1},{6,2},{7,3},{8,12},{9,13},{10,... | collective-permute-start | bytes 1572872 | tf_op jit(solution)/shard_map/ppermute | solution.py:28
  297.1 39.3 %collective-permute-start.43 = (bf16[128,2048]{1,0:T(8,128)(2,1)}, bf16[128,2048]{1,0:T(8,128)(2,1)S(1)}, u32[]{:S(2)}, u32[]{:S(2)}) collective-permute-start(bf16[128,2048]{1,0:T(8,128)(2,1)} %copy-done.16), channel_id=1, source_target_pairs={{0,6},{1,7},{2,4},{3,5},{4,2},{5,3},{6,0},{7,1},{8,14},{9,15},{10,... | collective-permute-start | bytes 1572872 | tf_op jit(solution)/shard_map/ppermute | solution.py:28
  298.0 23.9 %collective-permute-start.57 = (bf16[64,256]{1,0:T(8,128)(2,1)}, bf16[64,256]{1,0:T(8,128)(2,1)S(1)}, u32[]{:S(2)}, u32[]{:S(2)}) collective-permute-start(bf16[64,256]{1,0:T(8,128)(2,1)} %get-tuple-element.126), channel_id=1, source_target_pairs={{0,4},{1,5},{2,6},{3,7},{4,0},{5,1},{6,2},{7,3},{8,12},{9,13},{10,... | collective-permute-start | bytes 98312 | tf_op jit(solution)/shard_map/ppermute | solution.py:28
  299.1 22.8 %collective-permute-start.56 = (bf16[64,256]{1,0:T(8,128)(2,1)}, bf16[64,256]{1,0:T(8,128)(2,1)S(1)}, u32[]{:S(2)}, u32[]{:S(2)}) collective-permute-start(bf16[64,256]{1,0:T(8,128)(2,1)} %get-tuple-element.124), channel_id=1, source_target_pairs={{0,2},{1,3},{2,0},{3,1},{4,6},{5,7},{6,4},{7,5},{8,10},{9,11},{10,... | collective-permute-start | bytes 98312 | tf_op jit(solution)/shard_map/ppermute | solution.py:28
  (114 other events, 1250.0 us)

commit v2 on v1

v2 whole, which is shorter than its diff:
```python
import functools

import jax
import jax.numpy as jnp
from jax import lax
from jax.experimental import pallas as pl
from jax.experimental.pallas import tpu as pltpu
from jax.sharding import PartitionSpec as P

QUERY_HEADS = 32
KVH = 4
HEAD_SIZE = 128

adapter_scale = 2.0
neg_big = -1e30
att_scale = HEAD_SIZE ** (-0.5)
VMEM_BYTES = 56 * 1024 * 1024
COST_UNIT = 1000000


def contraction(left, right, left_dim, right_dim):
    return lax.dot_general(
        left, right, (((left_dim,), (right_dim,)), ((), ())), preferred_element_type=jnp.float32
    )


def across(value, step):
    count = lax.axis_size("dev")
    return lax.ppermute(value, "dev", [(i, i ^ step) for i in range(count)])


def shift(value, step):
    count = lax.axis_size("grp")
    return lax.ppermute(value, "grp", [(i, (i + step) % count) for i in range(count)])


def unread(count):
    return [pl.BlockSpec(memory_space=pl.ANY)] * count


def estimate(cost):
    return pl.CostEstimate(flops=0, bytes_accessed=int(cost * COST_UNIT), transcendentals=0)


def whole_of(shape):
    return pl.BlockSpec(shape, lambda i, place: (0,) * len(shape))


def kernel_call(body, place, operands, specs, outs, out_specs, after, scratch=(), steps=1, name=None, cost=1.0):
    deps = len(after)

    def kernel(place_ref, *refs):
        count = len(operands)
        body(place_ref, *refs[:count], *refs[count + deps :])

    return pl.pallas_call(
        kernel,
        grid_spec=pltpu.PrefetchScalarGridSpec(
            num_scalar_prefetch=1,
            grid=(steps,),
            in_specs=[*specs, *unread(deps)],
            out_specs=out_specs,
            scratch_shapes=list(scratch),
        ),
        out_shape=outs,
        compiler_params=pltpu.CompilerParams(
            dimension_semantics=("arbitrary",), vmem_limit_bytes=VMEM_BYTES
        ),
        cost_estimate=estimate(cost),
        name=name,
    )(place, *operands, *after)


def bf16(*shape):
    return jax.ShapeDtypeStruct(shape, jnp.bfloat16)


def f32(*shape):
    return jax.ShapeDtypeStruct(shape, jnp.float32)


def filled_cells(ranks, count):
    cell = lax.broadcasted_iota(jnp.int32, (count, ranks.shape[1]), 0).astype(jnp.float32)
    return ranks == cell


def chip_part(place_ref, refs, j):
    return refs[0].at[(place_ref[0] // 2) ^ j] if len(refs) == 1 else refs[j]


def dispatch(place, own, other, tables, cells, stacked, after):
    planes = len(own)
    pairs = tables[0].shape[1]
    width = own[0].shape[1]

    def body(place_ref, *refs):
        for i in range(planes):
            own_ref, other_ref, table_ref = refs[i], refs[planes + i], refs[2 * planes + i]
            tokens = jnp.concatenate([own_ref[...], other_ref[...]], axis=0)
            for j in range(pairs):
                filled = filled_cells(table_ref[0, j : j + 1, :], cells)
                weight = jnp.sum(
                    jnp.where(filled, table_ref[1, j : j + 1, :], 0.0), axis=1, keepdims=True
                )
                rows = jnp.dot(
                    filled.astype(jnp.bfloat16), tokens, preferred_element_type=jnp.float32
                )
                out = chip_part(place_ref, refs[3 * planes :], j)
                out[i * cells : (i + 1) * cells, :] = (rows * weight).astype(jnp.bfloat16)

    operands = [*own, *other, *tables]
    outs = [bf16(planes * cells, width)] * pairs
    if stacked:
        outs = [bf16(pairs, planes * cells, width)]
    return kernel_call(
        body,
        place,
        operands,
        [whole_of(a.shape) for a in operands],
        outs,
        [whole_of(a.shape) for a in outs],
        after,
        name="dispatch",
        cost=3.5,
    )


def combine(place, messages, tables, token_block, after):
    planes = len(tables)
    pairs, both = tables[0].shape[1:]
    cells, width = messages[0].shape[-2] // planes, messages[0].shape[-1]
    count = len(messages)

    def body(place_ref, *refs):
        for i in range(planes):
            table_ref = refs[count + i]
            own_ref, other_ref = refs[count + planes + 2 * i : count + planes + 2 * i + 2]
            total = None
            for j in range(pairs):
                filled = filled_cells(table_ref[0, j : j + 1, :], cells).astype(jnp.bfloat16)
                rows = chip_part(place_ref, refs[:count], j)[i * cells : (i + 1) * cells, :]
                part = contraction(filled, rows, 0, 0)
                total = part if total is None else total + part
            own_ref[...] = total[:token_block]
            other_ref[...] = total[token_block:].astype(jnp.bfloat16)

    operands = [*messages, *tables]
    outs = [f32(token_block, width), bf16(both - token_block, width)] * planes
    result = kernel_call(
        body,
        place,
        operands,
        [whole_of(a.shape) for a in operands],
        outs,
        [whole_of(a.shape) for a in outs],
        after,
        name="combine",
        cost=4.5,
    )
    return result[::2], result[1::2]


def expert(
    place, steps, parts, saved, reorder, down, gate_up, first, second, cells, pairs, outs, after
):
    planes = len(steps)
    chunk = cells * pairs
    rows = planes * chunk
    width_ff, width = down.shape
    rank = first.shape[0]
    span = 256
    blocks = width_ff // span
    sides = 2
    columns = width // sides
    count, results = len(parts), len(outs)
    split_in = count > 1 or parts[0].ndim == 3
    split_out = results > 1 or len(outs[0].shape) == 3

    def body(place_ref, *refs):
        rows_in = refs[:count]
        reorder_ref = refs[count]
        gates = refs[count + 1 : count + 1 + planes]
        ups = refs[count + 1 + planes : count + 1 + 2 * planes]
        down_ref, back_ref, first_ref, second_ref = refs[count + 1 + 2 * planes :][:4]
        rest = refs[count + 5 + 2 * planes :]
        rows_out, (grad_first_ref, grad_second_ref) = rest[:results], rest[results : results + 2]
        routed, low_grad, low_in, grad_pre = rest[results + 2 :]
        number = pl.program_id(0)

        @pl.when(number == 0)
        def _():
            if split_in:
                for i in range(planes):
                    for j in range(pairs):
                        at = i * chunk + j * cells
                        part = chip_part(place_ref, rows_in, j)
                        routed[at : at + cells, :] = part[i * cells : (i + 1) * cells, :]
            else:
                routed[...] = rows_in[0][...]
            low_grad[...] = contraction(routed[...], second_ref[...], 1, 1).astype(jnp.bfloat16)
            low_in[...] = jnp.zeros_like(low_in)

        for block in range(blocks):

            @pl.when(number == block)
            def _():
                order = reorder_ref[...]
                gate = [
                    jnp.dot(order, ref[...], preferred_element_type=jnp.float32) for ref in gates
                ]
                up = [jnp.dot(order, ref[...], preferred_element_type=jnp.float32) for ref in ups]
                gate = jnp.concatenate(gate, axis=0) if planes > 1 else gate[0]
                up = jnp.concatenate(up, axis=0) if planes > 1 else up[0]
                sigmoid = jax.nn.sigmoid(gate)
                active = gate * sigmoid
                slope = sigmoid * (1.0 + gate * (1.0 - sigmoid))
                hidden = (active * up).astype(jnp.bfloat16)
                low_in[...] += contraction(hidden, first_ref[...], 1, 1)
                grad_first_ref[...] = adapter_scale * contraction(low_grad[...], hidden, 0, 0)
                grad_hidden = contraction(
                    routed[...], down_ref[...], 1, 1
                ) + adapter_scale * jnp.dot(
                    low_grad[...], first_ref[...], preferred_element_type=jnp.float32
                )
                at = block * span
                grad_pre[:, at : at + span] = (grad_hidden * up * slope).astype(jnp.bfloat16)
                grad_pre[:, width_ff + at : width_ff + at + span] = (grad_hidden * active).astype(
                    jnp.bfloat16
                )

        for side in range(sides):

            @pl.when(number == blocks + side)
            def _():
                result = contraction(grad_pre[...], back_ref[...], 1, 1).astype(jnp.bfloat16)
                if split_out:
                    for i in range(planes):
                        for j in range(pairs):
                            at = i * chunk + j * cells
                            part = chip_part(place_ref, rows_out, j)
                            part[i * cells : (i + 1) * cells, :] = result[at : at + cells]
                else:
                    rows_out[0][...] = result
                grad_second_ref[...] = adapter_scale * contraction(
                    low_in[...].astype(jnp.bfloat16),
                    routed[:, side * columns : (side + 1) * columns],
                    0,
                    0,
                )

    def inner(i):
        return jnp.minimum(i, blocks - 1)

    def outer(i):
        return jnp.maximum(i - blocks, 0)

    def saved_block(step, offset):
        return pl.BlockSpec(
            (chunk, span), lambda i, place: (place[2 + step], offset + inner(i))
        )

    specs = [
        *[whole_of(a.shape) for a in parts],
        whole_of(reorder.shape),
        *[saved_block(step, 0) for step in steps],
        *[saved_block(step, blocks) for step in steps],
        pl.BlockSpec((span, width), lambda i, place: (inner(i), 0)),
        pl.BlockSpec((columns, 2 * width_ff), lambda i, place: (outer(i), 0)),
        pl.BlockSpec((rank, span), lambda i, place: (0, inner(i))),
        whole_of(second.shape),
    ]
    result = kernel_call(
        body,
        place,
        [*parts, reorder, *[saved] * (2 * planes), down, gate_up, first, second],
        specs,
        [*outs, f32(rank, width_ff), f32(rank, width)],
        [
            *[
                pl.BlockSpec(
                    (*a.shape[:-1], columns),
                    lambda i, place, lead=(0,) * (len(a.shape) - 1): (*lead, outer(i)),
                )
                for a in outs
            ],
            pl.BlockSpec((rank, span), lambda i, place: (0, inner(i))),
            pl.BlockSpec((rank, columns), lambda i, place: (0, outer(i))),
        ],
        after,
        scratch=[
            pltpu.VMEM((rows, width), jnp.bfloat16),
            pltpu.VMEM((rows, rank), jnp.bfloat16),
            pltpu.VMEM((rows, rank), jnp.float32),
            pltpu.VMEM((rows, 2 * width_ff), jnp.bfloat16),
        ],
        steps=blocks + sides,
        name="expert",
        cost=8.0 + 4.5 * planes,
    )
    return result[:results], result[results], result[results + 1]


def head_gradients(place, j, own, other, weight, first, second, attended, after):
    rows, width = own.shape
    heads_width = weight.shape[0]
    rank = first.shape[0]

    def body(place_ref, own_ref, other_ref, weight_ref, first_ref, second_ref, att_ref, grad_ref, term_ref):
        gradient = jnp.concatenate([own_ref[...], other_ref[...]], axis=0)
        low = contraction(gradient, second_ref[...], 1, 1).astype(jnp.bfloat16)
        result = contraction(gradient, weight_ref[...], 1, 1)
        result = result + adapter_scale * jnp.dot(
            low, first_ref[...], preferred_element_type=jnp.float32
        )
        grad_ref[...] = result.astype(jnp.bfloat16)
        core = place_ref[0] % 2
        term = None
        for half in range(2):
            at = pl.ds(pl.multiple_of((core ^ half) * rows, rows), rows)
            part = contraction(low[half * rows : (half + 1) * rows], att_ref[at, :], 0, 0)
            term = part if term is None else term + part
        term_ref[...] = adapter_scale * term

    operands = [own, other, weight, first, second, attended]
    specs = [whole_of(a.shape) for a in operands[:5]] + [
        pl.BlockSpec((2 * rows, heads_width), lambda i, place: ((place[0] // 2) ^ j, 0))
    ]
    outs = [bf16(2 * rows, heads_width), f32(rank, heads_width)]
    return kernel_call(
        body, place, operands, specs, outs, [whole_of(a.shape) for a in outs], after, name="head_gradients", cost=4.7
    )


def forward_kernel(place, q_ref, k_ref, v_ref, a_ref, *refs):
    probs_ref, att_ref, folded = refs[-3:]
    head = pl.program_id(0)
    rows = q_ref.shape[0]
    token_block = folded.shape[2]
    block = min(256, rows)

    @pl.when(head == 0)
    def _():
        folded[...] = jnp.zeros_like(folded)

    for first in range(0, rows, block):
        last = first + block
        scores = contraction(q_ref[first:last, :], k_ref[:last, :], 1, 1) * att_scale
        row = first + lax.broadcasted_iota(jnp.int32, scores.shape, 0)
        column = lax.broadcasted_iota(jnp.int32, scores.shape, 1)
        scores = jnp.where(row >= column, scores, neg_big)
        weights = jnp.exp(scores - jnp.max(scores, axis=1, keepdims=True))
        weights = weights * (1.0 / jnp.sum(weights, axis=1, keepdims=True))
        low = weights.astype(jnp.bfloat16)
        probs_ref[0, first:last, :last] = low
        attended = jnp.dot(low, v_ref[:last, :], preferred_element_type=jnp.float32).astype(
            jnp.bfloat16
        )
        att_ref[first:last, :] = attended
        part = contraction(a_ref[...], attended, 1, 1).astype(jnp.bfloat16).astype(jnp.float32)
        for inner in range(0, block, token_block):
            number = (first + inner) // token_block
            folded[number] = folded[number] + part[:, inner : inner + token_block]


def attention_forward(place, queries, keys, values, first_factor, token_block, span, earlier, after):
    rows, width = queries.shape
    heads = width // HEAD_SIZE
    rank = first_factor.shape[0]
    start, count = span
    of_head = pl.BlockSpec((rows, HEAD_SIZE), lambda h, place: (0, start + h))
    of_group = pl.BlockSpec((rows, HEAD_SIZE), lambda h, place: (0, place[1]))
    part = (rows // token_block, rank, token_block)
    return pl.pallas_call(
        forward_kernel,
        grid_spec=pltpu.PrefetchScalarGridSpec(
            num_scalar_prefetch=1,
            grid=(count,),
            in_specs=[
                of_head,
                of_group,
                of_group,
                pl.BlockSpec((rank, HEAD_SIZE), lambda h, place: (0, start + h)),
                *unread(len(earlier) + len(after)),
            ],
            out_specs=[
                pl.BlockSpec((1, rows, rows), lambda h, place: (start + h, 0, 0)),
                of_head,
                pl.BlockSpec(part, lambda h, place: (0, 0, 0)),
            ],
        ),
        out_shape=[
            bf16(heads, rows, rows),
            bf16(rows, width),
            f32(*part),
        ],
        input_output_aliases={5 + n: n for n in range(len(earlier))},
        compiler_params=pltpu.CompilerParams(
            dimension_semantics=("arbitrary",), vmem_limit_bytes=VMEM_BYTES
        ),
        cost_estimate=estimate(2.2 * rows / 512 * count),
        name="attention_forward",
    )(place, queries, keys, values, first_factor, *earlier, *after)


def backward_kernel(place, q_ref, k_ref, v_ref, att_ref, probs_ref, *refs):
    dq_ref, even_ref, odd_ref, dk, dv, g_ref = refs[-6:]
    head = pl.program_id(0)
    rows = q_ref.shape[0]
    block = min(256, rows)
    pairs, token_block = even_ref.shape[:2]
    for j in range(pairs):
        for half in range(2):
            number = place[0] ^ (2 * j + half)
            at = pl.ds(pl.multiple_of(number * token_block, token_block), token_block)
            g_ref[at, :] = refs[j][half * token_block : (half + 1) * token_block, :]

    @pl.when(head == 0)
    def _():
        dk[...] = jnp.zeros_like(dk)
        dv[...] = jnp.zeros_like(dv)

    for first in range(0, rows, block):
        last = first + block
        gradient = g_ref[first:last, :]
        query = q_ref[first:last, :]
        probs = probs_ref[0, first:last, :last]
        grad_probs = contraction(gradient, v_ref[:last, :], 1, 1)
        delta = jnp.sum(
            gradient.astype(jnp.float32) * att_ref[first:last, :].astype(jnp.float32),
            axis=1,
            keepdims=True,
        )
        grad_scores = (probs.astype(jnp.float32) * (grad_probs - delta)).astype(jnp.bfloat16)
        dq_ref[first:last, :] = att_scale * jnp.dot(
            grad_scores, k_ref[:last, :], preferred_element_type=jnp.float32
        )
        dk[:last, :] += contraction(grad_scores, query, 0, 0)
        dv[:last, :] += contraction(probs, gradient, 0, 0)

    @pl.when(head == pl.num_programs(0) - 1)
    def _():
        for j in range(even_ref.shape[0]):
            for half, ref in enumerate((even_ref, odd_ref)):
                number = place[0] ^ (2 * j + half)
                at = pl.ds(pl.multiple_of(number * token_block, token_block), token_block)
                ref[j, :, :HEAD_SIZE] = (dk[at, :] * att_scale).astype(ref.dtype)
                ref[j, :, HEAD_SIZE:] = dv[at, :].astype(ref.dtype)


def attention_backward(place, queries, keys, values, attended, probs, gradients, token_block, after):
    rows, width = queries.shape
    heads = width // HEAD_SIZE
    pairs = rows // token_block // 2
    of_head = pl.BlockSpec((rows, HEAD_SIZE), lambda h, place: (0, h))
    of_group = pl.BlockSpec((rows, HEAD_SIZE), lambda h, place: (0, place[1]))
    part = pl.BlockSpec((pairs, token_block, 2 * HEAD_SIZE), lambda h, place: (0, 0, 0))
    part_shape = (pairs, token_block, 2 * HEAD_SIZE)
    return pl.pallas_call(
        backward_kernel,
        grid_spec=pltpu.PrefetchScalarGridSpec(
            num_scalar_prefetch=1,
            grid=(heads,),
            in_specs=[
                of_head,
                of_group,
                of_group,
                of_head,
                pl.BlockSpec((1, rows, rows), lambda h, place: (h, 0, 0)),
                *[pl.BlockSpec((2 * token_block, HEAD_SIZE), lambda h, place: (0, h))] * pairs,
                *unread(len(after)),
            ],
            out_specs=[of_head, part, part],
            scratch_shapes=[
                pltpu.VMEM((rows, HEAD_SIZE), jnp.float32),
                pltpu.VMEM((rows, HEAD_SIZE), jnp.float32),
                pltpu.VMEM((rows, HEAD_SIZE), jnp.bfloat16),
            ],
        ),
        out_shape=[
            jax.ShapeDtypeStruct((rows, width), jnp.float32),
            jax.ShapeDtypeStruct(part_shape, jnp.float32),
            jax.ShapeDtypeStruct(part_shape, jnp.bfloat16),
        ],
        compiler_params=pltpu.CompilerParams(
            dimension_semantics=("arbitrary",), vmem_limit_bytes=VMEM_BYTES
        ),
        cost_estimate=estimate(11.8),
        name="attention_backward",
    )(place, queries, keys, values, attended, probs, *gradients, *after)


def planes_sum(parts, grp_index):
    count = len(parts)
    total = None
    for plane in range(count):
        term = parts[0].astype(jnp.float32)
        for step in range(1, count):
            here = (grp_index - step) % count == plane
            term = jnp.where(here, parts[step].astype(jnp.float32), term)
        total = term if total is None else total + term
    return total


def on_device(
    output_gradient,
    expert_choice_index,
    routing_weight,
    stored_gate_preact,
    gate_up_weight,
    down_weight,
    down_first_factor,
    down_second_factor,
    rotated_queries,
    rotated_keys,
    stored_values,
    output_weight,
    output_first_factor,
    output_second_factor,
):
    tok_rows, model_width = output_gradient.shape
    top_count = expert_choice_index.shape[1]
    grp_count = lax.axis_size("grp")
    dev_count = lax.axis_size("dev")
    pairs = dev_count // 2
    experts = grp_count * dev_count
    slot_count = stored_gate_preact.shape[1]
    capacity = slot_count // experts
    cells = 2 * capacity
    chunk = dev_count * capacity
    grp_index = lax.axis_index("grp")
    dev_index = lax.axis_index("dev")
    heads = rotated_queries.shape[1] // HEAD_SIZE
    group_size = QUERY_HEADS // KVH
    planes = (grp_index - jnp.arange(grp_count, dtype=jnp.int32)) % grp_count
    place = jnp.concatenate(
        [jnp.stack([dev_index, dev_index * heads // group_size]).astype(jnp.int32), planes]
    )

    ring = sorted(range(1, grp_count), key=lambda s: (min(s, grp_count - s), s))
    middle = (2 * len(ring) + 2) // 3
    groups = [g for g in ([0], ring[:middle], ring[middle:]) if g]

    choice = jnp.concatenate(
        [expert_choice_index.T.astype(jnp.float32), routing_weight.T], axis=0
    )
    tokens = {0: output_gradient}
    near_tokens = {0: across(output_gradient, 1)}
    choice = jnp.stack([choice, across(choice, 1)])

    token = jnp.arange(tok_rows, dtype=jnp.int32)
    earlier = (token[:, None] < token[None, :]).astype(jnp.bfloat16)
    plane_experts = (
        grp_index * dev_count + (dev_index ^ (2 * jnp.arange(pairs, dtype=jnp.int32)))
    ).astype(jnp.float32)

    def table_of(choice):
        ids, weights = choice[:, :top_count], choice[:, top_count:]
        named = ids[:, :, None, :] == plane_experts[None, None, :, None]
        chosen = jnp.any(named, axis=1)
        weight_of = jnp.sum(jnp.where(named, weights[:, :, None, :], 0.0), axis=1)
        rank_of = lax.dot_general(
            chosen.astype(jnp.bfloat16),
            earlier,
            (((2,), (0,)), ((), ())),
            preferred_element_type=jnp.float32,
        )
        first_cell = jnp.arange(2, dtype=jnp.float32)[:, None, None] * capacity
        ranks = jnp.where(chosen, rank_of + first_cell, -1.0)
        return jnp.stack(
            [
                jnp.concatenate([ranks[0], ranks[1]], axis=1),
                jnp.concatenate([weight_of[0], weight_of[1]], axis=1),
            ]
        )

    tables = {0: table_of(choice)}

    line = jnp.arange(chunk, dtype=jnp.int32)
    saved_line = (dev_index ^ (line // capacity)) * capacity + line % capacity
    reorder = (saved_line[:, None] == line[None, :]).astype(jnp.bfloat16)

    aligned = cells % 16 == 0
    last = []

    chips = [[2 * j + core for j in range(pairs)] for core in range(2)]

    def exchanged(parts):
        if len(parts) == 1:
            return [
                lax.all_to_all(parts[0], "dev", 0, 0, axis_index_groups=chips, tiled=True)
            ]
        return [parts[0]] + [across(parts[j], 2 * j) for j in range(1, pairs)]

    def dispatched(group, stacked):
        messages = dispatch(
            place,
            [tokens[s] for s in group],
            [near_tokens[s] for s in group],
            [tables[s] for s in group],
            cells,
            stacked and aligned,
            last,
        )
        last[:] = messages[:1]
        return exchanged(messages)

    def worked(group, parts, stacked):
        rows = len(group) * cells
        if not aligned:
            parts = [part.reshape(len(group), cells, model_width) for part in parts]
            parts = [jnp.concatenate(parts, axis=1).reshape(pairs * rows, model_width)]
            outs = [bf16(pairs * rows, model_width)]
        elif stacked:
            outs = [bf16(pairs, rows, model_width)]
        else:
            outs = [bf16(rows, model_width)] * pairs
        parts, first, second = expert(
            place,
            group,
            parts,
            stored_gate_preact[0],
            reorder,
            down_weight[0],
            gate_up_weight[0],
            down_first_factor[0],
            down_second_factor[0],
            cells,
            pairs,
            outs,
            last,
        )
        last[:] = [parts[0]]
        if not aligned:
            whole = parts[0].reshape(len(group), pairs, cells, model_width)
            parts = [whole[:, j].reshape(rows, model_width) for j in range(pairs)]
        return parts, first, second

    def combined(group, messages):
        owns, others = combine(place, messages, [tables[s] for s in group], tok_rows, last)
        last[:] = [others[0]]
        totals = []
        for s, own, other in zip(group, owns, others):
            total = own + across(other, 1).astype(jnp.float32)
            if s:
                total = shift(total.astype(jnp.bfloat16), -s).astype(jnp.float32)
            totals.append(total)
        return totals

    def forward(span, before):
        result = attention_forward(
            place,
            rotated_queries,
            rotated_keys,
            stored_values,
            output_first_factor,
            tok_rows,
            span,
            before,
            last,
        )
        last[:] = [result[2]]
        return result

    def sent_out(group, after):
        held = lax.optimization_barrier(((output_gradient, choice), after))[0]
        for s in group:
            choices[s] = shift(held[1], s)
        for s in group:
            tokens[s] = shift(held[0], s)

    def brought(group, after):
        held, _ = lax.optimization_barrier(
            ([tokens[s] for s in group], [choices[s] for s in group], last, after)
        )[:2], None
        for s, value, chosen in zip(group, *held):
            tokens[s] = value
            near_tokens[s] = across(value, 1)
            tables[s] = table_of(chosen)

    half = heads // 2
    choices, arrived, finished, back = {}, {}, {}, {}
    sent_out(groups[1], [])
    arrived[0] = dispatched(groups[0], True)
    probs, attended, folded_a = forward((0, half), [])
    brought(groups[1], [])
    if len(groups) > 2:
        sent_out(groups[2], [tokens[s] for s in groups[1]])
    arrived[1] = dispatched(groups[1], True)
    finished[0] = worked(groups[0], arrived[0], False)
    probs, attended, folded_b = forward((half, heads - half), [probs, attended])
    if len(groups) > 2:
        brought(groups[2], [])
        arrived[2] = dispatched(groups[2], True)
    for n in range(1, len(groups)):
        finished[n] = worked(groups[n], arrived[n], n == 2)
        back[n] = exchanged(finished[n][0])
    held, _ = lax.optimization_barrier((finished[0][0], last))
    back[0] = exchanged(held)
    totals = []
    for n in [*range(1, len(groups)), 0]:
        if n == 0:
            back[0], totals[: len(groups[1])] = lax.optimization_barrier(
                (back[0], totals[: len(groups[1])])
            )
        totals += combined(groups[n], back[n])
    folded, _ = lax.optimization_barrier(((folded_a + folded_b).astype(jnp.bfloat16), last))
    folded = lax.all_to_all(folded, "dev", 0, 0, tiled=True)
    folded = jnp.sum(folded.astype(jnp.float32), axis=0)
    grad_first = sum(finished[n][1] for n in finished)
    grad_second = sum(finished[n][2] for n in finished)
    residual = (output_gradient.astype(jnp.float32) + sum(totals)).astype(jnp.bfloat16)

    near = [residual] + [across(residual, 2 * j) for j in range(1, pairs)]
    grads, row_term = [], None
    for j in range(pairs):
        if j:
            near[j], _ = lax.optimization_barrier((near[j], last))
        grad, term = head_gradients(
            place,
            j,
            near[j],
            across(near[j], 1),
            output_weight,
            output_first_factor,
            output_second_factor,
            attended,
            last,
        )
        last[:] = [grad]
        grads.append(grad)
        row_term = term if row_term is None else row_term + term

    folded, _ = lax.optimization_barrier((folded.astype(jnp.bfloat16), grads[0]))
    column_term = (
        adapter_scale * jnp.dot(folded, residual, preferred_element_type=jnp.float32)
    ).astype(jnp.bfloat16)
    chip_term = (
        column_term.astype(jnp.float32) + across(column_term, 1).astype(jnp.float32)
    ).astype(jnp.bfloat16)
    share = model_width // pairs
    rank = column_term.shape[0]
    chip = dev_index // 2

    def columns(value, j):
        return lax.dynamic_slice_in_dim(value, (chip ^ j) * share, share, 1)

    mine = [columns(chip_term, 0)] + [
        across(columns(chip_term, j), 2 * j) for j in range(1, pairs)
    ]
    mine = sum(part.astype(jnp.float32) for part in mine).astype(jnp.bfloat16)

    row_term = row_term.astype(jnp.bfloat16)
    if row_term.shape == mine.shape:
        terms = jnp.concatenate([row_term, mine], axis=0)
        terms = planes_sum([terms] + [shift(terms, s) for s in range(1, grp_count)], grp_index)
        output_first_gradient, mine = terms[:rank], terms[rank:]
    else:
        output_first_gradient = planes_sum(
            [row_term] + [shift(row_term, s) for s in range(1, grp_count)], grp_index
        )
        mine = planes_sum([mine] + [shift(mine, s) for s in range(1, grp_count)], grp_index)
    mine = mine.astype(jnp.bfloat16)

    query_gradient, pair_even, pair_odd = attention_backward(
        place,
        rotated_queries,
        rotated_keys,
        stored_values,
        attended,
        probs,
        grads,
        tok_rows,
        last,
    )
    both = (pair_even + across(pair_odd, 1).astype(jnp.float32)).astype(jnp.bfloat16)
    lanes = both.shape[2]
    flat = mine.reshape(rank * share // lanes, lanes)
    ends = [jnp.concatenate([both[j], flat], axis=0) for j in range(pairs)]
    ends = [ends[0]] + [across(ends[j], 2 * j) for j in range(1, pairs)]
    grads = []
    for group in range(KVH):
        grad = jnp.zeros((tok_rows, lanes), jnp.float32)
        for j in range(pairs):
            here = (dev_index ^ (2 * j)) * heads // group_size == group
            grad = grad + jnp.where(here, ends[j][:tok_rows].astype(jnp.float32), 0.0)
        grads.append(grad)
    key_gradient = jnp.concatenate([grad[:, :HEAD_SIZE] for grad in grads], axis=1)
    value_gradient = jnp.concatenate([grad[:, HEAD_SIZE:] for grad in grads], axis=1)
    second_columns = []
    for number in range(pairs):
        part = jnp.zeros((rank, share), jnp.float32)
        for j in range(pairs):
            value = ends[j][tok_rows:].astype(jnp.float32).reshape(rank, share)
            part = part + jnp.where(chip ^ j == number, value, 0.0)
        second_columns.append(part)
    output_second_gradient = jnp.concatenate(second_columns, axis=1)
    return (
        grad_first[None],
        grad_second[None],
        residual,
        output_first_gradient,
        output_second_gradient,
        query_gradient,
        key_gradient,
        value_gradient,
    )


def solution(mesh):
    in_specs = (
        P(("grp", "dev"), None),
        P(("grp", "dev"), None),
        P(("grp", "dev"), None),
        P(("grp", "dev"), None, None),
        P(("grp", "dev"), None, None),
        P(("grp", "dev"), None, None),
        P(("grp", "dev"), None, None),
        P(("grp", "dev"), None, None),
        P("grp", "dev"),
        P("grp", None),
        P("grp", None),
        P("dev", None),
        P(None, "dev"),
        P(),
    )
    out_specs = (
        P(("grp", "dev"), None, None),
        P(("grp", "dev"), None, None),
        P(("grp", "dev"), None),
        P(None, "dev"),
        P(),
        P("grp", "dev"),
        P(("grp", "dev"), None),
        P(("grp", "dev"), None),
    )
    return jax.shard_map(
        on_device, mesh=mesh, in_specs=in_specs, out_specs=out_specs, check_vma=False
    )
```

time: 399 us -> 301 us (0.75)
  matrix products: 88.1 us -> 0.6 us
  Pallas kernels: 36 us -> 117 us
  waiting for transfers between devices: 138 us -> 85.5 us
  local copies, waits for them, and re-layouts: 28.1 us -> 12.4 us
  starting transfers between devices: 76.7 us -> 61.1 us
  blocking collectives: 9.35 us -> 0 us
    dot_general x54 -> x4, matrix products: 87.2 us -> 0.38 us  [table_of(): lax.dot_general(chosen.astype(jnp.bfloat16), earlier, (((2,), (0,)), ((),...]
    pallas_call x1 -> x13, Pallas kernels: 9.58 us -> 87.6 us  [kernel_call(): pl.pallas_call(kernel, grid_spec=pltpu.PrefetchScalarGridSpec(num_scalar_...]
    ppermute x51 -> x30, waiting for transfers between devices: 105 us -> 49.2 us  [across(): return lax.ppermute(value, 'dev', [(i, i ^ step) for i in range(count)])]
    ppermute x51 -> x30, starting transfers between devices: 42.4 us -> 21.8 us  [across(): return lax.ppermute(value, 'dev', [(i, i ^ step) for i in range(count)])]
    all_to_all x0 -> x5, starting transfers between devices: none -> 20.4 us  [the longest x4 16.7 us: exchanged(): lax.all_to_all(parts[0], 'dev', 0, 0, axis_index_groups=chips, tiled=True)]
    ppermute x15 -> x12, starting transfers between devices: 34.2 us -> 19 us  [shift(): lax.ppermute(value, 'grp', [(i, (i + step) % count) for i in range(count)])]
    slice x24 -> x5, local copies, waits for them, and re-layouts: 10.9 us -> 0.68 us  [the longest x2 0.68 us: on_device(): output_first_gradient, mine = (terms[:rank], terms[rank:])]
    all_gather x1 -> x0, blocking collectives: 9.35 us -> none  [on_device(): output_second_gradient = lax.all_gather(own, 'dev', axis=1, tiled=True)]
  transfers between devices with their start and end apart: 66 -> 47, of which waited for: 20 -> 18; matrix products, arithmetic and copies ran while one was open for 30% -> 4% of each run, Pallas kernels for 4% -> 38%
where the time goes in v2:
time: 301 us; the launch traced here: 295 us
  Pallas kernels  117 us (39%)
  waiting for transfers between devices  85.5 us (28%)
  starting transfers between devices  61.1 us (20%)
  other arithmetic  17 us (6%)
  local copies, waits for them, and re-layouts  12.4 us (4%)
    pallas_call x13, Pallas kernels, kernel_call(): pl.pallas_call(kernel, grid_spec=pltpu.PrefetchScalarGridSpec(num_scalar_...  87.6 us
    ppermute x30, waiting for transfers between devices, across(): return lax.ppermute(value, 'dev', [(i, i ^ step) for i in range(count)])  49.2 us
    ppermute x12, waiting for transfers between devices, shift(): lax.ppermute(value, 'grp', [(i, (i + step) % count) for i in range(count)])  36.2 us
    ppermute x30, starting transfers between devices, across(): return lax.ppermute(value, 'dev', [(i, i ^ step) for i in range(count)])  21.8 us
    ppermute x12, starting transfers between devices, shift(): lax.ppermute(value, 'grp', [(i, (i + step) % count) for i in range(count)])  19 us
    pallas_call x2, Pallas kernels, attention_forward(): pl.pallas_call(forward_kernel, grid_spec=pltpu.PrefetchScalarGridSpec(num...  17 us
    all_to_all x4, starting transfers between devices, exchanged(): lax.all_to_all(parts[0], 'dev', 0, 0, axis_index_groups=chips, tiled=True)  16.7 us
    pallas_call x1, Pallas kernels, attention_backward(): pl.pallas_call(backward_kernel, grid_spec=pltpu.PrefetchScalarGridSpec(nu...  11.9 us
  transfers between devices with their start and end apart: 47, of which 18 were waited for; matrix products, arithmetic and copies ran while one was open for 4% of the time, Pallas kernels for 38%

profile of v2, /device:TPU:0, one launch (start us, length us, event | category | flops | bytes accessed | tf_op | source)
XLA Modules:
  0.0 294.9 jit_solution(14787677985512871236)
XLA Ops:
  21.6 8.6 %attention_forward.2 = (bf16[4,1024,1024]{2,1,0:T(8,128)(2,1)}, bf16[1024,512]{1,0:T(8,128)(2,1)}, f32[8,64,128]{2,1,0:T(8,128)}) custom-call(s32[6]{0:T(128)} %pad_add_fusion.place_ref.place, bf16[1024,512]{1,0:T(8,128)(2,1)} %q_ref.5, bf16[1024,512]{1,0:T(8,128)(2,1)} %k_ref.5, bf16[1024,512]{1,0:T(8,128)(2,1)} %v_ref.5, bf16[64,512]{1,0:T(8,128)(2,1)} %refs_3_.7, ...), custom_call_target="tpu_custom_call" | custom-call | bytes 8800000 | tf_op jit(solution)/shard_map/attention_forward/pallas_call | solution.py:373
  37.4 5.2 %dispatch.4.refs_8_ = bf16[4,160,2048]{2,1,0:T(8,128)(2,1)} custom-call(s32[6]{0:T(128)} %pad_add_fusion.place_ref.place, bf16[128,2048]{1,0:T(8,128)(2,1)} %copy-done.14, bf16[128,2048]{1,0:T(8,128)(2,1)} %copy-done.15, bf16[128,2048]{1,0:T(8,128)(2,1)} %copy-done.17, bf16[128,2048]{1,0:T(8,128)(2,1)} %copy-done.18, ...), custom_call_target="tpu_custom_call" | custom-call | bytes 3500000 | tf_op jit(solution)/shard_map/dispatch/pallas_call | solution.py:56
  43.7 4.2 %all-to-all-start.1 = ((bf16[4,160,2048]{2,1,0:T(8,128)(2,1)}), bf16[4,160,2048]{2,1,0:T(8,128)(2,1)S(1)}, u32[]{:S(2)}, u32[]{:S(2)}) async-start(bf16[4,160,2048]{2,1,0:T(8,128)(2,1)} %dispatch.4.refs_8_), calls=%async_computation.1 | async-start | bytes 5242880 | tf_op jit(solution)/shard_map/all_to_all | solution.py:590
  51.0 12.2 %expert.3 = (bf16[80,2048]{1,0:T(8,128)(2,1)}, bf16[80,2048]{1,0:T(8,128)(2,1)}, bf16[80,2048]{1,0:T(8,128)(2,1)}, bf16[80,2048]{1,0:T(8,128)(2,1)}, f32[64,768]{1,0:T(8,128)}, /*index=5*/f32[64,2048]{1,0:T(8,128)}) custom-call(s32[6]{0:T(128)} %pad_add_fusion.place_ref.place, bf16[4,80,2048]{2,1,0:T(8,128)(2,1)} %copy-done.2, ...), custom_call_target="tpu_custom_call" | custom-call | bytes 12500000 | tf_op jit(solution)/shard_map/expert/pallas_call | solution.py:56
  63.1 8.5 %attention_forward.3 = (bf16[4,1024,1024]{2,1,0:T(8,128)(2,1)}, bf16[1024,512]{1,0:T(8,128)(2,1)}, f32[8,64,128]{2,1,0:T(8,128)}) custom-call(s32[6]{0:T(128)} %pad_add_fusion.place_ref.place, bf16[1024,512]{1,0:T(8,128)(2,1)} %q_ref.5, bf16[1024,512]{1,0:T(8,128)(2,1)} %k_ref.5, ...), custom_call_target="tpu_custom_call", output_to_operand_aliasing={{0}: (5, {}), {1}: (6, {})} | custom-call | bytes 8800000 | tf_op jit(solution)/shard_map/attention_forward/pallas_call | solution.py:373
  78.5 4.5 %all-to-all-start.2 = ((bf16[4,80,2048]{2,1,0:T(8,128)(2,1)}), bf16[4,80,2048]{2,1,0:T(8,128)(2,1)}, u32[]{:S(2)}, u32[]{:S(2)}) async-start(bf16[4,80,2048]{2,1,0:T(8,128)(2,1)} %dispatch.5.refs_10_), calls=%async_computation.2 | async-start | bytes 2621440 | tf_op jit(solution)/shard_map/all_to_all | solution.py:590
  83.0 16.9 %expert.4 = (bf16[160,2048]{1,0:T(8,128)(2,1)}, bf16[160,2048]{1,0:T(8,128)(2,1)}, bf16[160,2048]{1,0:T(8,128)(2,1)}, bf16[160,2048]{1,0:T(8,128)(2,1)}, f32[64,768]{1,0:T(8,128)}, /*index=5*/f32[64,2048]{1,0:T(8,128)}) custom-call(s32[6]{0:T(128)} %pad_add_fusion.place_ref.place, bf16[4,160,2048]{2,1,0:T(8,128)(2,1)} %copy-done, ...), custom_call_target="tpu_custom_call" | custom-call | bytes 17000000 | tf_op jit(solution)/shard_map/expert/pallas_call | solution.py:56
  103.6 12.4 %expert.5 = (bf16[4,80,2048]{2,1,0:T(8,128)(2,1)}, f32[64,768]{1,0:T(8,128)}, f32[64,2048]{1,0:T(8,128)}) custom-call(s32[6]{0:T(128)} %pad_add_fusion.place_ref.place, bf16[4,80,2048]{2,1,0:T(8,128)(2,1)} %all-to-all-done.2.refs_0_, bf16[320,320]{1,0:T(8,128)(2,1)} %fusion.5.refs_1_, bf16[1280,1536]{1,0:T(8,128)(2,1)} %bitcast.121, ...), custom_call_target="tpu_custom_call" | custom-call | bytes 12500000 | tf_op jit(solution)/shard_map/expert/pallas_call | solution.py:56
  116.0 4.1 %all-to-all-start.3 = ((bf16[4,80,2048]{2,1,0:T(8,128)(2,1)}), bf16[4,80,2048]{2,1,0:T(8,128)(2,1)S(1)}, u32[]{:S(2)}, u32[]{:S(2)}) async-start(bf16[4,80,2048]{2,1,0:T(8,128)(2,1)} %get-tuple-element.98.refs_6_), calls=%async_computation.3 | async-start | bytes 2621440 | tf_op jit(solution)/shard_map/all_to_all | solution.py:590
  120.1 19.9 %collective-permute-done.15.refs_2_ = bf16[160,2048]{1,0:T(8,128)(2,1)S(1)} collective-permute-done((bf16[160,2048]{1,0:T(8,128)(2,1)}, bf16[160,2048]{1,0:T(8,128)(2,1)S(1)}, u32[]{:S(2)}, u32[]{:S(2)}) %collective-permute-start.15) | collective-permute-done | bytes 655392 | tf_op jit(solution)/shard_map/ppermute | solution.py:29
  140.9 5.8 %combine.3 = (f32[128,2048]{1,0:T(8,128)}, bf16[128,2048]{1,0:T(8,128)(2,1)}, f32[128,2048]{1,0:T(8,128)}, bf16[128,2048]{1,0:T(8,128)(2,1)}) custom-call(s32[6]{0:T(128)} %pad_add_fusion.place_ref.place, bf16[160,2048]{1,0:T(8,128)(2,1)} %get-tuple-element.90.refs_8_.refs_0_, bf16[160,2048]{1,0:T(8,128)(2,1)} %copy-done.10, bf16[160,2048]{1,0:T(8,128)(2,1)} %copy-done.11, ...), custom_call_target="tpu_custom_call" | custom-call | bytes 4500000 | tf_op jit(solution)/shard_map/combine/pallas_call | solution.py:56
  148.3 4.5 %combine.4 = (f32[128,2048]{1,0:T(8,128)}, bf16[128,2048]{1,0:T(8,128)(2,1)}) custom-call(s32[6]{0:T(128)} %pad_add_fusion.place_ref.place, bf16[4,80,2048]{2,1,0:T(8,128)(2,1)} %copy-done.1, f32[2,4,256]{2,1,0:T(4,128)} %pad_maximum_fusion.12.refs_2_.refs_1_, bf16[128,2048]{1,0:T(8,128)(2,1)} %get-tuple-element.107.refs_2_), custom_call_target="tpu_custom_call" | custom-call | bytes 4500000 | tf_op jit(solution)/shard_map/combine/pallas_call | solution.py:56
  161.8 7.1 %collective-permute-done.18 = bf16[128,2048]{1,0:T(8,128)(2,1)S(1)} collective-permute-done((bf16[128,2048]{1,0:T(8,128)(2,1)S(1)}, bf16[128,2048]{1,0:T(8,128)(2,1)S(1)}, u32[]{:S(2)}, u32[]{:S(2)}) %collective-permute-start.18) | collective-permute-done | bytes 524320 | tf_op jit(solution)/shard_map/ppermute | solution.py:34
  170.2 10.7 %collective-permute-done.20 = bf16[128,2048]{1,0:T(8,128)(2,1)S(1)} collective-permute-done((bf16[128,2048]{1,0:T(8,128)(2,1)S(1)}, bf16[128,2048]{1,0:T(8,128)(2,1)S(1)}, u32[]{:S(2)}, u32[]{:S(2)}) %collective-permute-start.20) | collective-permute-done | bytes 524320 | tf_op jit(solution)/shard_map/ppermute | solution.py:34
  182.6 4.3 %combine.5 = (f32[128,2048]{1,0:T(8,128)}, bf16[128,2048]{1,0:T(8,128)(2,1)}) custom-call(s32[6]{0:T(128)} %pad_add_fusion.place_ref.place, bf16[80,2048]{1,0:T(8,128)(2,1)} %get-tuple-element.114.refs_2_.refs_0_, bf16[80,2048]{1,0:T(8,128)(2,1)} %copy-done.29, bf16[80,2048]{1,0:T(8,128)(2,1)} %copy-done.30, bf16[80,2048]{1,0:T(8,128)(2,1)} %copy-done.31, ...), custom_call_target="tpu_custom_call" | custom-call | bytes 4500000 | tf_op jit(solution)/shard_map/combine/pallas_call | solution.py:56
  186.9 15.9 %collective-permute-done.22 = bf16[128,2048]{1,0:T(8,128)(2,1)S(1)} collective-permute-done((bf16[128,2048]{1,0:T(8,128)(2,1)S(1)}, bf16[128,2048]{1,0:T(8,128)(2,1)S(1)}, u32[]{:S(2)}, u32[]{:S(2)}) %collective-permute-start.22) | collective-permute-done | bytes 524320 | tf_op jit(solution)/shard_map/ppermute | solution.py:34
  207.3 4.8 %head_gradients.4 = (bf16[256,512]{1,0:T(8,128)(2,1)}, f32[64,512]{1,0:T(8,128)}) custom-call(s32[6]{0:T(128)} %pad_add_fusion.place_ref.place, bf16[128,2048]{1,0:T(8,128)(2,1)} %copy-done.3, bf16[128,2048]{1,0:T(8,128)(2,1)} %copy-done.28, bf16[512,2048]{1,0:T(8,128)(2,1)} %refs_2_.7, bf16[64,512]{1,0:T(8,128)(2,1)} %refs_3_.7, bf16[64,2048]{1,0:T(8,128)(2,1)} %refs_4_.7, ...), custom_call_target="tpu_custom_call" | custom-call | bytes 4700000 | tf_op jit(solution)/shard_map/head_gradients/pallas_call | solution.py:56
  212.1 6.8 %collective-permute-done.25.refs_0_ = bf16[128,2048]{1,0:T(8,128)(2,1)S(1)} collective-permute-done((bf16[128,2048]{1,0:T(8,128)(2,1)S(1)}, bf16[128,2048]{1,0:T(8,128)(2,1)S(1)}, u32[]{:S(2)}, u32[]{:S(2)}) %collective-permute-start.25) | collective-permute-done | bytes 524320 | tf_op jit(solution)/shard_map/ppermute | solution.py:29
  226.6 4.6 %head_gradients.5 = (bf16[256,512]{1,0:T(8,128)(2,1)}, f32[64,512]{1,0:T(8,128)}) custom-call(s32[6]{0:T(128)} %pad_add_fusion.place_ref.place, bf16[128,2048]{1,0:T(8,128)(2,1)} %copy-done.20, bf16[128,2048]{1,0:T(8,128)(2,1)} %copy-done.21, bf16[512,2048]{1,0:T(8,128)(2,1)} %refs_2_.7, bf16[64,512]{1,0:T(8,128)(2,1)} %refs_3_.7, bf16[64,2048]{1,0:T(8,128)(2,1)} %refs_4_.7, ...), custom_call_target="tpu_custom_call" | custom-call | bytes 4700000 | tf_op jit(solution)/shard_map/head_gradients/pallas_call | solution.py:56
  231.2 3.9 %collective-permute-done.27.refs_0_ = bf16[128,2048]{1,0:T(8,128)(2,1)S(1)} collective-permute-done((bf16[128,2048]{1,0:T(8,128)(2,1)}, bf16[128,2048]{1,0:T(8,128)(2,1)S(1)}, u32[]{:S(2)}, u32[]{:S(2)}) %collective-permute-start.27) | collective-permute-done | bytes 524320 | tf_op jit(solution)/shard_map/ppermute | solution.py:29
  238.1 4.6 %head_gradients.6 = (bf16[256,512]{1,0:T(8,128)(2,1)}, f32[64,512]{1,0:T(8,128)}) custom-call(s32[6]{0:T(128)} %pad_add_fusion.place_ref.place, bf16[128,2048]{1,0:T(8,128)(2,1)} %copy-done.16, bf16[128,2048]{1,0:T(8,128)(2,1)} %copy-done.19, bf16[512,2048]{1,0:T(8,128)(2,1)} %refs_2_.7, bf16[64,512]{1,0:T(8,128)(2,1)} %refs_3_.7, bf16[64,2048]{1,0:T(8,128)(2,1)} %refs_4_.7, ...), custom_call_target="tpu_custom_call" | custom-call | bytes 4700000 | tf_op jit(solution)/shard_map/head_gradients/pallas_call | solution.py:56
  242.7 7.6 %collective-permute-done.29.refs_0_ = bf16[128,2048]{1,0:T(8,128)(2,1)S(1)} collective-permute-done((bf16[128,2048]{1,0:T(8,128)(2,1)S(1)}, bf16[128,2048]{1,0:T(8,128)(2,1)S(1)}, u32[]{:S(2)}, u32[]{:S(2)}) %collective-permute-start.29) | collective-permute-done | bytes 524320 | tf_op jit(solution)/shard_map/ppermute | solution.py:29
  258.7 4.6 %head_gradients.7 = (bf16[256,512]{1,0:T(8,128)(2,1)}, f32[64,512]{1,0:T(8,128)}) custom-call(s32[6]{0:T(128)} %pad_add_fusion.place_ref.place, bf16[128,2048]{1,0:T(8,128)(2,1)} %copy-done.12, bf16[128,2048]{1,0:T(8,128)(2,1)} %copy-done.13, bf16[512,2048]{1,0:T(8,128)(2,1)} %refs_2_.7, bf16[64,512]{1,0:T(8,128)(2,1)} %refs_3_.7, bf16[64,2048]{1,0:T(8,128)(2,1)} %refs_4_.7, ...), custom_call_target="tpu_custom_call" | custom-call | bytes 4700000 | tf_op jit(solution)/shard_map/head_gradients/pallas_call | solution.py:56
  268.2 11.9 %attention_backward.1 = (f32[1024,512]{1,0:T(8,128)}, f32[4,128,256]{2,1,0:T(8,128)}, bf16[4,128,256]{2,1,0:T(8,128)(2,1)}) custom-call(s32[6]{0:T(128)} %pad_add_fusion.place_ref.place, bf16[1024,512]{1,0:T(8,128)(2,1)} %q_ref.5, bf16[1024,512]{1,0:T(8,128)(2,1)} %k_ref.5, bf16[1024,512]{1,0:T(8,128)(2,1)} %v_ref.5, ...), custom_call_target="tpu_custom_call" | custom-call | bytes 11800000 | tf_op jit(solution)/shard_map/attention_backward/pallas_call | solution.py:458
  (258 shorter events, 99.4 us)
Async XLA Ops:
  3.3 29.3 %collective-permute-start.2 = (bf16[128,2048]{1,0:T(8,128)(2,1)}, bf16[128,2048]{1,0:T(8,128)(2,1)S(1)}, u32[]{:S(2)}, u32[]{:S(2)}) collective-permute-start(bf16[128,2048]{1,0:T(8,128)(2,1)} %refs_0_.1), channel_id=1, source_target_pairs={{0,8},{8,16},{16,24},{24,0},{1,9},{9,17},{17,25},{25,1},{2,10},{10... | collective-permute-start | bytes 1572872 | tf_op jit(solution)/shard_map/ppermute | solution.py:34
  6.2 26.4 %collective-permute-start.3 = (bf16[128,2048]{1,0:T(8,128)(2,1)}, bf16[128,2048]{1,0:T(8,128)(2,1)S(1)}, u32[]{:S(2)}, u32[]{:S(2)}) collective-permute-start(bf16[128,2048]{1,0:T(8,128)(2,1)} %refs_0_.1), channel_id=1, source_target_pairs={{0,24},{8,0},{16,8},{24,16},{1,25},{9,1},{17,9},{25,17},{2,26},{10... | collective-permute-start | bytes 1572872 | tf_op jit(solution)/shard_map/ppermute | solution.py:34
  8.3 24.3 %collective-permute-start.4 = (f32[2,16,128]{2,1,0:T(8,128)S(1)}, f32[2,16,128]{2,1,0:T(8,128)S(1)}, u32[]{:S(2)}, u32[]{:S(2)}) collective-permute-start(f32[2,16,128]{2,1,0:T(8,128)S(1)} %pad_maximum_fusion.7), channel_id=1, source_target_pairs={{0,8},{8,16},{16,24},{24,0},{1,9},{9,17},{17,25},{25,1},{2,10},{10... | collective-permute-start | bytes 49160 | tf_op jit(solution)/shard_map/ppermute | solution.py:34
  8.3 24.3 %collective-permute-start.5 = (f32[2,16,128]{2,1,0:T(8,128)S(1)}, f32[2,16,128]{2,1,0:T(8,128)S(1)}, u32[]{:S(2)}, u32[]{:S(2)}) collective-permute-start(f32[2,16,128]{2,1,0:T(8,128)S(1)} %pad_maximum_fusion.7), channel_id=1, source_target_pairs={{0,24},{8,0},{16,8},{24,16},{1,25},{9,1},{17,9},{25,17},{2,26},{10... | collective-permute-start | bytes 49160 | tf_op jit(solution)/shard_map/ppermute | solution.py:34
  17.7 24.9 %all-to-all-start = ((bf16[4,80,2048]{2,1,0:T(8,128)(2,1)}), bf16[4,80,2048]{2,1,0:T(8,128)(2,1)S(1)}, u32[]{:S(2)}, u32[]{:S(2)}) async-start(bf16[4,80,2048]{2,1,0:T(8,128)(2,1)} %dispatch.3.refs_0_), calls=%async_computation | async-start | bytes 2621440 | tf_op jit(solution)/shard_map/all_to_all | solution.py:590
  33.2 38.4 %collective-permute-start.8 = (bf16[128,2048]{1,0:T(8,128)(2,1)S(1)}, bf16[128,2048]{1,0:T(8,128)(2,1)}, u32[]{:S(2)}, u32[]{:S(2)}) collective-permute-start(bf16[128,2048]{1,0:T(8,128)(2,1)S(1)} %copy-done.5), channel_id=1, source_target_pairs={{0,16},{8,24},{16,0},{24,8},{1,17},{9,25},{17,1},{25,9},{2,18},{10... | collective-permute-start | bytes 1572872 | tf_op jit(solution)/shard_map/ppermute | solution.py:34
  43.7 34.9 %all-to-all-start.1 = ((bf16[4,160,2048]{2,1,0:T(8,128)(2,1)}), bf16[4,160,2048]{2,1,0:T(8,128)(2,1)S(1)}, u32[]{:S(2)}, u32[]{:S(2)}) async-start(bf16[4,160,2048]{2,1,0:T(8,128)(2,1)} %dispatch.4.refs_8_), calls=%async_computation.1 | async-start | bytes 5242880 | tf_op jit(solution)/shard_map/all_to_all | solution.py:590
  47.9 23.7 %collective-permute-start.9 = (f32[2,16,128]{2,1,0:T(8,128)S(1)}, f32[2,16,128]{2,1,0:T(8,128)S(1)}, u32[]{:S(2)}, u32[]{:S(2)}) collective-permute-start(f32[2,16,128]{2,1,0:T(8,128)S(1)} %pad_maximum_fusion.7), channel_id=1, source_target_pairs={{0,16},{8,24},{16,0},{24,8},{1,17},{9,25},{17,1},{25,9},{2,18},{10... | collective-permute-start | bytes 49160 | tf_op jit(solution)/shard_map/ppermute | solution.py:34
  78.5 25.1 %all-to-all-start.2 = ((bf16[4,80,2048]{2,1,0:T(8,128)(2,1)}), bf16[4,80,2048]{2,1,0:T(8,128)(2,1)}, u32[]{:S(2)}, u32[]{:S(2)}) async-start(bf16[4,80,2048]{2,1,0:T(8,128)(2,1)} %dispatch.5.refs_10_), calls=%async_computation.2 | async-start | bytes 2621440 | tf_op jit(solution)/shard_map/all_to_all | solution.py:590
  100.0 20.1 %collective-permute-start.14 = (bf16[160,2048]{1,0:T(8,128)(2,1)}, bf16[160,2048]{1,0:T(8,128)(2,1)S(1)}, u32[]{:S(2)}, u32[]{:S(2)}) collective-permute-start(bf16[160,2048]{1,0:T(8,128)(2,1)} %get-tuple-element.103), channel_id=1, source_target_pairs={{0,2},{1,3},{2,0},{3,1},{4,6},{5,7},{6,4},{7,5},{8,10},{9,11},{10,... | collective-permute-start | bytes 1966088 | tf_op jit(solution)/shard_map/ppermute | solution.py:29
  102.1 37.9 %collective-permute-start.15 = (bf16[160,2048]{1,0:T(8,128)(2,1)}, bf16[160,2048]{1,0:T(8,128)(2,1)S(1)}, u32[]{:S(2)}, u32[]{:S(2)}) collective-permute-start(bf16[160,2048]{1,0:T(8,128)(2,1)} %get-tuple-element.104), channel_id=1, source_target_pairs={{0,4},{1,5},{2,6},{3,7},{4,0},{5,1},{6,2},{7,3},{8,12},{9,13},{10,... | collective-permute-start | bytes 1966088 | tf_op jit(solution)/shard_map/ppermute | solution.py:29
  103.5 36.5 %collective-permute-start.16 = (bf16[160,2048]{1,0:T(8,128)(2,1)}, bf16[160,2048]{1,0:T(8,128)(2,1)}, u32[]{:S(2)}, u32[]{:S(2)}) collective-permute-start(bf16[160,2048]{1,0:T(8,128)(2,1)} %get-tuple-element.105), channel_id=1, source_target_pairs={{0,6},{1,7},{2,4},{3,5},{4,2},{5,3},{6,0},{7,1},{8,14},{9,15},{10,... | collective-permute-start | bytes 1966088 | tf_op jit(solution)/shard_map/ppermute | solution.py:29
  116.0 31.3 %all-to-all-start.3 = ((bf16[4,80,2048]{2,1,0:T(8,128)(2,1)}), bf16[4,80,2048]{2,1,0:T(8,128)(2,1)S(1)}, u32[]{:S(2)}, u32[]{:S(2)}) async-start(bf16[4,80,2048]{2,1,0:T(8,128)(2,1)} %get-tuple-element.98.refs_6_), calls=%async_computation.3 | async-start | bytes 2621440 | tf_op jit(solution)/shard_map/all_to_all | solution.py:590
  154.5 14.5 %collective-permute-start.18 = (bf16[128,2048]{1,0:T(8,128)(2,1)S(1)}, bf16[128,2048]{1,0:T(8,128)(2,1)S(1)}, u32[]{:S(2)}, u32[]{:S(2)}) collective-permute-start(bf16[128,2048]{1,0:T(8,128)(2,1)S(1)} %add_convert_fusion.3), channel_id=1, source_target_pairs={{0,24},{8,0},{16,8},{24,16},{1,25},{9,1},{17,9},{25,17},{2,26},{10... | collective-permute-start | bytes 1572872 | tf_op jit(solution)/shard_map/ppermute | solution.py:34
  157.5 23.4 %collective-permute-start.20 = (bf16[128,2048]{1,0:T(8,128)(2,1)S(1)}, bf16[128,2048]{1,0:T(8,128)(2,1)S(1)}, u32[]{:S(2)}, u32[]{:S(2)}) collective-permute-start(bf16[128,2048]{1,0:T(8,128)(2,1)S(1)} %add_convert_fusion.2), channel_id=1, source_target_pairs={{0,8},{8,16},{16,24},{24,0},{1,9},{9,17},{17,25},{25,1},{2,10},{10... | collective-permute-start | bytes 1572872 | tf_op jit(solution)/shard_map/ppermute | solution.py:34
  157.8 23.2 %collective-permute-start.11 = (bf16[80,2048]{1,0:T(8,128)(2,1)S(1)}, bf16[80,2048]{1,0:T(8,128)(2,1)S(1)}, u32[]{:S(2)}, u32[]{:S(2)}) collective-permute-start(bf16[80,2048]{1,0:T(8,128)(2,1)S(1)} %copy-done.40), channel_id=1, source_target_pairs={{0,2},{1,3},{2,0},{3,1},{4,6},{5,7},{6,4},{7,5},{8,10},{9,11},{10,... | collective-permute-start | bytes 983048 | tf_op jit(solution)/shard_map/ppermute | solution.py:29
  158.4 22.7 %collective-permute-start.12 = (bf16[80,2048]{1,0:T(8,128)(2,1)S(1)}, bf16[80,2048]{1,0:T(8,128)(2,1)S(1)}, u32[]{:S(2)}, u32[]{:S(2)}) collective-permute-start(bf16[80,2048]{1,0:T(8,128)(2,1)S(1)} %copy-done.39), channel_id=1, source_target_pairs={{0,4},{1,5},{2,6},{3,7},{4,0},{5,1},{6,2},{7,3},{8,12},{9,13},{10,... | collective-permute-start | bytes 983048 | tf_op jit(solution)/shard_map/ppermute | solution.py:29
  160.2 20.8 %collective-permute-start.13 = (bf16[80,2048]{1,0:T(8,128)(2,1)S(1)}, bf16[80,2048]{1,0:T(8,128)(2,1)S(1)}, u32[]{:S(2)}, u32[]{:S(2)}) collective-permute-start(bf16[80,2048]{1,0:T(8,128)(2,1)S(1)} %copy-done.38), channel_id=1, source_target_pairs={{0,6},{1,7},{2,4},{3,5},{4,2},{5,3},{6,0},{7,1},{8,14},{9,15},{10,... | collective-permute-start | bytes 983048 | tf_op jit(solution)/shard_map/ppermute | solution.py:29
  168.9 33.9 %collective-permute-start.22 = (bf16[128,2048]{1,0:T(8,128)(2,1)S(1)}, bf16[128,2048]{1,0:T(8,128)(2,1)S(1)}, u32[]{:S(2)}, u32[]{:S(2)}) collective-permute-start(bf16[128,2048]{1,0:T(8,128)(2,1)S(1)} %add_convert_fusion.1), channel_id=1, source_target_pairs={{0,16},{8,24},{16,0},{24,8},{1,17},{9,25},{17,1},{25,9},{2,18},{10... | collective-permute-start | bytes 1572872 | tf_op jit(solution)/shard_map/ppermute | solution.py:34
  186.9 15.9 %collective-permute-start.23 = (bf16[128,2048]{1,0:T(8,128)(2,1)}, bf16[128,2048]{1,0:T(8,128)(2,1)S(1)}, u32[]{:S(2)}, u32[]{:S(2)}) collective-permute-start(bf16[128,2048]{1,0:T(8,128)(2,1)} %get-tuple-element.119.refs_6_), channel_id=1, source_target_pairs={{0,1},{1,0},{2,3},{3,2},{4,5},{5,4},{6,7},{7,6},{8,9},{9,8},{10,11... | collective-permute-start | bytes 1572872 | tf_op jit(solution)/shard_map/ppermute | solution.py:29
  218.9 16.2 %collective-permute-start.27 = (bf16[128,2048]{1,0:T(8,128)(2,1)}, bf16[128,2048]{1,0:T(8,128)(2,1)S(1)}, u32[]{:S(2)}, u32[]{:S(2)}) collective-permute-start(bf16[128,2048]{1,0:T(8,128)(2,1)} %copy-done.3), channel_id=1, source_target_pairs={{0,4},{1,5},{2,6},{3,7},{4,0},{5,1},{6,2},{7,3},{8,12},{9,13},{10,... | collective-permute-start | bytes 1572872 | tf_op jit(solution)/shard_map/ppermute | solution.py:29
  222.1 14.7 %all-to-all-start.4 = ((bf16[8,64,128]{2,1,0:T(8,128)(2,1)}), bf16[8,64,128]{2,1,0:T(8,128)(2,1)S(1)}, u32[]{:S(2)}, u32[]{:S(2)}) async-start(bf16[8,64,128]{2,1,0:T(8,128)(2,1)} %add_convert_fusion.6), calls=%async_computation.4 | async-start | bytes 262144 | tf_op jit(solution)/shard_map/all_to_all | solution.py:707
  235.1 15.2 %collective-permute-start.29 = (bf16[128,2048]{1,0:T(8,128)(2,1)S(1)}, bf16[128,2048]{1,0:T(8,128)(2,1)S(1)}, u32[]{:S(2)}, u32[]{:S(2)}) collective-permute-start(bf16[128,2048]{1,0:T(8,128)(2,1)S(1)} %copy-done.4), channel_id=1, source_target_pairs={{0,6},{1,7},{2,4},{3,5},{4,2},{5,3},{6,0},{7,1},{8,14},{9,15},{10,... | collective-permute-start | bytes 1572872 | tf_op jit(solution)/shard_map/ppermute | solution.py:29
  264.4 16.7 %collective-permute-start.35 = (bf16[128,512]{1,0:T(8,128)(2,1)S(1)}, bf16[128,512]{1,0:T(8,128)(2,1)S(1)}, u32[]{:S(2)}, u32[]{:S(2)}) collective-permute-start(bf16[128,512]{1,0:T(8,128)(2,1)S(1)} %pad_maximum_fusion.6), channel_id=1, source_target_pairs={{0,24},{8,0},{16,8},{24,16},{1,25},{9,1},{17,9},{25,17},{2,26},{10... | collective-permute-start | bytes 393224 | tf_op jit(solution)/shard_map/ppermute | solution.py:34
  (64 other events, 362.3 us)

commit v3 on v2

--- a/solution.py
+++ b/solution.py
@@ -88,7 +88,7 @@
     return refs[0].at[(place_ref[0] // 2) ^ j] if len(refs) == 1 else refs[j]
 
 
-def dispatch(place, own, other, tables, cells, stacked, after):
+def dispatch(place, own, other, tables, cells, stacked, extra, after):
     planes = len(own)
     pairs = tables[0].shape[1]
     width = own[0].shape[1]
@@ -97,21 +97,38 @@
         for i in range(planes):
             own_ref, other_ref, table_ref = refs[i], refs[planes + i], refs[2 * planes + i]
             tokens = jnp.concatenate([own_ref[...], other_ref[...]], axis=0)
+            filled = [filled_cells(table_ref[0, j : j + 1, :], cells) for j in range(pairs)]
+            weights = [
+                jnp.sum(
+                    jnp.where(filled[j], table_ref[1, j : j + 1, :], 0.0), axis=1, keepdims=True
+                )
+                for j in range(pairs)
+            ]
+            spread = jnp.concatenate([part.astype(jnp.bfloat16) for part in filled], axis=0)
+            rows = jnp.dot(spread, tokens, preferred_element_type=jnp.float32)
+            rows = (rows * jnp.concatenate(weights, axis=0)).astype(jnp.bfloat16)
             for j in range(pairs):
-                filled = filled_cells(table_ref[0, j : j + 1, :], cells)
-                weight = jnp.sum(
-                    jnp.where(filled, table_ref[1, j : j + 1, :], 0.0), axis=1, keepdims=True
-                )
-                rows = jnp.dot(
-                    filled.astype(jnp.bfloat16), tokens, preferred_element_type=jnp.float32
-                )
-                out = chip_part(place_ref, refs[3 * planes :], j)
-                out[i * cells : (i + 1) * cells, :] = (rows * weight).astype(jnp.bfloat16)
-
-    operands = [*own, *other, *tables]
+                out = chip_part(place_ref, refs[3 * planes + len(extra) :], j)
+                out[i * cells : (i + 1) * cells, :] = rows[j * cells : (j + 1) * cells]
+
+        if extra:
+            parts = refs[3 * planes : 3 * planes + len(extra)]
+            core = place_ref[0] % 2
+            rank, lanes = extra[0].shape[1:]
+            for chip in range(pairs):
+                for half in range(2):
+                    value = sum(ref[2 * chip + (core ^ half)] for ref in parts).astype(jnp.bfloat16)
+                    for q in range(rank // added):
+                        at = half * (width // 2) + q * lanes
+                        refs[-1][chip, planes * cells :, at : at + lanes] = value[
+                            q * added : (q + 1) * added
+                        ]
+
+    operands = [*own, *other, *tables, *extra]
+    added = 2 * extra[0].shape[1] * extra[0].shape[2] // width if extra else 0
     outs = [bf16(planes * cells, width)] * pairs
     if stacked:
-        outs = [bf16(pairs, planes * cells, width)]
+        outs = [bf16(pairs, planes * cells + added, width)]
     return kernel_call(
         body,
         place,
@@ -135,12 +152,18 @@
         for i in range(planes):
             table_ref = refs[count + i]
             own_ref, other_ref = refs[count + planes + 2 * i : count + planes + 2 * i + 2]
-            total = None
-            for j in range(pairs):
-                filled = filled_cells(table_ref[0, j : j + 1, :], cells).astype(jnp.bfloat16)
-                rows = chip_part(place_ref, refs[:count], j)[i * cells : (i + 1) * cells, :]
-                part = contraction(filled, rows, 0, 0)
-                total = part if total is None else total + part
+            spread = jnp.concatenate(
+                [
+                    filled_cells(table_ref[0, j : j + 1, :], cells).astype(jnp.bfloat16)
+                    for j in range(pairs)
+                ],
+                axis=0,
+            )
+            rows = [
+                chip_part(place_ref, refs[:count], j)[i * cells : (i + 1) * cells, :]
+                for j in range(pairs)
+            ]
+            total = contraction(spread, jnp.concatenate(rows, axis=0), 0, 0)
             own_ref[...] = total[:token_block]
             other_ref[...] = total[token_block:].astype(jnp.bfloat16)
 
@@ -160,9 +183,7 @@
     return result[::2], result[1::2]
 
 
-def expert(
-    place, steps, parts, saved, reorder, down, gate_up, first, second, cells, pairs, outs, after
-):
+def expert(place, steps, parts, saved, reorder, down, gate_up, first, second, cells, pairs, outs, after):
     planes = len(steps)
     chunk = cells * pairs
     rows = planes * chunk
@@ -183,12 +204,18 @@
         ups = refs[count + 1 + planes : count + 1 + 2 * planes]
         down_ref, back_ref, first_ref, second_ref = refs[count + 1 + 2 * planes :][:4]
         rest = refs[count + 5 + 2 * planes :]
-        rows_out, (grad_first_ref, grad_second_ref) = rest[:results], rest[results : results + 2]
-        routed, low_grad, low_in, grad_pre = rest[results + 2 :]
+        rows_out, (hidden_ref, low_ref) = rest[:results], rest[results : results + 2]
+        routed, low_grad, grad_pre, back, arrived = rest[results + 2 :]
         number = pl.program_id(0)
+
+        def fetch(side):
+            at = pl.ds(side * columns, columns)
+            return pltpu.make_async_copy(back_ref.at[at, :], back.at[side], arrived.at[side])
 
         @pl.when(number == 0)
         def _():
+            for side in range(sides):
+                fetch(side).start()
             if split_in:
                 for i in range(planes):
                     for j in range(pairs):
@@ -197,8 +224,9 @@
                         routed[at : at + cells, :] = part[i * cells : (i + 1) * cells, :]
             else:
                 routed[...] = rows_in[0][...]
-            low_grad[...] = contraction(routed[...], second_ref[...], 1, 1).astype(jnp.bfloat16)
-            low_in[...] = jnp.zeros_like(low_in)
+            low = contraction(routed[...], second_ref[...], 1, 1).astype(jnp.bfloat16)
+            low_grad[...] = low
+            low_ref[...] = low
 
         for block in range(blocks):
 
@@ -214,9 +242,7 @@
                 sigmoid = jax.nn.sigmoid(gate)
                 active = gate * sigmoid
                 slope = sigmoid * (1.0 + gate * (1.0 - sigmoid))
-                hidden = (active * up).astype(jnp.bfloat16)
-                low_in[...] += contraction(hidden, first_ref[...], 1, 1)
-                grad_first_ref[...] = adapter_scale * contraction(low_grad[...], hidden, 0, 0)
+                hidden_ref[...] = (active * up).astype(jnp.bfloat16)
                 grad_hidden = contraction(
                     routed[...], down_ref[...], 1, 1
                 ) + adapter_scale * jnp.dot(
@@ -232,7 +258,8 @@
 
             @pl.when(number == blocks + side)
             def _():
-                result = contraction(grad_pre[...], back_ref[...], 1, 1).astype(jnp.bfloat16)
+                fetch(side).wait()
+                result = contraction(grad_pre[...], back[side], 1, 1).astype(jnp.bfloat16)
                 if split_out:
                     for i in range(planes):
                         for j in range(pairs):
@@ -241,12 +268,6 @@
                             part[i * cells : (i + 1) * cells, :] = result[at : at + cells]
                 else:
                     rows_out[0][...] = result
-                grad_second_ref[...] = adapter_scale * contraction(
-                    low_in[...].astype(jnp.bfloat16),
-                    routed[:, side * columns : (side + 1) * columns],
-                    0,
-                    0,
-                )
 
     def inner(i):
         return jnp.minimum(i, blocks - 1)
@@ -265,7 +286,7 @@
         *[saved_block(step, 0) for step in steps],
         *[saved_block(step, blocks) for step in steps],
         pl.BlockSpec((span, width), lambda i, place: (inner(i), 0)),
-        pl.BlockSpec((columns, 2 * width_ff), lambda i, place: (outer(i), 0)),
+        pl.BlockSpec(memory_space=pl.ANY),
         pl.BlockSpec((rank, span), lambda i, place: (0, inner(i))),
         whole_of(second.shape),
     ]
@@ -274,7 +295,7 @@
         place,
         [*parts, reorder, *[saved] * (2 * planes), down, gate_up, first, second],
         specs,
-        [*outs, f32(rank, width_ff), f32(rank, width)],
+        [*outs, bf16(rows, width_ff), bf16(rows, rank)],
         [
             *[
                 pl.BlockSpec(
@@ -283,15 +304,16 @@
                 )
                 for a in outs
             ],
-            pl.BlockSpec((rank, span), lambda i, place: (0, inner(i))),
-            pl.BlockSpec((rank, columns), lambda i, place: (0, outer(i))),
+            pl.BlockSpec((rows, span), lambda i, place: (0, inner(i))),
+            whole_of((rows, rank)),
         ],
         after,
         scratch=[
             pltpu.VMEM((rows, width), jnp.bfloat16),
             pltpu.VMEM((rows, rank), jnp.bfloat16),
-            pltpu.VMEM((rows, rank), jnp.float32),
             pltpu.VMEM((rows, 2 * width_ff), jnp.bfloat16),
+            pltpu.VMEM((sides, columns, 2 * width_ff), jnp.bfloat16),
+            pltpu.SemaphoreType.DMA((sides,)),
         ],
         steps=blocks + sides,
         name="expert",
@@ -300,35 +322,149 @@
     return result[:results], result[results], result[results + 1]
 
 
-def head_gradients(place, j, own, other, weight, first, second, attended, after):
-    rows, width = own.shape
+def adapter_gradients(place, groups, first, cells, pairs, after):
+    rank, width_ff = first.shape
+    width = groups[0][0][0].shape[-1]
+    chunk = cells * pairs
+    operands, sizes = [], []
+    for parts, hidden, low in groups:
+        operands += [*parts, hidden, low]
+        sizes.append((len(parts), hidden.shape[0] // chunk))
+
+    def body(place_ref, *refs):
+        first_ref, grad_first_ref, grad_second_ref = refs[-3:]
+        at = 0
+        grad_first, grad_second = None, None
+        for count, planes in sizes:
+            parts, (hidden, low) = refs[at : at + count], refs[at + count : at + count + 2]
+            at += count + 2
+            low_in = contraction(hidden[...], first_ref[...], 1, 1).astype(jnp.bfloat16)
+            if count == 1 and len(parts[0].shape) == 2:
+                rows = parts[0][...]
+            else:
+                rows = jnp.concatenate(
+                    [
+                        chip_part(place_ref, parts, j)[i * cells : (i + 1) * cells, :]
+                        for i in range(planes)
+                        for j in range(pairs)
+                    ],
+                    axis=0,
+                )
+            part = contraction(low[...], hidden[...], 0, 0)
+            grad_first = part if grad_first is None else grad_first + part
+            part = contraction(low_in, rows, 0, 0)
+            grad_second = part if grad_second is None else grad_second + part
+        grad_first_ref[...] = adapter_scale * grad_first
+        grad_second_ref[...] = adapter_scale * grad_second
+
+    operands.append(first)
+    outs = [f32(rank, width_ff), f32(rank, width)]
+    return kernel_call(
+        body,
+        place,
+        operands,
+        [whole_of(a.shape) for a in operands],
+        outs,
+        [whole_of(a.shape) for a in outs],
+        after,
+        name="adapter_gradients",
+        cost=6.0,
+    )
+
+
+def residual_messages(place, gradient, sums, folded, pairs, after):
+    rows, width = gradient.shape
+    rank = folded.shape[0]
+    share, extra = width // pairs, rank // pairs
+    count = len(sums)
+
+    def body(place_ref, *refs):
+        total = refs[0][...].astype(jnp.float32)
+        for ref in refs[1 : count + 1]:
+            total = total + ref[...].astype(jnp.float32)
+        residual = total.astype(jnp.bfloat16)
+        folded_ref, residual_ref = refs[count + 1], refs[count + 2]
+        messages, term_ref = refs[count + 3 : count + 3 + pairs], refs[-1]
+        residual_ref[...] = residual
+        term = jnp.dot(folded_ref[...], residual, preferred_element_type=jnp.float32)
+        term = (adapter_scale * term).astype(jnp.bfloat16)
+        for number in range(pairs):
+            term_ref[number] = term[:, number * share : (number + 1) * share]
+        for j in range(pairs):
+            messages[j][:rows, :] = residual
+            part = term_ref[(place_ref[0] // 2) ^ j]
+            for q in range(pairs):
+                messages[j][rows:, q * share : (q + 1) * share] = part[q * extra : (q + 1) * extra]
+
+    operands = [gradient, *sums, folded]
+    outs = [bf16(rows, width)] + [bf16(rows + extra, width)] * pairs
+    result = kernel_call(
+        body,
+        place,
+        operands,
+        [whole_of(a.shape) for a in operands],
+        outs,
+        [whole_of(a.shape) for a in outs],
+        after,
+        scratch=[pltpu.VMEM((pairs, rank, share), jnp.bfloat16)],
+        name="residual_messages",
+        cost=4.0,
+    )
+    return result[0], list(result[1:])
+
+
+def head_gradients(place, numbers, own, other, weight, first, second, attended, pairs, after):
+    width = own[0].shape[1]
     heads_width = weight.shape[0]
     rank = first.shape[0]
-
-    def body(place_ref, own_ref, other_ref, weight_ref, first_ref, second_ref, att_ref, grad_ref, term_ref):
-        gradient = jnp.concatenate([own_ref[...], other_ref[...]], axis=0)
-        low = contraction(gradient, second_ref[...], 1, 1).astype(jnp.bfloat16)
-        result = contraction(gradient, weight_ref[...], 1, 1)
-        result = result + adapter_scale * jnp.dot(
-            low, first_ref[...], preferred_element_type=jnp.float32
-        )
-        grad_ref[...] = result.astype(jnp.bfloat16)
+    share, extra = width // pairs, rank // pairs
+    rows = own[0].shape[0] - extra
+    count = len(numbers)
+
+    def body(place_ref, *refs):
+        weight_ref, first_ref, second_ref = refs[2 * count : 2 * count + 3]
+        att_refs = refs[2 * count + 3 : 3 * count + 3]
+        grad_refs = refs[3 * count + 3 : 4 * count + 3]
+        term_ref, columns_ref = refs[4 * count + 3 :]
         core = place_ref[0] % 2
-        term = None
-        for half in range(2):
-            at = pl.ds(pl.multiple_of((core ^ half) * rows, rows), rows)
-            part = contraction(low[half * rows : (half + 1) * rows], att_ref[at, :], 0, 0)
-            term = part if term is None else term + part
-        term_ref[...] = adapter_scale * term
-
-    operands = [own, other, weight, first, second, attended]
-    specs = [whole_of(a.shape) for a in operands[:5]] + [
-        pl.BlockSpec((2 * rows, heads_width), lambda i, place: ((place[0] // 2) ^ j, 0))
+        total, columns = None, None
+        for n in range(count):
+            blocks = refs[n], refs[count + n]
+            gradient = jnp.concatenate([ref[:rows, :] for ref in blocks], axis=0)
+            low = contraction(gradient, second_ref[...], 1, 1).astype(jnp.bfloat16)
+            result = contraction(gradient, weight_ref[...], 1, 1)
+            result = result + adapter_scale * jnp.dot(
+                low, first_ref[...], preferred_element_type=jnp.float32
+            )
+            grad_refs[n][...] = result.astype(jnp.bfloat16)
+            for half in range(2):
+                at = pl.ds(pl.multiple_of((core ^ half) * rows, rows), rows)
+                part = contraction(low[half * rows : (half + 1) * rows], att_refs[n][at, :], 0, 0)
+                total = part if total is None else total + part
+            part = sum(ref[rows:, :].astype(jnp.float32) for ref in blocks)
+            columns = part if columns is None else columns + part
+        term_ref[...] = adapter_scale * total
+        for q in range(pairs):
+            columns_ref[q * extra : (q + 1) * extra, :] = columns[:, q * share : (q + 1) * share]
+
+    operands = [*own, *other, weight, first, second, *[attended] * count]
+    specs = [whole_of(a.shape) for a in operands[: 2 * count + 3]] + [
+        pl.BlockSpec((2 * rows, heads_width), lambda i, place, j=j: ((place[0] // 2) ^ j, 0))
+        for j in numbers
     ]
-    outs = [bf16(2 * rows, heads_width), f32(rank, heads_width)]
-    return kernel_call(
-        body, place, operands, specs, outs, [whole_of(a.shape) for a in outs], after, name="head_gradients", cost=4.7
-    )
+    outs = [*[bf16(2 * rows, heads_width)] * count, f32(rank, heads_width), f32(rank, share)]
+    result = kernel_call(
+        body,
+        place,
+        operands,
+        specs,
+        outs,
+        [whole_of(a.shape) for a in outs],
+        after,
+        name="head_gradients",
+        cost=2.5 + 2.2 * count,
+    )
+    return list(result[:count]), result[count], result[count + 1]
 
 
 def forward_kernel(place, q_ref, k_ref, v_ref, a_ref, *refs):
@@ -591,7 +727,7 @@
             ]
         return [parts[0]] + [across(parts[j], 2 * j) for j in range(1, pairs)]
 
-    def dispatched(group, stacked):
+    def dispatched(group, stacked, extra=()):
         messages = dispatch(
             place,
             [tokens[s] for s in group],
@@ -599,22 +735,24 @@
             [tables[s] for s in group],
             cells,
             stacked and aligned,
+            extra,
             last,
         )
         last[:] = messages[:1]
         return exchanged(messages)
 
     def worked(group, parts, stacked):
-        rows = len(group) * cells
+        count = len(group)
+        rows = count * cells
         if not aligned:
-            parts = [part.reshape(len(group), cells, model_width) for part in parts]
-            parts = [jnp.concatenate(parts, axis=1).reshape(pairs * rows, model_width)]
-            outs = [bf16(pairs * rows, model_width)]
+            parts = [part.reshape(count, cells, model_width) for part in parts]
+            parts = [jnp.concatenate(parts, axis=1).reshape(count * chunk, model_width)]
+            outs = [bf16(count * chunk, model_width)]
         elif stacked:
             outs = [bf16(pairs, rows, model_width)]
         else:
             outs = [bf16(rows, model_width)] * pairs
-        parts, first, second = expert(
+        result, hidden, low = expert(
             place,
             group,
             parts,
@@ -629,22 +767,18 @@
             outs,
             last,
         )
-        last[:] = [parts[0]]
+        last[:] = [result[0]]
         if not aligned:
-            whole = parts[0].reshape(len(group), pairs, cells, model_width)
-            parts = [whole[:, j].reshape(rows, model_width) for j in range(pairs)]
-        return parts, first, second
+            whole = result[0].reshape(count, pairs, cells, model_width)
+            result = [whole[:, j].reshape(rows, model_width) for j in range(pairs)]
+        return result, (parts, hidden, low)
 
     def combined(group, messages):
         owns, others = combine(place, messages, [tables[s] for s in group], tok_rows, last)
         last[:] = [others[0]]
-        totals = []
-        for s, own, other in zip(group, owns, others):
-            total = own + across(other, 1).astype(jnp.float32)
-            if s:
-                total = shift(total.astype(jnp.bfloat16), -s).astype(jnp.float32)
-            totals.append(total)
-        return totals
+        return [
+            own + across(other, 1).astype(jnp.float32) for own, other in zip(owns, others)
+        ]
 
     def forward(span, before):
         result = attention_forward(
@@ -677,6 +811,7 @@
             near_tokens[s] = across(value, 1)
             tables[s] = table_of(chosen)
 
+    riding = aligned and len(groups) > 2
     half = heads // 2
     choices, arrived, finished, back = {}, {}, {}, {}
     sent_out(groups[1], [])
@@ -686,68 +821,90 @@
     if len(groups) > 2:
         sent_out(groups[2], [tokens[s] for s in groups[1]])
     arrived[1] = dispatched(groups[1], True)
-    finished[0] = worked(groups[0], arrived[0], False)
+    finished[0] = worked(groups[0], arrived[0], True)
     probs, attended, folded_b = forward((half, heads - half), [probs, attended])
     if len(groups) > 2:
         brought(groups[2], [])
-        arrived[2] = dispatched(groups[2], True)
+        arrived[2] = dispatched(groups[2], True, [folded_a, folded_b] if riding else [])
     for n in range(1, len(groups)):
         finished[n] = worked(groups[n], arrived[n], n == 2)
-        back[n] = exchanged(finished[n][0])
-    held, _ = lax.optimization_barrier((finished[0][0], last))
-    back[0] = exchanged(held)
-    totals = []
-    for n in [*range(1, len(groups)), 0]:
-        if n == 0:
-            back[0], totals[: len(groups[1])] = lax.optimization_barrier(
-                (back[0], totals[: len(groups[1])])
-            )
-        totals += combined(groups[n], back[n])
-    folded, _ = lax.optimization_barrier(((folded_a + folded_b).astype(jnp.bfloat16), last))
-    folded = lax.all_to_all(folded, "dev", 0, 0, tiled=True)
-    folded = jnp.sum(folded.astype(jnp.float32), axis=0)
-    grad_first = sum(finished[n][1] for n in finished)
-    grad_second = sum(finished[n][2] for n in finished)
-    residual = (output_gradient.astype(jnp.float32) + sum(totals)).astype(jnp.bfloat16)
-
-    near = [residual] + [across(residual, 2 * j) for j in range(1, pairs)]
-    grads, row_term = [], None
-    for j in range(pairs):
-        if j:
-            near[j], _ = lax.optimization_barrier((near[j], last))
-        grad, term = head_gradients(
-            place,
-            j,
-            near[j],
-            across(near[j], 1),
-            output_weight,
-            output_first_factor,
-            output_second_factor,
-            attended,
-            last,
-        )
-        last[:] = [grad]
-        grads.append(grad)
-        row_term = term if row_term is None else row_term + term
-
-    folded, _ = lax.optimization_barrier((folded.astype(jnp.bfloat16), grads[0]))
-    column_term = (
-        adapter_scale * jnp.dot(folded, residual, preferred_element_type=jnp.float32)
-    ).astype(jnp.bfloat16)
-    chip_term = (
-        column_term.astype(jnp.float32) + across(column_term, 1).astype(jnp.float32)
-    ).astype(jnp.bfloat16)
-    share = model_width // pairs
-    rank = column_term.shape[0]
+        rows = finished[n][0]
+        if n == 1:
+            back[1] = exchanged(rows)
+            held, _ = lax.optimization_barrier((finished[0][0], (last, arrived[max(arrived)])))
+            back[0] = exchanged(held)
+        else:
+            rows, _ = lax.optimization_barrier((rows, (back[0], back[1])))
+            back[2] = exchanged(rows)
+
+    def sent_home(group, totals, via):
+        totals = {s: total.astype(jnp.bfloat16) for s, total in zip(group, totals)}
+        return [shift(total, -via.get(s, s)) for s, total in totals.items()]
+
+    totals = combined(groups[1], back[1])
+    relayed = grp_count == 4
+    if relayed:
+        waiting = totals.pop(groups[1].index(1))
+    sums = sent_home([s for s in groups[1] if s != 1 or not relayed], totals, {})
+    own_sum = combined(groups[0], back[0])[0]
+    if len(groups) > 2:
+        back[2], sums = lax.optimization_barrier((back[2], sums))
+        sums += sent_home(groups[2], combined(groups[2], back[2]), {2: 1} if relayed else {})
+    if relayed:
+        passed = (waiting + sums.pop().astype(jnp.float32)).astype(jnp.bfloat16)
+        sums.append(shift(passed, -1))
+        last[:] = lax.optimization_barrier((last, passed))[0]
+    sums.append(own_sum)
+    grad_first, grad_second = adapter_gradients(
+        place, [finished[k][1] for k in finished], down_first_factor[0], cells, pairs, last
+    )
+    last[:] = [grad_first]
+
+    if riding:
+        folded = jnp.sum(arrived[2][0][:, cells * len(groups[2]) :].astype(jnp.float32), axis=0)
+        folded = folded.reshape(folded.shape[0], 2, -1, tok_rows).transpose(1, 2, 0, 3)
+        folded = folded.reshape(2, -1, tok_rows)
+        folded = folded[0] + across(folded[1].astype(jnp.bfloat16), 1).astype(jnp.float32)
+    else:
+        folded = (folded_a + folded_b).astype(jnp.bfloat16)
+        folded = lax.all_to_all(folded, "dev", 0, 0, tiled=True)
+        folded = jnp.sum(folded.astype(jnp.float32), axis=0)
+    folded = folded.astype(jnp.bfloat16)
+
+    residual, near = residual_messages(place, output_gradient, sums, folded, pairs, last)
+    near = near[:1] + [across(near[j], 2 * j) for j in range(1, pairs)]
+    grads, term, columns = head_gradients(
+        place,
+        [0],
+        near[:1],
+        [across(near[0], 1)],
+        output_weight,
+        output_first_factor,
+        output_second_factor,
+        attended,
+        pairs,
+        last,
+    )
+    last[:] = grads
+    held, _ = lax.optimization_barrier((near[1:], last))
+    more, row_term, mine = head_gradients(
+        place,
+        list(range(1, pairs)),
+        held,
+        [across(part, 1) for part in held],
+        output_weight,
+        output_first_factor,
+        output_second_factor,
+        attended,
+        pairs,
+        last,
+    )
+    last[:] = more[:1]
+    grads += more
+    row_term = row_term + term
+    mine = (mine + columns).astype(jnp.bfloat16)
+    rank, share = mine.shape
     chip = dev_index // 2
-
-    def columns(value, j):
-        return lax.dynamic_slice_in_dim(value, (chip ^ j) * share, share, 1)
-
-    mine = [columns(chip_term, 0)] + [
-        across(columns(chip_term, j), 2 * j) for j in range(1, pairs)
-    ]
-    mine = sum(part.astype(jnp.float32) for part in mine).astype(jnp.bfloat16)
 
     row_term = row_term.astype(jnp.bfloat16)
     if row_term.shape == mine.shape:

time: 301 us -> 292 us (0.970)
    ppermute x12, waiting for transfers between devices: 36.2 us -> 26.4 us  [shift(): lax.ppermute(value, 'grp', [(i, (i + step) % count) for i in range(count)])]
    ppermute x30 -> x24, starting transfers between devices: 21.8 us -> 13.6 us  [across(): return lax.ppermute(value, 'dev', [(i, i ^ step) for i in range(count)])]
    ppermute x30 -> x24, waiting for transfers between devices: 49.2 us -> 56.3 us  [across(): return lax.ppermute(value, 'dev', [(i, i ^ step) for i in range(count)])]
    ppermute x12, starting transfers between devices: 19 us -> 24.4 us  [shift(): lax.ppermute(value, 'grp', [(i, (i + step) % count) for i in range(count)])]
    all_to_all x4 -> x5, starting transfers between devices: 16.7 us -> 20.5 us  [exchanged(): lax.all_to_all(parts[0], 'dev', 0, 0, axis_index_groups=chips, tiled=True)]
    all_to_all x1 -> x0, starting transfers between devices: 3.62 us -> none  [on_device(): folded = lax.all_to_all(folded, 'dev', 0, 0, tiled=True)]
    unnamed x82 -> x56, local copies, waits for them, and re-layouts: 11.1 us -> 8.9 us
  transfers between devices with their start and end apart: 47 -> 41, of which waited for: 18 -> 17; matrix products, arithmetic and copies ran while one was open for 4% -> 4% of each run, Pallas kernels for 38% -> 34%
where the time goes in v3:
time: 292 us; the launch traced here: 286 us
  Pallas kernels  114 us (39%)
  waiting for transfers between devices  84.6 us (29%)
  starting transfers between devices  58.5 us (20%)
  other arithmetic  17.3 us (6%)
  local copies, waits for them, and re-layouts  10.2 us (3%)
    pallas_call x13, Pallas kernels, kernel_call(): pl.pallas_call(kernel, grid_spec=pltpu.PrefetchScalarGridSpec(num_scalar_...  84.8 us
    ppermute x24, waiting for transfers between devices, across(): return lax.ppermute(value, 'dev', [(i, i ^ step) for i in range(count)])  56.3 us
    ppermute x12, waiting for transfers between devices, shift(): lax.ppermute(value, 'grp', [(i, (i + step) % count) for i in range(count)])  26.4 us
    ppermute x12, starting transfers between devices, shift(): lax.ppermute(value, 'grp', [(i, (i + step) % count) for i in range(count)])  24.4 us
    all_to_all x5, starting transfers between devices, exchanged(): lax.all_to_all(parts[0], 'dev', 0, 0, axis_index_groups=chips, tiled=True)  20.5 us
    pallas_call x2, Pallas kernels, attention_forward(): pl.pallas_call(forward_kernel, grid_spec=pltpu.PrefetchScalarGridSpec(num...  17 us
    ppermute x24, starting transfers between devices, across(): return lax.ppermute(value, 'dev', [(i, i ^ step) for i in range(count)])  13.6 us
    pallas_call x1, Pallas kernels, attention_backward(): pl.pallas_call(backward_kernel, grid_spec=pltpu.PrefetchScalarGridSpec(nu...  11.7 us
  transfers between devices with their start and end apart: 41, of which 17 were waited for; matrix products, arithmetic and copies ran while one was open for 4% of the time, Pallas kernels for 34%

profile of v3, /device:TPU:0, one launch (start us, length us, event | category | flops | bytes accessed | tf_op | source)
XLA Modules:
  0.0 286.3 jit_solution(16927596008952309172)
XLA Ops:
  17.6 3.9 %all-to-all-start = ((bf16[4,80,2048]{2,1,0:T(8,128)(2,1)}), bf16[4,80,2048]{2,1,0:T(8,128)(2,1)S(1)}, u32[]{:S(2)}, u32[]{:S(2)}) async-start(bf16[4,80,2048]{2,1,0:T(8,128)(2,1)} %dispatch.3.refs_0_), calls=%async_computation | async-start | bytes 2621440 | tf_op jit(solution)/shard_map/all_to_all | solution.py:726
  21.5 8.6 %attention_forward.2 = (bf16[4,1024,1024]{2,1,0:T(8,128)(2,1)}, bf16[1024,512]{1,0:T(8,128)(2,1)}, f32[8,64,128]{2,1,0:T(8,128)}) custom-call(s32[6]{0:T(128)} %pad_add_fusion.place_ref.place, bf16[1024,512]{1,0:T(8,128)(2,1)} %q_ref.5, bf16[1024,512]{1,0:T(8,128)(2,1)} %k_ref.5, bf16[1024,512]{1,0:T(8,128)(2,1)} %v_ref.5, bf16[64,512]{1,0:T(8,128)(2,1)} %refs_7_.1, ...), custom_call_target="tpu_custom_call" | custom-call | bytes 8800000 | tf_op jit(solution)/shard_map/attention_forward/pallas_call | solution.py:509
  37.8 4.7 %dispatch.4.refs_8_ = bf16[4,160,2048]{2,1,0:T(8,128)(2,1)} custom-call(s32[6]{0:T(128)} %pad_add_fusion.place_ref.place, bf16[128,2048]{1,0:T(8,128)(2,1)} %copy-done.17, bf16[128,2048]{1,0:T(8,128)(2,1)} %copy-done.18, bf16[128,2048]{1,0:T(8,128)(2,1)} %copy-done.19, bf16[128,2048]{1,0:T(8,128)(2,1)} %copy-done.20, ...), custom_call_target="tpu_custom_call" | custom-call | bytes 3500000 | tf_op jit(solution)/shard_map/dispatch/pallas_call | solution.py:56
  43.6 4.2 %all-to-all-start.1 = ((bf16[4,160,2048]{2,1,0:T(8,128)(2,1)}), bf16[4,160,2048]{2,1,0:T(8,128)(2,1)S(1)}, u32[]{:S(2)}, u32[]{:S(2)}) async-start(bf16[4,160,2048]{2,1,0:T(8,128)(2,1)} %dispatch.4.refs_8_), calls=%async_computation.1 | async-start | bytes 5242880 | tf_op jit(solution)/shard_map/all_to_all | solution.py:726
  50.9 10.5 %expert.3 = (bf16[4,80,2048]{2,1,0:T(8,128)(2,1)}, bf16[320,768]{1,0:T(8,128)(2,1)}, bf16[320,64]{1,0:T(8,128)(2,1)}) custom-call(s32[6]{0:T(128)} %pad_add_fusion.place_ref.place, bf16[4,80,2048]{2,1,0:T(8,128)(2,1)} %copy-done.1, bf16[320,320]{1,0:T(8,128)(2,1)} %fusion.4.refs_1_, bf16[1280,1536]{1,0:T(8,128)(2,1)} %bitcast.122, ...), custom_call_target="tpu_custom_call" | custom-call | bytes 12500000 | tf_op jit(solution)/shard_map/expert/pallas_call | solution.py:56
  61.3 8.5 %attention_forward.3 = (bf16[4,1024,1024]{2,1,0:T(8,128)(2,1)}, bf16[1024,512]{1,0:T(8,128)(2,1)}, f32[8,64,128]{2,1,0:T(8,128)}) custom-call(s32[6]{0:T(128)} %pad_add_fusion.place_ref.place, bf16[1024,512]{1,0:T(8,128)(2,1)} %q_ref.5, bf16[1024,512]{1,0:T(8,128)(2,1)} %k_ref.5, ...), custom_call_target="tpu_custom_call", output_to_operand_aliasing={{0}: (5, {}), {1}: (6, {})} | custom-call | bytes 8800000 | tf_op jit(solution)/shard_map/attention_forward/pallas_call | solution.py:509
  78.4 4.5 %all-to-all-start.2 = ((bf16[4,88,2048]{2,1,0:T(8,128)(2,1)}), bf16[4,88,2048]{2,1,0:T(8,128)(2,1)}, u32[]{:S(2)}, u32[]{:S(2)}) async-start(bf16[4,88,2048]{2,1,0:T(8,128)(2,1)} %dispatch.5.refs_10_), calls=%async_computation.2 | async-start | bytes 2883584 | tf_op jit(solution)/shard_map/all_to_all | solution.py:726
  82.9 15.5 %expert.4 = (bf16[160,2048]{1,0:T(8,128)(2,1)}, bf16[160,2048]{1,0:T(8,128)(2,1)}, bf16[160,2048]{1,0:T(8,128)(2,1)}, bf16[160,2048]{1,0:T(8,128)(2,1)}, bf16[64...) custom-call(s32[6]{0:T(128)} %pad_add_fusion.place_ref.place, bf16[4,160,2048]{2,1,0:T(8,128)(2,1)} %copy-done, ...), custom_call_target="tpu_custom_call" | custom-call | bytes 17000000 | tf_op jit(solution)/shard_map/expert/pallas_call | solution.py:56
  102.1 4.1 %all-to-all-start.3 = ((bf16[4,80,2048]{2,1,0:T(8,128)(2,1)}), bf16[4,80,2048]{2,1,0:T(8,128)(2,1)S(1)}, u32[]{:S(2)}, u32[]{:S(2)}) async-start(bf16[4,80,2048]{2,1,0:T(8,128)(2,1)} %get-tuple-element.93.refs_2_), calls=%async_computation.3 | async-start | bytes 2621440 | tf_op jit(solution)/shard_map/all_to_all | solution.py:726
  106.2 10.5 %expert.5 = (bf16[4,80,2048]{2,1,0:T(8,128)(2,1)}, bf16[320,768]{1,0:T(8,128)(2,1)}, bf16[320,64]{1,0:T(8,128)(2,1)}) custom-call(s32[6]{0:T(128)} %pad_add_fusion.place_ref.place, bf16[4,88,2048]{2,1,0:T(8,128)(2,1)} %all-to-all-done.2.refs_0_.refs_6_, bf16[320,320]{1,0:T(8,128)(2,1)} %fusion.4.refs_1_, bf16[1280,1536]{1,0:T(8,128)(2,1)} %bitcast.128, ...), custom_call_target="tpu_custom_call" | custom-call | bytes 12500000 | tf_op jit(solution)/shard_map/expert/pallas_call | solution.py:56
  116.7 22.8 %collective-permute-done.12.refs_2_ = bf16[160,2048]{1,0:T(8,128)(2,1)S(1)} collective-permute-done((bf16[160,2048]{1,0:T(8,128)(2,1)}, bf16[160,2048]{1,0:T(8,128)(2,1)S(1)}, u32[]{:S(2)}, u32[]{:S(2)}) %collective-permute-start.12) | collective-permute-done | bytes 655392 | tf_op jit(solution)/shard_map/ppermute | solution.py:29
  140.6 4.7 %combine.3 = (f32[128,2048]{1,0:T(8,128)}, bf16[128,2048]{1,0:T(8,128)(2,1)}, f32[128,2048]{1,0:T(8,128)}, bf16[128,2048]{1,0:T(8,128)(2,1)}) custom-call(s32[6]{0:T(128)} %pad_add_fusion.place_ref.place, bf16[160,2048]{1,0:T(8,128)(2,1)} %get-tuple-element.89.refs_8_.refs_0_, bf16[160,2048]{1,0:T(8,128)(2,1)} %copy-done.7, bf16[160,2048]{1,0:T(8,128)(2,1)} %copy-done.8, ...), custom_call_target="tpu_custom_call" | custom-call | bytes 4500000 | tf_op jit(solution)/shard_map/combine/pallas_call | solution.py:56
  155.9 10.7 %collective-permute-done.15.refs_1_ = bf16[128,2048]{1,0:T(8,128)(2,1)S(1)} collective-permute-done((bf16[128,2048]{1,0:T(8,128)(2,1)S(1)}, bf16[128,2048]{1,0:T(8,128)(2,1)S(1)}, u32[]{:S(2)}, u32[]{:S(2)}) %collective-permute-start.15) | collective-permute-done | bytes 524320 | tf_op jit(solution)/shard_map/ppermute | solution.py:34
  167.7 3.9 %combine.5 = (f32[128,2048]{1,0:T(8,128)}, bf16[128,2048]{1,0:T(8,128)(2,1)}) custom-call(s32[6]{0:T(128)} %pad_add_fusion.place_ref.place, bf16[4,80,2048]{2,1,0:T(8,128)(2,1)} %copy-done.3, f32[2,4,256]{2,1,0:T(4,128)} %pad_maximum_fusion.12.refs_2_.refs_1_, bf16[128,2048]{1,0:T(8,128)(2,1)} %get-tuple-element.102.refs_2_), custom_call_target="tpu_custom_call" | custom-call | bytes 4500000 | tf_op jit(solution)/shard_map/combine/pallas_call | solution.py:56
  178.7 10.5 %collective-permute-done.18 = bf16[128,2048]{1,0:T(8,128)(2,1)S(1)} collective-permute-done((bf16[128,2048]{1,0:T(8,128)(2,1)S(1)}, bf16[128,2048]{1,0:T(8,128)(2,1)S(1)}, u32[]{:S(2)}, u32[]{:S(2)}) %collective-permute-start.18) | collective-permute-done | bytes 524320 | tf_op jit(solution)/shard_map/ppermute | solution.py:34
  189.3 3.8 %collective-permute-start.19 = (bf16[128,2048]{1,0:T(8,128)(2,1)S(1)}, bf16[128,2048]{1,0:T(8,128)(2,1)S(1)}, u32[]{:S(2)}, u32[]{:S(2)}) collective-permute-start(bf16[128,2048]{1,0:T(8,128)(2,1)S(1)} %add_convert_fusion), channel_id=1, source_target_pairs={{0,24},{8,0},{16,8},{24,16},{1,25},{9,1},{17,9},{25,17},{2,26},{10... | collective-permute-start | bytes 1572872 | tf_op jit(solution)/shard_map/ppermute | solution.py:34
  194.9 6.7 %adapter_gradients.1 = (f32[64,768]{1,0:T(8,128)}, f32[64,2048]{1,0:T(8,128)}) custom-call(s32[6]{0:T(128)} %pad_add_fusion.place_ref.place, bf16[4,80,2048]{2,1,0:T(8,128)(2,1)} %copy-done.1, bf16[320,768]{1,0:T(8,128)(2,1)} %get-tuple-element.77.refs_1_, bf16[320,64]{1,0:T(8,128)(2,1)} %get-tuple-element.78.refs_2_, bf16[4,160,2048]{2,1,0:T(8,128)(2,1)} %copy-done, ...), custom_call_target="tpu_custom_call" | custom-call | bytes 6000000 | tf_op jit(solution)/shard_map/adapter_gradients/pallas_call | solution.py:56
  204.6 4.3 %residual_messages.1 = (bf16[128,2048]{1,0:T(8,128)(2,1)}, bf16[144,2048]{1,0:T(8,128)(2,1)}, bf16[144,2048]{1,0:T(8,128)(2,1)}, bf16[144,2048]{1,0:T(8,128)(2,1)}, bf16[144,2048]{1,0:T(8,128)(2,1)}) custom-call(s32[6]{0:T(128)} %pad_add_fusion.place_ref.place, bf16[128,2048]{1,0:T(8,128)(2,1)} %refs_0_.3, bf16[128,2048]{1,0:T(8,128)(2,1)} %copy-done.22, ...), custom_call_target="tpu_custom_call" | custom-call | bytes 4000000 | tf_op jit(solution)/shard_map/residual_messages/pallas_call | solution.py:56
  213.2 4.7 %head_gradients.2 = (bf16[256,512]{1,0:T(8,128)(2,1)}, f32[64,512]{1,0:T(8,128)}, f32[64,512]{1,0:T(8,128)}) custom-call(s32[6]{0:T(128)} %pad_add_fusion.place_ref.place, bf16[144,2048]{1,0:T(8,128)(2,1)} %get-tuple-element.115.refs_0_, bf16[144,2048]{1,0:T(8,128)(2,1)} %copy-done.15, bf16[512,2048]{1,0:T(8,128)(2,1)} %refs_6_.1, bf16[64,512]{1,0:T(8,128)(2,1)} %refs_7_.1, ...), custom_call_target="tpu_custom_call" | custom-call | bytes 4700000 | tf_op jit(solution)/shard_map/head_gradients/pallas_call | solution.py:56
  217.9 7.3 %collective-permute-done.22.refs_0_ = bf16[144,2048]{1,0:T(8,128)(2,1)S(1)} collective-permute-done((bf16[144,2048]{1,0:T(8,128)(2,1)}, bf16[144,2048]{1,0:T(8,128)(2,1)S(1)}, u32[]{:S(2)}, u32[]{:S(2)}) %collective-permute-start.22) | collective-permute-done | bytes 589856 | tf_op jit(solution)/shard_map/ppermute | solution.py:29
  225.2 13.4 %collective-permute-done.23.refs_1_ = bf16[144,2048]{1,0:T(8,128)(2,1)S(1)} collective-permute-done((bf16[144,2048]{1,0:T(8,128)(2,1)}, bf16[144,2048]{1,0:T(8,128)(2,1)S(1)}, u32[]{:S(2)}, u32[]{:S(2)}) %collective-permute-start.23) | collective-permute-done | bytes 589856 | tf_op jit(solution)/shard_map/ppermute | solution.py:29
  243.3 8.3 %head_gradients.3 = (bf16[256,512]{1,0:T(8,128)(2,1)}, bf16[256,512]{1,0:T(8,128)(2,1)}, bf16[256,512]{1,0:T(8,128)(2,1)}, f32[64,512]{1,0:T(8,128)}, f32[64,512]{1,0:T(8,128)}) custom-call(s32[6]{0:T(128)} %pad_add_fusion.place_ref.place, bf16[144,2048]{1,0:T(8,128)(2,1)} %copy-done.10, bf16[144,2048]{1,0:T(8,128)(2,1)} %copy-done.11, ...), custom_call_target="tpu_custom_call" | custom-call | bytes 9100000 | tf_op jit(solution)/shard_map/head_gradients/pallas_call | solution.py:56
  253.4 4.3 %collective-permute-start.29 = (bf16[128,512]{1,0:T(8,128)(2,1)S(1)}, bf16[128,512]{1,0:T(8,128)(2,1)S(1)}, u32[]{:S(2)}, u32[]{:S(2)}) collective-permute-start(bf16[128,512]{1,0:T(8,128)(2,1)S(1)} %pad_maximum_fusion.6), channel_id=1, source_target_pairs={{0,24},{8,0},{16,8},{24,16},{1,25},{9,1},{17,9},{25,17},{2,26},{10... | collective-permute-start | bytes 393224 | tf_op jit(solution)/shard_map/ppermute | solution.py:34
  258.7 11.7 %attention_backward.1 = (f32[1024,512]{1,0:T(8,128)}, f32[4,128,256]{2,1,0:T(8,128)}, bf16[4,128,256]{2,1,0:T(8,128)(2,1)}) custom-call(s32[6]{0:T(128)} %pad_add_fusion.place_ref.place, bf16[1024,512]{1,0:T(8,128)(2,1)} %q_ref.5, bf16[1024,512]{1,0:T(8,128)(2,1)} %k_ref.5, bf16[1024,512]{1,0:T(8,128)(2,1)} %v_ref.5, ...), custom_call_target="tpu_custom_call" | custom-call | bytes 11800000 | tf_op jit(solution)/shard_map/attention_backward/pallas_call | solution.py:594
  (214 shorter events, 92.4 us)
Async XLA Ops:
  3.7 29.3 %collective-permute-start.2 = (bf16[128,2048]{1,0:T(8,128)(2,1)}, bf16[128,2048]{1,0:T(8,128)(2,1)S(1)}, u32[]{:S(2)}, u32[]{:S(2)}) collective-permute-start(bf16[128,2048]{1,0:T(8,128)(2,1)} %refs_0_.3), channel_id=1, source_target_pairs={{0,8},{8,16},{16,24},{24,0},{1,9},{9,17},{17,25},{25,1},{2,10},{10... | collective-permute-start | bytes 1572872 | tf_op jit(solution)/shard_map/ppermute | solution.py:34
  6.4 26.6 %collective-permute-start.3 = (bf16[128,2048]{1,0:T(8,128)(2,1)}, bf16[128,2048]{1,0:T(8,128)(2,1)S(1)}, u32[]{:S(2)}, u32[]{:S(2)}) collective-permute-start(bf16[128,2048]{1,0:T(8,128)(2,1)} %refs_0_.3), channel_id=1, source_target_pairs={{0,24},{8,0},{16,8},{24,16},{1,25},{9,1},{17,9},{25,17},{2,26},{10... | collective-permute-start | bytes 1572872 | tf_op jit(solution)/shard_map/ppermute | solution.py:34
  8.5 24.5 %collective-permute-start.4 = (f32[2,16,128]{2,1,0:T(8,128)S(1)}, f32[2,16,128]{2,1,0:T(8,128)S(1)}, u32[]{:S(2)}, u32[]{:S(2)}) collective-permute-start(f32[2,16,128]{2,1,0:T(8,128)S(1)} %pad_maximum_fusion.7), channel_id=1, source_target_pairs={{0,8},{8,16},{16,24},{24,0},{1,9},{9,17},{17,25},{25,1},{2,10},{10... | collective-permute-start | bytes 49160 | tf_op jit(solution)/shard_map/ppermute | solution.py:34
  8.5 24.5 %collective-permute-start.5 = (f32[2,16,128]{2,1,0:T(8,128)S(1)}, f32[2,16,128]{2,1,0:T(8,128)S(1)}, u32[]{:S(2)}, u32[]{:S(2)}) collective-permute-start(f32[2,16,128]{2,1,0:T(8,128)S(1)} %pad_maximum_fusion.7), channel_id=1, source_target_pairs={{0,24},{8,0},{16,8},{24,16},{1,25},{9,1},{17,9},{25,17},{2,26},{10... | collective-permute-start | bytes 49160 | tf_op jit(solution)/shard_map/ppermute | solution.py:34
  17.6 24.9 %all-to-all-start = ((bf16[4,80,2048]{2,1,0:T(8,128)(2,1)}), bf16[4,80,2048]{2,1,0:T(8,128)(2,1)S(1)}, u32[]{:S(2)}, u32[]{:S(2)}) async-start(bf16[4,80,2048]{2,1,0:T(8,128)(2,1)} %dispatch.3.refs_0_), calls=%async_computation | async-start | bytes 2621440 | tf_op jit(solution)/shard_map/all_to_all | solution.py:726
  34.0 35.8 %collective-permute-start.8 = (bf16[128,2048]{1,0:T(8,128)(2,1)S(1)}, bf16[128,2048]{1,0:T(8,128)(2,1)}, u32[]{:S(2)}, u32[]{:S(2)}) collective-permute-start(bf16[128,2048]{1,0:T(8,128)(2,1)S(1)} %copy-done.4), channel_id=1, source_target_pairs={{0,16},{8,24},{16,0},{24,8},{1,17},{9,25},{17,1},{25,9},{2,18},{10... | collective-permute-start | bytes 1572872 | tf_op jit(solution)/shard_map/ppermute | solution.py:34
  43.6 34.9 %all-to-all-start.1 = ((bf16[4,160,2048]{2,1,0:T(8,128)(2,1)}), bf16[4,160,2048]{2,1,0:T(8,128)(2,1)S(1)}, u32[]{:S(2)}, u32[]{:S(2)}) async-start(bf16[4,160,2048]{2,1,0:T(8,128)(2,1)} %dispatch.4.refs_8_), calls=%async_computation.1 | async-start | bytes 5242880 | tf_op jit(solution)/shard_map/all_to_all | solution.py:726
  47.8 22.0 %collective-permute-start.9 = (f32[2,16,128]{2,1,0:T(8,128)S(1)}, f32[2,16,128]{2,1,0:T(8,128)S(1)}, u32[]{:S(2)}, u32[]{:S(2)}) collective-permute-start(f32[2,16,128]{2,1,0:T(8,128)S(1)} %pad_maximum_fusion.7), channel_id=1, source_target_pairs={{0,16},{8,24},{16,0},{24,8},{1,17},{9,25},{17,1},{25,9},{2,18},{10... | collective-permute-start | bytes 49160 | tf_op jit(solution)/shard_map/ppermute | solution.py:34
  78.4 23.7 %all-to-all-start.2 = ((bf16[4,88,2048]{2,1,0:T(8,128)(2,1)}), bf16[4,88,2048]{2,1,0:T(8,128)(2,1)}, u32[]{:S(2)}, u32[]{:S(2)}) async-start(bf16[4,88,2048]{2,1,0:T(8,128)(2,1)} %dispatch.5.refs_10_), calls=%async_computation.2 | async-start | bytes 2883584 | tf_op jit(solution)/shard_map/all_to_all | solution.py:726
  98.5 18.2 %collective-permute-start.11 = (bf16[160,2048]{1,0:T(8,128)(2,1)}, bf16[160,2048]{1,0:T(8,128)(2,1)S(1)}, u32[]{:S(2)}, u32[]{:S(2)}) collective-permute-start(bf16[160,2048]{1,0:T(8,128)(2,1)} %get-tuple-element.94), channel_id=1, source_target_pairs={{0,2},{1,3},{2,0},{3,1},{4,6},{5,7},{6,4},{7,5},{8,10},{9,11},{10,... | collective-permute-start | bytes 1966088 | tf_op jit(solution)/shard_map/ppermute | solution.py:29
  100.6 38.9 %collective-permute-start.12 = (bf16[160,2048]{1,0:T(8,128)(2,1)}, bf16[160,2048]{1,0:T(8,128)(2,1)S(1)}, u32[]{:S(2)}, u32[]{:S(2)}) collective-permute-start(bf16[160,2048]{1,0:T(8,128)(2,1)} %get-tuple-element.95), channel_id=1, source_target_pairs={{0,4},{1,5},{2,6},{3,7},{4,0},{5,1},{6,2},{7,3},{8,12},{9,13},{10,... | collective-permute-start | bytes 1966088 | tf_op jit(solution)/shard_map/ppermute | solution.py:29
  102.0 37.5 %collective-permute-start.13 = (bf16[160,2048]{1,0:T(8,128)(2,1)}, bf16[160,2048]{1,0:T(8,128)(2,1)S(1)}, u32[]{:S(2)}, u32[]{:S(2)}) collective-permute-start(bf16[160,2048]{1,0:T(8,128)(2,1)} %get-tuple-element.96), channel_id=1, source_target_pairs={{0,6},{1,7},{2,4},{3,5},{4,2},{5,3},{6,0},{7,1},{8,14},{9,15},{10,... | collective-permute-start | bytes 1966088 | tf_op jit(solution)/shard_map/ppermute | solution.py:29
  102.1 43.2 %all-to-all-start.3 = ((bf16[4,80,2048]{2,1,0:T(8,128)(2,1)}), bf16[4,80,2048]{2,1,0:T(8,128)(2,1)S(1)}, u32[]{:S(2)}, u32[]{:S(2)}) async-start(bf16[4,80,2048]{2,1,0:T(8,128)(2,1)} %get-tuple-element.93.refs_2_), calls=%async_computation.3 | async-start | bytes 2621440 | tf_op jit(solution)/shard_map/all_to_all | solution.py:726
  145.3 21.3 %all-to-all-start.4 = ((bf16[4,80,2048]{2,1,0:T(8,128)(2,1)}), bf16[4,80,2048]{2,1,0:T(8,128)(2,1)S(1)}, u32[]{:S(2)}, u32[]{:S(2)}) async-start(bf16[4,80,2048]{2,1,0:T(8,128)(2,1)} %get-tuple-element.97.refs_6_), calls=%async_computation.4 | async-start | bytes 2621440 | tf_op jit(solution)/shard_map/all_to_all | solution.py:726
  150.5 16.2 %collective-permute-start.15 = (bf16[128,2048]{1,0:T(8,128)(2,1)S(1)}, bf16[128,2048]{1,0:T(8,128)(2,1)S(1)}, u32[]{:S(2)}, u32[]{:S(2)}) collective-permute-start(bf16[128,2048]{1,0:T(8,128)(2,1)S(1)} %add_convert_fusion.2), channel_id=1, source_target_pairs={{0,8},{8,16},{16,24},{24,0},{1,9},{9,17},{17,25},{25,1},{2,10},{10... | collective-permute-start | bytes 1572872 | tf_op jit(solution)/shard_map/ppermute | solution.py:34
  175.1 14.0 %collective-permute-start.18 = (bf16[128,2048]{1,0:T(8,128)(2,1)S(1)}, bf16[128,2048]{1,0:T(8,128)(2,1)S(1)}, u32[]{:S(2)}, u32[]{:S(2)}) collective-permute-start(bf16[128,2048]{1,0:T(8,128)(2,1)S(1)} %add_convert_fusion.1), channel_id=1, source_target_pairs={{0,24},{8,0},{16,8},{24,16},{1,25},{9,1},{17,9},{25,17},{2,26},{10... | collective-permute-start | bytes 1572872 | tf_op jit(solution)/shard_map/ppermute | solution.py:34
  178.1 15.1 %collective-permute-start.21 = (bf16[64,128]{1,0:T(8,128)(2,1)S(1)}, bf16[64,128]{1,0:T(8,128)(2,1)S(1)}, u32[]{:S(2)}, u32[]{:S(2)}) collective-permute-start(bf16[64,128]{1,0:T(8,128)(2,1)S(1)} %fusion.47), channel_id=1, source_target_pairs={{0,1},{1,0},{2,3},{3,2},{4,5},{5,4},{6,7},{7,6},{8,9},{9,8},{10,11... | collective-permute-start | bytes 49160 | tf_op jit(solution)/shard_map/ppermute | solution.py:29
  178.2 15.6 %collective-permute-start.20 = (bf16[128,2048]{1,0:T(8,128)(2,1)S(1)}, bf16[128,2048]{1,0:T(8,128)(2,1)S(1)}, u32[]{:S(2)}, u32[]{:S(2)}) collective-permute-start(bf16[128,2048]{1,0:T(8,128)(2,1)S(1)} %copy-done.23), channel_id=1, source_target_pairs={{0,1},{1,0},{2,3},{3,2},{4,5},{5,4},{6,7},{7,6},{8,9},{9,8},{10,11... | collective-permute-start | bytes 1572872 | tf_op jit(solution)/shard_map/ppermute | solution.py:29
  189.3 14.5 %collective-permute-start.19 = (bf16[128,2048]{1,0:T(8,128)(2,1)S(1)}, bf16[128,2048]{1,0:T(8,128)(2,1)S(1)}, u32[]{:S(2)}, u32[]{:S(2)}) collective-permute-start(bf16[128,2048]{1,0:T(8,128)(2,1)S(1)} %add_convert_fusion), channel_id=1, source_target_pairs={{0,24},{8,0},{16,8},{24,16},{1,25},{9,1},{17,9},{25,17},{2,26},{10... | collective-permute-start | bytes 1572872 | tf_op jit(solution)/shard_map/ppermute | solution.py:34
  208.9 16.3 %collective-permute-start.22 = (bf16[144,2048]{1,0:T(8,128)(2,1)}, bf16[144,2048]{1,0:T(8,128)(2,1)S(1)}, u32[]{:S(2)}, u32[]{:S(2)}) collective-permute-start(bf16[144,2048]{1,0:T(8,128)(2,1)} %get-tuple-element.112), channel_id=1, source_target_pairs={{0,2},{1,3},{2,0},{3,1},{4,6},{5,7},{6,4},{7,5},{8,10},{9,11},{10,... | collective-permute-start | bytes 1769480 | tf_op jit(solution)/shard_map/ppermute | solution.py:29
  210.3 28.3 %collective-permute-start.23 = (bf16[144,2048]{1,0:T(8,128)(2,1)}, bf16[144,2048]{1,0:T(8,128)(2,1)S(1)}, u32[]{:S(2)}, u32[]{:S(2)}) collective-permute-start(bf16[144,2048]{1,0:T(8,128)(2,1)} %get-tuple-element.113), channel_id=1, source_target_pairs={{0,4},{1,5},{2,6},{3,7},{4,0},{5,1},{6,2},{7,3},{8,12},{9,13},{10,... | collective-permute-start | bytes 1769480 | tf_op jit(solution)/shard_map/ppermute | solution.py:29
  210.9 27.8 %collective-permute-start.24 = (bf16[144,2048]{1,0:T(8,128)(2,1)}, bf16[144,2048]{1,0:T(8,128)(2,1)S(1)}, u32[]{:S(2)}, u32[]{:S(2)}) collective-permute-start(bf16[144,2048]{1,0:T(8,128)(2,1)} %get-tuple-element.114), channel_id=1, source_target_pairs={{0,6},{1,7},{2,4},{3,5},{4,2},{5,3},{6,0},{7,1},{8,14},{9,15},{10,... | collective-permute-start | bytes 1769480 | tf_op jit(solution)/shard_map/ppermute | solution.py:29
  253.4 17.1 %collective-permute-start.29 = (bf16[128,512]{1,0:T(8,128)(2,1)S(1)}, bf16[128,512]{1,0:T(8,128)(2,1)S(1)}, u32[]{:S(2)}, u32[]{:S(2)}) collective-permute-start(bf16[128,512]{1,0:T(8,128)(2,1)S(1)} %pad_maximum_fusion.6), channel_id=1, source_target_pairs={{0,24},{8,0},{16,8},{24,16},{1,25},{9,1},{17,9},{25,17},{2,26},{10... | collective-permute-start | bytes 393224 | tf_op jit(solution)/shard_map/ppermute | solution.py:34
  257.8 12.8 %collective-permute-start.31 = (bf16[128,512]{1,0:T(8,128)(2,1)S(1)}, bf16[128,512]{1,0:T(8,128)(2,1)S(1)}, u32[]{:S(2)}, u32[]{:S(2)}) collective-permute-start(bf16[128,512]{1,0:T(8,128)(2,1)S(1)} %pad_maximum_fusion.6), channel_id=1, source_target_pairs={{0,8},{8,16},{16,24},{24,0},{1,9},{9,17},{17,25},{25,1},{2,10},{10... | collective-permute-start | bytes 393224 | tf_op jit(solution)/shard_map/ppermute | solution.py:34
  (45 other events, 297.1 us)

commit v4 on v3

--- a/solution.py
+++ b/solution.py
@@ -14,7 +14,7 @@
 adapter_scale = 2.0
 neg_big = -1e30
 att_scale = HEAD_SIZE ** (-0.5)
-VMEM_BYTES = 56 * 1024 * 1024
+VMEM_BYTES = 36 * 1024 * 1024
 COST_UNIT = 1000000
 
 
@@ -46,8 +46,15 @@
     return pl.BlockSpec(shape, lambda i, place: (0,) * len(shape))
 
 
-def kernel_call(body, place, operands, specs, outs, out_specs, after, scratch=(), steps=1, name=None, cost=1.0):
+def kernel_call(
+    body, place, operands, specs, outs, out_specs, after, scratch=(), steps=1, name=None, cost=1.0, held=0, far=True
+):
     deps = len(after)
+    after = in_hbm(*after) if far else after
+    operands, specs = list(operands), list(specs)
+    for n in range(held):
+        operands[n] = pltpu.with_memory_space_constraint(operands[n], pltpu.VMEM)
+        specs[n] = pl.BlockSpec(memory_space=pltpu.VMEM)
 
     def kernel(place_ref, *refs):
         count = len(operands)
@@ -71,12 +78,20 @@
     )(place, *operands, *after)
 
 
+def in_hbm(*arrays):
+    return [pltpu.with_memory_space_constraint(a, pltpu.HBM) for a in arrays]
+
+
 def bf16(*shape):
-    return jax.ShapeDtypeStruct(shape, jnp.bfloat16)
+    return pltpu.HBM(shape, jnp.bfloat16)
 
 
 def f32(*shape):
-    return jax.ShapeDtypeStruct(shape, jnp.float32)
+    return pltpu.HBM(shape, jnp.float32)
+
+
+def anywhere(*outs):
+    return [jax.ShapeDtypeStruct(a.shape, a.dtype) for a in outs]
 
 
 def filled_cells(ranks, count):
@@ -88,14 +103,14 @@
     return refs[0].at[(place_ref[0] // 2) ^ j] if len(refs) == 1 else refs[j]
 
 
-def dispatch(place, own, other, tables, cells, stacked, extra, after):
+def dispatch(place, own, other, tables, cells, stacked, extra, fresh, after):
     planes = len(own)
     pairs = tables[0].shape[1]
     width = own[0].shape[1]
 
     def body(place_ref, *refs):
         for i in range(planes):
-            own_ref, other_ref, table_ref = refs[i], refs[planes + i], refs[2 * planes + i]
+            other_ref, own_ref, table_ref = refs[i], refs[planes + i], refs[2 * planes + i]
             tokens = jnp.concatenate([own_ref[...], other_ref[...]], axis=0)
             filled = [filled_cells(table_ref[0, j : j + 1, :], cells) for j in range(pairs)]
             weights = [
@@ -124,7 +139,7 @@
                             q * added : (q + 1) * added
                         ]
 
-    operands = [*own, *other, *tables, *extra]
+    operands = [*other, *(own if fresh else in_hbm(*own)), *tables, *extra]
     added = 2 * extra[0].shape[1] * extra[0].shape[2] // width if extra else 0
     outs = [bf16(planes * cells, width)] * pairs
     if stacked:
@@ -138,6 +153,7 @@
         [whole_of(a.shape) for a in outs],
         after,
         name="dispatch",
+        held=2 * planes if fresh else planes,
         cost=3.5,
     )
 
@@ -178,6 +194,7 @@
         [whole_of(a.shape) for a in outs],
         after,
         name="combine",
+        held=count,
         cost=4.5,
     )
     return result[::2], result[1::2]
@@ -293,7 +310,7 @@
     result = kernel_call(
         body,
         place,
-        [*parts, reorder, *[saved] * (2 * planes), down, gate_up, first, second],
+        [*parts, reorder, *in_hbm(*[saved] * (2 * planes), down, gate_up, first, second)],
         specs,
         [*outs, bf16(rows, width_ff), bf16(rows, rank)],
         [
@@ -317,6 +334,7 @@
         ],
         steps=blocks + sides,
         name="expert",
+        held=count,
         cost=8.0 + 4.5 * planes,
     )
     return result[:results], result[results], result[results + 1]
@@ -357,7 +375,7 @@
         grad_first_ref[...] = adapter_scale * grad_first
         grad_second_ref[...] = adapter_scale * grad_second
 
-    operands.append(first)
+    operands += in_hbm(first)
     outs = [f32(rank, width_ff), f32(rank, width)]
     return kernel_call(
         body,
@@ -397,7 +415,7 @@
                 messages[j][rows:, q * share : (q + 1) * share] = part[q * extra : (q + 1) * extra]
 
     operands = [gradient, *sums, folded]
-    outs = [bf16(rows, width)] + [bf16(rows + extra, width)] * pairs
+    outs = anywhere(bf16(rows, width), *[bf16(rows + extra, width)] * pairs)
     result = kernel_call(
         body,
         place,
@@ -408,6 +426,7 @@
         after,
         scratch=[pltpu.VMEM((pairs, rank, share), jnp.bfloat16)],
         name="residual_messages",
+        held=count + 1,
         cost=4.0,
     )
     return result[0], list(result[1:])
@@ -447,12 +466,14 @@
         for q in range(pairs):
             columns_ref[q * extra : (q + 1) * extra, :] = columns[:, q * share : (q + 1) * share]
 
-    operands = [*own, *other, weight, first, second, *[attended] * count]
+    operands = [*own, *other, *in_hbm(weight, first, second, *[attended] * count)]
     specs = [whole_of(a.shape) for a in operands[: 2 * count + 3]] + [
         pl.BlockSpec((2 * rows, heads_width), lambda i, place, j=j: ((place[0] // 2) ^ j, 0))
         for j in numbers
     ]
-    outs = [*[bf16(2 * rows, heads_width)] * count, f32(rank, heads_width), f32(rank, share)]
+    outs = anywhere(
+        *[bf16(2 * rows, heads_width)] * count, f32(rank, heads_width), f32(rank, share)
+    )
     result = kernel_call(
         body,
         place,
@@ -462,6 +483,8 @@
         [whole_of(a.shape) for a in outs],
         after,
         name="head_gradients",
+        held=2 * count,
+        far=False,
         cost=2.5 + 2.2 * count,
     )
     return list(result[:count]), result[count], result[count + 1]
@@ -535,7 +558,7 @@
         ),
         cost_estimate=estimate(2.2 * rows / 512 * count),
         name="attention_forward",
-    )(place, queries, keys, values, first_factor, *earlier, *after)
+    )(place, *in_hbm(queries, keys, values, first_factor), *earlier, *after)
 
 
 def backward_kernel(place, q_ref, k_ref, v_ref, att_ref, probs_ref, *refs):
@@ -622,7 +645,7 @@
         ),
         cost_estimate=estimate(11.8),
         name="attention_backward",
-    )(place, queries, keys, values, attended, probs, *gradients, *after)
+    )(place, *in_hbm(queries, keys, values, attended, probs), *gradients, *after)
 
 
 def planes_sum(parts, grp_index):
@@ -736,6 +759,7 @@
             cells,
             stacked and aligned,
             extra,
+            group != [0],
             last,
         )
         last[:] = messages[:1]
@@ -831,11 +855,10 @@
         rows = finished[n][0]
         if n == 1:
             back[1] = exchanged(rows)
-            held, _ = lax.optimization_barrier((finished[0][0], (last, arrived[max(arrived)])))
-            back[0] = exchanged(held)
         else:
-            rows, _ = lax.optimization_barrier((rows, (back[0], back[1])))
             back[2] = exchanged(rows)
+    held, _ = lax.optimization_barrier((finished[0][0], back[max(back)]))
+    back[0] = exchanged(held)
 
     def sent_home(group, totals, via):
         totals = {s: total.astype(jnp.bfloat16) for s, total in zip(group, totals)}
@@ -846,15 +869,14 @@
     if relayed:
         waiting = totals.pop(groups[1].index(1))
     sums = sent_home([s for s in groups[1] if s != 1 or not relayed], totals, {})
-    own_sum = combined(groups[0], back[0])[0]
     if len(groups) > 2:
-        back[2], sums = lax.optimization_barrier((back[2], sums))
+        back[0], sums = lax.optimization_barrier((back[0], sums))
         sums += sent_home(groups[2], combined(groups[2], back[2]), {2: 1} if relayed else {})
     if relayed:
         passed = (waiting + sums.pop().astype(jnp.float32)).astype(jnp.bfloat16)
         sums.append(shift(passed, -1))
         last[:] = lax.optimization_barrier((last, passed))[0]
-    sums.append(own_sum)
+    sums.append(combined(groups[0], back[0])[0])
     grad_first, grad_second = adapter_gradients(
         place, [finished[k][1] for k in finished], down_first_factor[0], cells, pairs, last
     )

time: 292 us -> 275 us (0.942)
  Pallas kernels: 114 us -> 102 us
  waiting for transfers between devices: 84.6 us -> 95.5 us
  other arithmetic: 17.3 us -> 11.6 us
  local copies, waits for them, and re-layouts: 10.2 us -> 5.03 us
  starting transfers between devices: 58.5 us -> 53.6 us
    pallas_call x13, Pallas kernels: 84.8 us -> 74.4 us  [kernel_call(): pl.pallas_call(kernel, grid_spec=pltpu.PrefetchScalarGridSpec(num_scalar_...]
    ppermute x12, waiting for transfers between devices: 26.4 us -> 33.8 us  [shift(): lax.ppermute(value, 'grp', [(i, (i + step) % count) for i in range(count)])]
    ppermute x12, starting transfers between devices: 24.4 us -> 18.4 us  [shift(): lax.ppermute(value, 'grp', [(i, (i + step) % count) for i in range(count)])]
    unnamed x56 -> x36, local copies, waits for them, and re-layouts: 8.9 us -> 3.76 us
    all_to_all x5, waiting for transfers between devices: 1.91 us -> 6.45 us  [exchanged(): lax.all_to_all(parts[0], 'dev', 0, 0, axis_index_groups=chips, tiled=True)]
  transfers between devices with their start and end apart: 41 -> 41, of which waited for: 17 -> 22; matrix products, arithmetic and copies ran while one was open for 4% -> 2% of each run, Pallas kernels for 34% -> 33%
where the time goes in v4:
time: 275 us; the launch traced here: 270 us
  Pallas kernels  102 us (37%)
  waiting for transfers between devices  95.5 us (35%)
  starting transfers between devices  53.6 us (19%)
  other arithmetic  11.6 us (4%)
  local copies, waits for them, and re-layouts  5.03 us (2%)
    pallas_call x13, Pallas kernels, kernel_call(): pl.pallas_call(kernel, grid_spec=pltpu.PrefetchScalarGridSpec(num_scalar_...  74.4 us
    ppermute x24, waiting for transfers between devices, across(): return lax.ppermute(value, 'dev', [(i, i ^ step) for i in range(count)])  55.2 us
    ppermute x12, waiting for transfers between devices, shift(): lax.ppermute(value, 'grp', [(i, (i + step) % count) for i in range(count)])  33.8 us
    all_to_all x5, starting transfers between devices, exchanged(): lax.all_to_all(parts[0], 'dev', 0, 0, axis_index_groups=chips, tiled=True)  21.7 us
    ppermute x12, starting transfers between devices, shift(): lax.ppermute(value, 'grp', [(i, (i + step) % count) for i in range(count)])  18.4 us
    pallas_call x2, Pallas kernels, attention_forward(): pl.pallas_call(forward_kernel, grid_spec=pltpu.PrefetchScalarGridSpec(num...  16.7 us
    ppermute x24, starting transfers between devices, across(): return lax.ppermute(value, 'dev', [(i, i ^ step) for i in range(count)])  13.4 us
    pallas_call x1, Pallas kernels, attention_backward(): pl.pallas_call(backward_kernel, grid_spec=pltpu.PrefetchScalarGridSpec(nu...  11.1 us
  transfers between devices with their start and end apart: 41, of which 22 were waited for; matrix products, arithmetic and copies ran while one was open for 2% of the time, Pallas kernels for 33%

profile of v4, /device:TPU:0, one launch (start us, length us, event | category | flops | bytes accessed | tf_op | source)
XLA Modules:
  0.0 269.9 jit_solution(7244194957124484133)
XLA Ops:
  8.3 3.8 %collective-permute-start.5 = (f32[2,16,128]{2,1,0:T(8,128)S(1)}, f32[2,16,128]{2,1,0:T(8,128)S(1)}, u32[]{:S(2)}, u32[]{:S(2)}) collective-permute-start(f32[2,16,128]{2,1,0:T(8,128)S(1)} %pad_maximum_fusion.7), channel_id=1, source_target_pairs={{0,24},{8,0},{16,8},{24,16},{1,25},{9,1},{17,9},{25,17},{2,26},{10... | collective-permute-start | bytes 49160 | tf_op jit(solution)/shard_map/ppermute | solution.py:34
  15.7 4.0 %all-to-all-start = ((bf16[4,80,2048]{2,1,0:T(8,128)(2,1)}), bf16[4,80,2048]{2,1,0:T(8,128)(2,1)S(1)}, u32[]{:S(2)}, u32[]{:S(2)}) async-start(bf16[4,80,2048]{2,1,0:T(8,128)(2,1)} %dispatch.3.refs_0_), calls=%async_computation | async-start | bytes 2621440 | tf_op jit(solution)/shard_map/all_to_all | solution.py:749
  19.7 8.3 %attention_forward.2 = (bf16[4,1024,1024]{2,1,0:T(8,128)(2,1)}, bf16[1024,512]{1,0:T(8,128)(2,1)}, f32[8,64,128]{2,1,0:T(8,128)}) custom-call(s32[6]{0:T(128)S(1)} %pad_add_fusion.place_ref.place, bf16[1024,512]{1,0:T(8,128)(2,1)} %q_ref.5, bf16[1024,512]{1,0:T(8,128)(2,1)} %k_ref.5, bf16[1024,512]{1,0:T(8,128)(2,1)} %v_ref.5, bf16[64,512]{1,0:T(8,128)(2,1)} %refs_7_.1, ...), custom_call_target="tpu_custom_call" | custom-call | bytes 8800000 | tf_op jit(solution)/shard_map/attention_forward/pallas_call | solution.py:532
  28.1 4.6 %collective-permute-done.4 = f32[2,16,128]{2,1,0:T(8,128)S(1)} collective-permute-done((f32[2,16,128]{2,1,0:T(8,128)S(1)}, f32[2,16,128]{2,1,0:T(8,128)S(1)}, u32[]{:S(2)}, u32[]{:S(2)}) %collective-permute-start.4) | collective-permute-done | bytes 16416 | tf_op jit(solution)/shard_map/ppermute | solution.py:34
  35.6 4.3 %dispatch.4.refs_8_ = bf16[4,160,2048]{2,1,0:T(8,128)(2,1)} custom-call(s32[6]{0:T(128)S(1)} %pad_add_fusion.place_ref.place, bf16[128,2048]{1,0:T(8,128)(2,1)S(1)} %collective-permute-done.6.refs_0_, bf16[128,2048]{1,0:T(8,128)(2,1)S(1)} %collective-permute-done.7.refs_1_, bf16[128,2048]{1,0:T(8,128)(2,1)} %collective-permute-done.2.refs_2_, ...), custom_call_target="tpu_custom_call" | custom-call | bytes 3500000 | tf_op jit(solution)/shard_map/dispatch/pallas_call | solution.py:63
  40.9 4.2 %all-to-all-start.1 = ((bf16[4,160,2048]{2,1,0:T(8,128)(2,1)}), bf16[4,160,2048]{2,1,0:T(8,128)(2,1)S(1)}, u32[]{:S(2)}, u32[]{:S(2)}) async-start(bf16[4,160,2048]{2,1,0:T(8,128)(2,1)} %dispatch.4.refs_8_), calls=%async_computation.1 | async-start | bytes 5242880 | tf_op jit(solution)/shard_map/all_to_all | solution.py:749
  47.8 10.5 %expert.3 = (bf16[4,80,2048]{2,1,0:T(8,128)(2,1)}, bf16[320,768]{1,0:T(8,128)(2,1)}, bf16[320,64]{1,0:T(8,128)(2,1)}) custom-call(s32[6]{0:T(128)S(1)} %pad_add_fusion.place_ref.place, bf16[4,80,2048]{2,1,0:T(8,128)(2,1)S(1)} %copy-done.2, bf16[320,320]{1,0:T(8,128)(2,1)S(1)} %fusion.4.refs_1_, bf16[1280,1536]{1,0:T(8,128)(2,1)} %bitcast.123, ...), custom_call_target="tpu_custom_call" | custom-call | bytes 12500000 | tf_op jit(solution)/shard_map/expert/pallas_call | solution.py:63
  59.6 8.3 %attention_forward.3 = (bf16[4,1024,1024]{2,1,0:T(8,128)(2,1)}, bf16[1024,512]{1,0:T(8,128)(2,1)}, f32[8,64,128]{2,1,0:T(8,128)}) custom-call(s32[6]{0:T(128)S(1)} %pad_add_fusion.place_ref.place, bf16[1024,512]{1,0:T(8,128)(2,1)} %q_ref.5, bf16[1024,512]{1,0:T(8,128)(2,1)} %k_ref.5, ...), custom_call_target="tpu_custom_call", output_to_operand_aliasing={{0}: (5, {}), {1}: (6, {})} | custom-call | bytes 8800000 | tf_op jit(solution)/shard_map/attention_forward/pallas_call | solution.py:532
  76.1 4.5 %all-to-all-start.2 = ((bf16[4,88,2048]{2,1,0:T(8,128)(2,1)}), bf16[4,88,2048]{2,1,0:T(8,128)(2,1)}, u32[]{:S(2)}, u32[]{:S(2)}) async-start(bf16[4,88,2048]{2,1,0:T(8,128)(2,1)} %dispatch.5.refs_10_), calls=%async_computation.2 | async-start | bytes 2883584 | tf_op jit(solution)/shard_map/all_to_all | solution.py:749
  80.6 14.6 %expert.4 = (bf16[160,2048]{1,0:T(8,128)(2,1)}, bf16[160,2048]{1,0:T(8,128)(2,1)}, bf16[160,2048]{1,0:T(8,128)(2,1)}, bf16[160,2048]{1,0:T(8,128)(2,1)}, bf16[64...) custom-call(s32[6]{0:T(128)S(1)} %pad_add_fusion.place_ref.place, bf16[4,160,2048]{2,1,0:T(8,128)(2,1)S(1)} %all-to-all-done.1.refs_0_.refs_3_, ...), custom_call_target="tpu_custom_call" | custom-call | bytes 17000000 | tf_op jit(solution)/shard_map/expert/pallas_call | solution.py:63
  98.9 10.2 %expert.5 = (bf16[4,80,2048]{2,1,0:T(8,128)(2,1)}, bf16[320,768]{1,0:T(8,128)(2,1)}, bf16[320,64]{1,0:T(8,128)(2,1)}) custom-call(s32[6]{0:T(128)S(1)} %pad_add_fusion.place_ref.place, bf16[4,88,2048]{2,1,0:T(8,128)(2,1)} %all-to-all-done.2.refs_0_.refs_6_, bf16[320,320]{1,0:T(8,128)(2,1)S(1)} %fusion.4.refs_1_, bf16[1280,1536]{1,0:T(8,128)(2,1)} %bitcast.129, ...), custom_call_target="tpu_custom_call" | custom-call | bytes 12500000 | tf_op jit(solution)/shard_map/expert/pallas_call | solution.py:63
  109.1 4.7 %all-to-all-start.3 = ((bf16[4,80,2048]{2,1,0:T(8,128)(2,1)}), bf16[4,80,2048]{2,1,0:T(8,128)(2,1)}, u32[]{:S(2)}, u32[]{:S(2)}) async-start(bf16[4,80,2048]{2,1,0:T(8,128)(2,1)} %get-tuple-element.91.refs_6_), calls=%async_computation.3 | async-start | bytes 2621440 | tf_op jit(solution)/shard_map/all_to_all | solution.py:749
  113.8 19.1 %collective-permute-done.12.refs_2_ = bf16[160,2048]{1,0:T(8,128)(2,1)} collective-permute-done((bf16[160,2048]{1,0:T(8,128)(2,1)}, bf16[160,2048]{1,0:T(8,128)(2,1)}, u32[]{:S(2)}, u32[]{:S(2)}) %collective-permute-start.12) | collective-permute-done | bytes 655392 | tf_op jit(solution)/shard_map/ppermute | solution.py:29
  133.0 4.4 %combine.3 = (f32[128,2048]{1,0:T(8,128)}, bf16[128,2048]{1,0:T(8,128)(2,1)}, f32[128,2048]{1,0:T(8,128)}, bf16[128,2048]{1,0:T(8,128)(2,1)}) custom-call(s32[6]{0:T(128)S(1)} %pad_add_fusion.place_ref.place, bf16[160,2048]{1,0:T(8,128)(2,1)S(1)} %copy-done.5, bf16[160,2048]{1,0:T(8,128)(2,1)} %collective-permute-done.11.refs_1_, ...), custom_call_target="tpu_custom_call" | custom-call | bytes 4500000 | tf_op jit(solution)/shard_map/combine/pallas_call | solution.py:63
  137.4 3.8 %all-to-all-done.3.refs_0_ = bf16[4,80,2048]{2,1,0:T(8,128)(2,1)} async-done(((bf16[4,80,2048]{2,1,0:T(8,128)(2,1)}), bf16[4,80,2048]{2,1,0:T(8,128)(2,1)}, u32[]{:S(2)}, u32[]{:S(2)}) %all-to-all-start.3) | async-done | bytes 1310752 | tf_op jit(solution)/shard_map/all_to_all | solution.py:749
  145.4 4.3 %all-to-all-start.4 = ((bf16[4,80,2048]{2,1,0:T(8,128)(2,1)}), bf16[4,80,2048]{2,1,0:T(8,128)(2,1)}, u32[]{:S(2)}, u32[]{:S(2)}) async-start(bf16[4,80,2048]{2,1,0:T(8,128)(2,1)} %get-tuple-element.92.refs_2_), calls=%async_computation.4 | async-start | bytes 2621440 | tf_op jit(solution)/shard_map/all_to_all | solution.py:749
  157.0 10.8 %collective-permute-done.15.refs_1_ = bf16[128,2048]{1,0:T(8,128)(2,1)S(1)} collective-permute-done((bf16[128,2048]{1,0:T(8,128)(2,1)S(1)}, bf16[128,2048]{1,0:T(8,128)(2,1)S(1)}, u32[]{:S(2)}, u32[]{:S(2)}) %collective-permute-start.15) | collective-permute-done | bytes 524320 | tf_op jit(solution)/shard_map/ppermute | solution.py:34
  167.9 10.4 %collective-permute-done.18 = bf16[128,2048]{1,0:T(8,128)(2,1)} collective-permute-done((bf16[128,2048]{1,0:T(8,128)(2,1)}, bf16[128,2048]{1,0:T(8,128)(2,1)}, u32[]{:S(2)}, u32[]{:S(2)}) %collective-permute-start.18) | collective-permute-done | bytes 524320 | tf_op jit(solution)/shard_map/ppermute | solution.py:34
  186.3 4.8 %adapter_gradients.1 = (f32[64,768]{1,0:T(8,128)}, f32[64,2048]{1,0:T(8,128)}) custom-call(s32[6]{0:T(128)S(1)} %pad_add_fusion.place_ref.place, bf16[4,80,2048]{2,1,0:T(8,128)(2,1)S(1)} %copy-done.3, bf16[320,768]{1,0:T(8,128)(2,1)S(1)} %copy-done.11, bf16[320,64]{1,0:T(8,128)(2,1)S(1)} %copy-done.14, ...), custom_call_target="tpu_custom_call" | custom-call | bytes 6000000 | tf_op jit(solution)/shard_map/adapter_gradients/pallas_call | solution.py:63
  191.2 8.1 %collective-permute-done.19.refs_2_ = bf16[128,2048]{1,0:T(8,128)(2,1)S(1)} collective-permute-done((bf16[128,2048]{1,0:T(8,128)(2,1)S(1)}, bf16[128,2048]{1,0:T(8,128)(2,1)S(1)}, u32[]{:S(2)}, u32[]{:S(2)}) %collective-permute-start.19) | collective-permute-done | bytes 524320 | tf_op jit(solution)/shard_map/ppermute | solution.py:34
  208.0 9.1 %collective-permute-done.22.refs_0_ = bf16[144,2048]{1,0:T(8,128)(2,1)S(1)} collective-permute-done((bf16[144,2048]{1,0:T(8,128)(2,1)S(1)}, bf16[144,2048]{1,0:T(8,128)(2,1)S(1)}, u32[]{:S(2)}, u32[]{:S(2)}) %collective-permute-start.22) | collective-permute-done | bytes 589856 | tf_op jit(solution)/shard_map/ppermute | solution.py:29
  217.0 13.7 %collective-permute-done.23.refs_1_ = bf16[144,2048]{1,0:T(8,128)(2,1)S(1)} collective-permute-done((bf16[144,2048]{1,0:T(8,128)(2,1)S(1)}, bf16[144,2048]{1,0:T(8,128)(2,1)S(1)}, u32[]{:S(2)}, u32[]{:S(2)}) %collective-permute-start.23) | collective-permute-done | bytes 589856 | tf_op jit(solution)/shard_map/ppermute | solution.py:29
  234.4 6.4 %head_gradients.3 = (bf16[256,512]{1,0:T(8,128)(2,1)S(1)}, bf16[256,512]{1,0:T(8,128)(2,1)S(1)}, bf16[256,512]{1,0:T(8,128)(2,1)S(1)}, f32[64,512]{1,0:T(8,128)S(1)}, f32[64,512]{1,0:T(8,128)S(1)}) custom-call(s32[6]{0:T(128)S(1)} %pad_add_fusion.place_ref.place, bf16[144,2048]{1,0:T(8,128)(2,1)S(1)} %collective-permute-done.22.refs_0_, ...), custom_call_target="tpu_custom_call" | custom-call | bytes 9100000 | tf_op jit(solution)/shard_map/head_gradients/pallas_call | solution.py:63
  244.1 11.1 %attention_backward.1 = (f32[1024,512]{1,0:T(8,128)}, f32[4,128,256]{2,1,0:T(8,128)S(1)}, bf16[4,128,256]{2,1,0:T(8,128)(2,1)S(1)}) custom-call(s32[6]{0:T(128)S(1)} %pad_add_fusion.place_ref.place, bf16[1024,512]{1,0:T(8,128)(2,1)} %q_ref.5, bf16[1024,512]{1,0:T(8,128)(2,1)} %k_ref.5, bf16[1024,512]{1,0:T(8,128)(2,1)} %v_ref.5, ...), custom_call_target="tpu_custom_call" | custom-call | bytes 11800000 | tf_op jit(solution)/shard_map/attention_backward/pallas_call | solution.py:617
  (194 shorter events, 80.2 us)
Async XLA Ops:
  3.3 29.3 %collective-permute-start.2 = (bf16[128,2048]{1,0:T(8,128)(2,1)}, bf16[128,2048]{1,0:T(8,128)(2,1)}, u32[]{:S(2)}, u32[]{:S(2)}) collective-permute-start(bf16[128,2048]{1,0:T(8,128)(2,1)} %refs_0_.1), channel_id=1, source_target_pairs={{0,8},{8,16},{16,24},{24,0},{1,9},{9,17},{17,25},{25,1},{2,10},{10... | collective-permute-start | bytes 1572872 | tf_op jit(solution)/shard_map/ppermute | solution.py:34
  6.2 26.4 %collective-permute-start.3 = (bf16[128,2048]{1,0:T(8,128)(2,1)}, bf16[128,2048]{1,0:T(8,128)(2,1)}, u32[]{:S(2)}, u32[]{:S(2)}) collective-permute-start(bf16[128,2048]{1,0:T(8,128)(2,1)} %refs_0_.1), channel_id=1, source_target_pairs={{0,24},{8,0},{16,8},{24,16},{1,25},{9,1},{17,9},{25,17},{2,26},{10... | collective-permute-start | bytes 1572872 | tf_op jit(solution)/shard_map/ppermute | solution.py:34
  8.3 24.3 %collective-permute-start.4 = (f32[2,16,128]{2,1,0:T(8,128)S(1)}, f32[2,16,128]{2,1,0:T(8,128)S(1)}, u32[]{:S(2)}, u32[]{:S(2)}) collective-permute-start(f32[2,16,128]{2,1,0:T(8,128)S(1)} %pad_maximum_fusion.7), channel_id=1, source_target_pairs={{0,8},{8,16},{16,24},{24,0},{1,9},{9,17},{17,25},{25,1},{2,10},{10... | collective-permute-start | bytes 49160 | tf_op jit(solution)/shard_map/ppermute | solution.py:34
  8.3 24.3 %collective-permute-start.5 = (f32[2,16,128]{2,1,0:T(8,128)S(1)}, f32[2,16,128]{2,1,0:T(8,128)S(1)}, u32[]{:S(2)}, u32[]{:S(2)}) collective-permute-start(f32[2,16,128]{2,1,0:T(8,128)S(1)} %pad_maximum_fusion.7), channel_id=1, source_target_pairs={{0,24},{8,0},{16,8},{24,16},{1,25},{9,1},{17,9},{25,17},{2,26},{10... | collective-permute-start | bytes 49160 | tf_op jit(solution)/shard_map/ppermute | solution.py:34
  15.7 24.1 %all-to-all-start = ((bf16[4,80,2048]{2,1,0:T(8,128)(2,1)}), bf16[4,80,2048]{2,1,0:T(8,128)(2,1)S(1)}, u32[]{:S(2)}, u32[]{:S(2)}) async-start(bf16[4,80,2048]{2,1,0:T(8,128)(2,1)} %dispatch.3.refs_0_), calls=%async_computation | async-start | bytes 2621440 | tf_op jit(solution)/shard_map/all_to_all | solution.py:749
  33.7 34.3 %collective-permute-start.8 = (bf16[128,2048]{1,0:T(8,128)(2,1)S(1)}, bf16[128,2048]{1,0:T(8,128)(2,1)}, u32[]{:S(2)}, u32[]{:S(2)}) collective-permute-start(bf16[128,2048]{1,0:T(8,128)(2,1)S(1)} %copy-done.6), channel_id=1, source_target_pairs={{0,16},{8,24},{16,0},{24,8},{1,17},{9,25},{17,1},{25,9},{2,18},{10... | collective-permute-start | bytes 1572872 | tf_op jit(solution)/shard_map/ppermute | solution.py:34
  40.9 35.2 %all-to-all-start.1 = ((bf16[4,160,2048]{2,1,0:T(8,128)(2,1)}), bf16[4,160,2048]{2,1,0:T(8,128)(2,1)S(1)}, u32[]{:S(2)}, u32[]{:S(2)}) async-start(bf16[4,160,2048]{2,1,0:T(8,128)(2,1)} %dispatch.4.refs_8_), calls=%async_computation.1 | async-start | bytes 5242880 | tf_op jit(solution)/shard_map/all_to_all | solution.py:749
  45.2 22.8 %collective-permute-start.9 = (f32[2,16,128]{2,1,0:T(8,128)S(1)}, f32[2,16,128]{2,1,0:T(8,128)S(1)}, u32[]{:S(2)}, u32[]{:S(2)}) collective-permute-start(f32[2,16,128]{2,1,0:T(8,128)S(1)} %pad_maximum_fusion.7), channel_id=1, source_target_pairs={{0,16},{8,24},{16,0},{24,8},{1,17},{9,25},{17,1},{25,9},{2,18},{10... | collective-permute-start | bytes 49160 | tf_op jit(solution)/shard_map/ppermute | solution.py:34
  76.1 22.8 %all-to-all-start.2 = ((bf16[4,88,2048]{2,1,0:T(8,128)(2,1)}), bf16[4,88,2048]{2,1,0:T(8,128)(2,1)}, u32[]{:S(2)}, u32[]{:S(2)}) async-start(bf16[4,88,2048]{2,1,0:T(8,128)(2,1)} %dispatch.5.refs_10_), calls=%async_computation.2 | async-start | bytes 2883584 | tf_op jit(solution)/shard_map/all_to_all | solution.py:749
  95.2 18.6 %collective-permute-start.11 = (bf16[160,2048]{1,0:T(8,128)(2,1)}, bf16[160,2048]{1,0:T(8,128)(2,1)}, u32[]{:S(2)}, u32[]{:S(2)}) collective-permute-start(bf16[160,2048]{1,0:T(8,128)(2,1)} %get-tuple-element.93), channel_id=1, source_target_pairs={{0,2},{1,3},{2,0},{3,1},{4,6},{5,7},{6,4},{7,5},{8,10},{9,11},{10,... | collective-permute-start | bytes 1966088 | tf_op jit(solution)/shard_map/ppermute | solution.py:29
  97.3 35.7 %collective-permute-start.12 = (bf16[160,2048]{1,0:T(8,128)(2,1)}, bf16[160,2048]{1,0:T(8,128)(2,1)}, u32[]{:S(2)}, u32[]{:S(2)}) collective-permute-start(bf16[160,2048]{1,0:T(8,128)(2,1)} %get-tuple-element.94), channel_id=1, source_target_pairs={{0,4},{1,5},{2,6},{3,7},{4,0},{5,1},{6,2},{7,3},{8,12},{9,13},{10,... | collective-permute-start | bytes 1966088 | tf_op jit(solution)/shard_map/ppermute | solution.py:29
  98.7 34.2 %collective-permute-start.13 = (bf16[160,2048]{1,0:T(8,128)(2,1)}, bf16[160,2048]{1,0:T(8,128)(2,1)}, u32[]{:S(2)}, u32[]{:S(2)}) collective-permute-start(bf16[160,2048]{1,0:T(8,128)(2,1)} %get-tuple-element.95), channel_id=1, source_target_pairs={{0,6},{1,7},{2,4},{3,5},{4,2},{5,3},{6,0},{7,1},{8,14},{9,15},{10,... | collective-permute-start | bytes 1966088 | tf_op jit(solution)/shard_map/ppermute | solution.py:29
  109.1 32.1 %all-to-all-start.3 = ((bf16[4,80,2048]{2,1,0:T(8,128)(2,1)}), bf16[4,80,2048]{2,1,0:T(8,128)(2,1)}, u32[]{:S(2)}, u32[]{:S(2)}) async-start(bf16[4,80,2048]{2,1,0:T(8,128)(2,1)} %get-tuple-element.91.refs_6_), calls=%async_computation.3 | async-start | bytes 2621440 | tf_op jit(solution)/shard_map/all_to_all | solution.py:749
  137.4 12.3 %collective-permute-start.14 = (bf16[128,2048]{1,0:T(8,128)(2,1)}, bf16[128,2048]{1,0:T(8,128)(2,1)S(1)}, u32[]{:S(2)}, u32[]{:S(2)}) collective-permute-start(bf16[128,2048]{1,0:T(8,128)(2,1)} %get-tuple-element.97), channel_id=1, source_target_pairs={{0,1},{1,0},{2,3},{3,2},{4,5},{5,4},{6,7},{7,6},{8,9},{9,8},{10,11... | collective-permute-start | bytes 1572872 | tf_op jit(solution)/shard_map/ppermute | solution.py:29
  144.9 22.9 %collective-permute-start.16 = (bf16[128,2048]{1,0:T(8,128)(2,1)}, bf16[128,2048]{1,0:T(8,128)(2,1)}, u32[]{:S(2)}, u32[]{:S(2)}) collective-permute-start(bf16[128,2048]{1,0:T(8,128)(2,1)} %get-tuple-element.99.refs_2_), channel_id=1, source_target_pairs={{0,1},{1,0},{2,3},{3,2},{4,5},{5,4},{6,7},{7,6},{8,9},{9,8},{10,11... | collective-permute-start | bytes 1572872 | tf_op jit(solution)/shard_map/ppermute | solution.py:29
  145.4 22.4 %all-to-all-start.4 = ((bf16[4,80,2048]{2,1,0:T(8,128)(2,1)}), bf16[4,80,2048]{2,1,0:T(8,128)(2,1)}, u32[]{:S(2)}, u32[]{:S(2)}) async-start(bf16[4,80,2048]{2,1,0:T(8,128)(2,1)} %get-tuple-element.92.refs_2_), calls=%async_computation.4 | async-start | bytes 2621440 | tf_op jit(solution)/shard_map/all_to_all | solution.py:749
  151.2 16.7 %collective-permute-start.15 = (bf16[128,2048]{1,0:T(8,128)(2,1)S(1)}, bf16[128,2048]{1,0:T(8,128)(2,1)S(1)}, u32[]{:S(2)}, u32[]{:S(2)}) collective-permute-start(bf16[128,2048]{1,0:T(8,128)(2,1)S(1)} %add_convert_fusion.2), channel_id=1, source_target_pairs={{0,8},{8,16},{16,24},{24,0},{1,9},{9,17},{17,25},{25,1},{2,10},{10... | collective-permute-start | bytes 1572872 | tf_op jit(solution)/shard_map/ppermute | solution.py:34
  153.7 24.5 %collective-permute-start.18 = (bf16[128,2048]{1,0:T(8,128)(2,1)}, bf16[128,2048]{1,0:T(8,128)(2,1)}, u32[]{:S(2)}, u32[]{:S(2)}) collective-permute-start(bf16[128,2048]{1,0:T(8,128)(2,1)} %add_convert_fusion.1), channel_id=1, source_target_pairs={{0,24},{8,0},{16,8},{24,16},{1,25},{9,1},{17,9},{25,17},{2,26},{10... | collective-permute-start | bytes 1572872 | tf_op jit(solution)/shard_map/ppermute | solution.py:34
  185.3 13.9 %collective-permute-start.19 = (bf16[128,2048]{1,0:T(8,128)(2,1)S(1)}, bf16[128,2048]{1,0:T(8,128)(2,1)S(1)}, u32[]{:S(2)}, u32[]{:S(2)}) collective-permute-start(bf16[128,2048]{1,0:T(8,128)(2,1)S(1)} %add_convert_fusion), channel_id=1, source_target_pairs={{0,24},{8,0},{16,8},{24,16},{1,25},{9,1},{17,9},{25,17},{2,26},{10... | collective-permute-start | bytes 1572872 | tf_op jit(solution)/shard_map/ppermute | solution.py:34
  200.9 16.1 %collective-permute-start.22 = (bf16[144,2048]{1,0:T(8,128)(2,1)S(1)}, bf16[144,2048]{1,0:T(8,128)(2,1)S(1)}, u32[]{:S(2)}, u32[]{:S(2)}) collective-permute-start(bf16[144,2048]{1,0:T(8,128)(2,1)S(1)} %get-tuple-element.110), channel_id=1, source_target_pairs={{0,2},{1,3},{2,0},{3,1},{4,6},{5,7},{6,4},{7,5},{8,10},{9,11},{10,... | collective-permute-start | bytes 1769480 | tf_op jit(solution)/shard_map/ppermute | solution.py:29
  202.6 28.1 %collective-permute-start.23 = (bf16[144,2048]{1,0:T(8,128)(2,1)S(1)}, bf16[144,2048]{1,0:T(8,128)(2,1)S(1)}, u32[]{:S(2)}, u32[]{:S(2)}) collective-permute-start(bf16[144,2048]{1,0:T(8,128)(2,1)S(1)} %get-tuple-element.111), channel_id=1, source_target_pairs={{0,4},{1,5},{2,6},{3,7},{4,0},{5,1},{6,2},{7,3},{8,12},{9,13},{10,... | collective-permute-start | bytes 1769480 | tf_op jit(solution)/shard_map/ppermute | solution.py:29
  204.0 26.6 %collective-permute-start.24 = (bf16[144,2048]{1,0:T(8,128)(2,1)S(1)}, bf16[144,2048]{1,0:T(8,128)(2,1)S(1)}, u32[]{:S(2)}, u32[]{:S(2)}) collective-permute-start(bf16[144,2048]{1,0:T(8,128)(2,1)S(1)} %get-tuple-element.112), channel_id=1, source_target_pairs={{0,6},{1,7},{2,4},{3,5},{4,2},{5,3},{6,0},{7,1},{8,14},{9,15},{10,... | collective-permute-start | bytes 1769480 | tf_op jit(solution)/shard_map/ppermute | solution.py:29
  240.9 14.3 %collective-permute-start.29 = (bf16[128,512]{1,0:T(8,128)(2,1)S(1)}, bf16[128,512]{1,0:T(8,128)(2,1)S(1)}, u32[]{:S(2)}, u32[]{:S(2)}) collective-permute-start(bf16[128,512]{1,0:T(8,128)(2,1)S(1)} %pad_maximum_fusion.6), channel_id=1, source_target_pairs={{0,24},{8,0},{16,8},{24,16},{1,25},{9,1},{17,9},{25,17},{2,26},{10... | collective-permute-start | bytes 393224 | tf_op jit(solution)/shard_map/ppermute | solution.py:34
  243.2 12.0 %collective-permute-start.31 = (bf16[128,512]{1,0:T(8,128)(2,1)S(1)}, bf16[128,512]{1,0:T(8,128)(2,1)S(1)}, u32[]{:S(2)}, u32[]{:S(2)}) collective-permute-start(bf16[128,512]{1,0:T(8,128)(2,1)S(1)} %pad_maximum_fusion.6), channel_id=1, source_target_pairs={{0,8},{8,16},{16,24},{24,0},{1,9},{9,17},{17,25},{25,1},{2,10},{10... | collective-permute-start | bytes 393224 | tf_op jit(solution)/shard_map/ppermute | solution.py:34
  (35 other events, 219.3 us)

commit v5 on v4

--- a/solution.py
+++ b/solution.py
@@ -872,11 +872,13 @@
     if len(groups) > 2:
         back[0], sums = lax.optimization_barrier((back[0], sums))
         sums += sent_home(groups[2], combined(groups[2], back[2]), {2: 1} if relayed else {})
+    own_sum = combined(groups[0], back[0])[0]
     if relayed:
+        waiting, _ = lax.optimization_barrier((waiting, last))
         passed = (waiting + sums.pop().astype(jnp.float32)).astype(jnp.bfloat16)
         sums.append(shift(passed, -1))
         last[:] = lax.optimization_barrier((last, passed))[0]
-    sums.append(combined(groups[0], back[0])[0])
+    sums.append(own_sum)
     grad_first, grad_second = adapter_gradients(
         place, [finished[k][1] for k in finished], down_first_factor[0], cells, pairs, last
     )

time: 275 us -> 270 us (0.982)
  waiting for transfers between devices: 95.5 us -> 87.9 us
    ppermute x12, waiting for transfers between devices: 33.8 us -> 26.7 us  [shift(): lax.ppermute(value, 'grp', [(i, (i + step) % count) for i in range(count)])]
  transfers between devices with their start and end apart: 41 -> 41, of which waited for: 22 -> 20; matrix products, arithmetic and copies ran while one was open for 2% -> 4% of each run, Pallas kernels for 33% -> 36%
where the time goes in v5:
time: 270 us; the launch traced here: 265 us
  Pallas kernels  102 us (38%)
  waiting for transfers between devices  87.9 us (33%)
  starting transfers between devices  52.9 us (20%)
  other arithmetic  14.2 us (5%)
  local copies, waits for them, and re-layouts  5.62 us (2%)
    pallas_call x13, Pallas kernels, kernel_call(): pl.pallas_call(kernel, grid_spec=pltpu.PrefetchScalarGridSpec(num_scalar_...  74.6 us
    ppermute x24, waiting for transfers between devices, across(): return lax.ppermute(value, 'dev', [(i, i ^ step) for i in range(count)])  54.8 us
    ppermute x12, waiting for transfers between devices, shift(): lax.ppermute(value, 'grp', [(i, (i + step) % count) for i in range(count)])  26.7 us
    all_to_all x5, starting transfers between devices, exchanged(): lax.all_to_all(parts[0], 'dev', 0, 0, axis_index_groups=chips, tiled=True)  21.7 us
    ppermute x12, starting transfers between devices, shift(): lax.ppermute(value, 'grp', [(i, (i + step) % count) for i in range(count)])  18.3 us
    pallas_call x2, Pallas kernels, attention_forward(): pl.pallas_call(forward_kernel, grid_spec=pltpu.PrefetchScalarGridSpec(num...  16.7 us
    ppermute x24, starting transfers between devices, across(): return lax.ppermute(value, 'dev', [(i, i ^ step) for i in range(count)])  12.9 us
    pallas_call x1, Pallas kernels, attention_backward(): pl.pallas_call(backward_kernel, grid_spec=pltpu.PrefetchScalarGridSpec(nu...  11.1 us
  transfers between devices with their start and end apart: 41, of which 20 were waited for; matrix products, arithmetic and copies ran while one was open for 4% of the time, Pallas kernels for 36%

profile of v5, /device:TPU:0, one launch (start us, length us, event | category | flops | bytes accessed | tf_op | source)
XLA Modules:
  0.0 265.0 jit_solution(16243176055153364726)
XLA Ops:
  15.7 4.0 %all-to-all-start = ((bf16[4,80,2048]{2,1,0:T(8,128)(2,1)}), bf16[4,80,2048]{2,1,0:T(8,128)(2,1)S(1)}, u32[]{:S(2)}, u32[]{:S(2)}) async-start(bf16[4,80,2048]{2,1,0:T(8,128)(2,1)} %dispatch.3.refs_0_), calls=%async_computation | async-start | bytes 2621440 | tf_op jit(solution)/shard_map/all_to_all | solution.py:749
  19.7 8.3 %attention_forward.2 = (bf16[4,1024,1024]{2,1,0:T(8,128)(2,1)}, bf16[1024,512]{1,0:T(8,128)(2,1)}, f32[8,64,128]{2,1,0:T(8,128)}) custom-call(s32[6]{0:T(128)S(1)} %pad_add_fusion.place_ref.place, bf16[1024,512]{1,0:T(8,128)(2,1)} %q_ref.5, bf16[1024,512]{1,0:T(8,128)(2,1)} %k_ref.5, bf16[1024,512]{1,0:T(8,128)(2,1)} %v_ref.5, bf16[64,512]{1,0:T(8,128)(2,1)} %refs_7_.1, ...), custom_call_target="tpu_custom_call" | custom-call | bytes 8800000 | tf_op jit(solution)/shard_map/attention_forward/pallas_call | solution.py:532
  28.1 4.5 %collective-permute-done.4 = f32[2,16,128]{2,1,0:T(8,128)S(1)} collective-permute-done((f32[2,16,128]{2,1,0:T(8,128)S(1)}, f32[2,16,128]{2,1,0:T(8,128)S(1)}, u32[]{:S(2)}, u32[]{:S(2)}) %collective-permute-start.4) | collective-permute-done | bytes 16416 | tf_op jit(solution)/shard_map/ppermute | solution.py:34
  35.6 4.3 %dispatch.4.refs_8_ = bf16[4,160,2048]{2,1,0:T(8,128)(2,1)} custom-call(s32[6]{0:T(128)S(1)} %pad_add_fusion.place_ref.place, bf16[128,2048]{1,0:T(8,128)(2,1)S(1)} %collective-permute-done.6.refs_0_, bf16[128,2048]{1,0:T(8,128)(2,1)S(1)} %collective-permute-done.7.refs_1_, bf16[128,2048]{1,0:T(8,128)(2,1)} %collective-permute-done.2.refs_2_, ...), custom_call_target="tpu_custom_call" | custom-call | bytes 3500000 | tf_op jit(solution)/shard_map/dispatch/pallas_call | solution.py:63
  40.9 4.2 %all-to-all-start.1 = ((bf16[4,160,2048]{2,1,0:T(8,128)(2,1)}), bf16[4,160,2048]{2,1,0:T(8,128)(2,1)S(1)}, u32[]{:S(2)}, u32[]{:S(2)}) async-start(bf16[4,160,2048]{2,1,0:T(8,128)(2,1)} %dispatch.4.refs_8_), calls=%async_computation.1 | async-start | bytes 5242880 | tf_op jit(solution)/shard_map/all_to_all | solution.py:749
  47.8 10.4 %expert.3 = (bf16[4,80,2048]{2,1,0:T(8,128)(2,1)}, bf16[320,768]{1,0:T(8,128)(2,1)}, bf16[320,64]{1,0:T(8,128)(2,1)}) custom-call(s32[6]{0:T(128)S(1)} %pad_add_fusion.place_ref.place, bf16[4,80,2048]{2,1,0:T(8,128)(2,1)S(1)} %copy-done.2, bf16[320,320]{1,0:T(8,128)(2,1)S(1)} %fusion.4.refs_1_, bf16[1280,1536]{1,0:T(8,128)(2,1)} %bitcast.123, ...), custom_call_target="tpu_custom_call" | custom-call | bytes 12500000 | tf_op jit(solution)/shard_map/expert/pallas_call | solution.py:63
  59.6 8.3 %attention_forward.3 = (bf16[4,1024,1024]{2,1,0:T(8,128)(2,1)}, bf16[1024,512]{1,0:T(8,128)(2,1)}, f32[8,64,128]{2,1,0:T(8,128)}) custom-call(s32[6]{0:T(128)S(1)} %pad_add_fusion.place_ref.place, bf16[1024,512]{1,0:T(8,128)(2,1)} %q_ref.5, bf16[1024,512]{1,0:T(8,128)(2,1)} %k_ref.5, ...), custom_call_target="tpu_custom_call", output_to_operand_aliasing={{0}: (5, {}), {1}: (6, {})} | custom-call | bytes 8800000 | tf_op jit(solution)/shard_map/attention_forward/pallas_call | solution.py:532
  76.1 4.5 %all-to-all-start.2 = ((bf16[4,88,2048]{2,1,0:T(8,128)(2,1)}), bf16[4,88,2048]{2,1,0:T(8,128)(2,1)}, u32[]{:S(2)}, u32[]{:S(2)}) async-start(bf16[4,88,2048]{2,1,0:T(8,128)(2,1)} %dispatch.5.refs_10_), calls=%async_computation.2 | async-start | bytes 2883584 | tf_op jit(solution)/shard_map/all_to_all | solution.py:749
  80.6 14.6 %expert.4 = (bf16[160,2048]{1,0:T(8,128)(2,1)}, bf16[160,2048]{1,0:T(8,128)(2,1)}, bf16[160,2048]{1,0:T(8,128)(2,1)}, bf16[160,2048]{1,0:T(8,128)(2,1)}, bf16[64...) custom-call(s32[6]{0:T(128)S(1)} %pad_add_fusion.place_ref.place, bf16[4,160,2048]{2,1,0:T(8,128)(2,1)S(1)} %all-to-all-done.1.refs_0_.refs_3_, ...), custom_call_target="tpu_custom_call" | custom-call | bytes 17000000 | tf_op jit(solution)/shard_map/expert/pallas_call | solution.py:63
  98.8 10.3 %expert.5 = (bf16[4,80,2048]{2,1,0:T(8,128)(2,1)}, bf16[320,768]{1,0:T(8,128)(2,1)}, bf16[320,64]{1,0:T(8,128)(2,1)}) custom-call(s32[6]{0:T(128)S(1)} %pad_add_fusion.place_ref.place, bf16[4,88,2048]{2,1,0:T(8,128)(2,1)} %all-to-all-done.2.refs_0_.refs_6_, bf16[320,320]{1,0:T(8,128)(2,1)S(1)} %fusion.4.refs_1_, bf16[1280,1536]{1,0:T(8,128)(2,1)} %bitcast.129, ...), custom_call_target="tpu_custom_call" | custom-call | bytes 12500000 | tf_op jit(solution)/shard_map/expert/pallas_call | solution.py:63
  109.1 4.7 %all-to-all-start.3 = ((bf16[4,80,2048]{2,1,0:T(8,128)(2,1)}), bf16[4,80,2048]{2,1,0:T(8,128)(2,1)}, u32[]{:S(2)}, u32[]{:S(2)}) async-start(bf16[4,80,2048]{2,1,0:T(8,128)(2,1)} %get-tuple-element.92.refs_6_), calls=%async_computation.3 | async-start | bytes 2621440 | tf_op jit(solution)/shard_map/all_to_all | solution.py:749
  113.8 19.1 %collective-permute-done.12.refs_2_ = bf16[160,2048]{1,0:T(8,128)(2,1)} collective-permute-done((bf16[160,2048]{1,0:T(8,128)(2,1)}, bf16[160,2048]{1,0:T(8,128)(2,1)}, u32[]{:S(2)}, u32[]{:S(2)}) %collective-permute-start.12) | collective-permute-done | bytes 655392 | tf_op jit(solution)/shard_map/ppermute | solution.py:29
  132.9 4.4 %combine.3 = (f32[128,2048]{1,0:T(8,128)}, bf16[128,2048]{1,0:T(8,128)(2,1)}, f32[128,2048]{1,0:T(8,128)}, bf16[128,2048]{1,0:T(8,128)(2,1)}) custom-call(s32[6]{0:T(128)S(1)} %pad_add_fusion.place_ref.place, bf16[160,2048]{1,0:T(8,128)(2,1)S(1)} %copy-done.5, bf16[160,2048]{1,0:T(8,128)(2,1)} %collective-permute-done.11.refs_1_, ...), custom_call_target="tpu_custom_call" | custom-call | bytes 4500000 | tf_op jit(solution)/shard_map/combine/pallas_call | solution.py:63
  137.4 3.8 %all-to-all-done.3.refs_0_ = bf16[4,80,2048]{2,1,0:T(8,128)(2,1)} async-done(((bf16[4,80,2048]{2,1,0:T(8,128)(2,1)}), bf16[4,80,2048]{2,1,0:T(8,128)(2,1)}, u32[]{:S(2)}, u32[]{:S(2)}) %all-to-all-start.3) | async-done | bytes 1310752 | tf_op jit(solution)/shard_map/all_to_all | solution.py:749
  146.4 4.3 %all-to-all-start.4 = ((bf16[4,80,2048]{2,1,0:T(8,128)(2,1)}), bf16[4,80,2048]{2,1,0:T(8,128)(2,1)}, u32[]{:S(2)}, u32[]{:S(2)}) async-start(bf16[4,80,2048]{2,1,0:T(8,128)(2,1)} %get-tuple-element.93.refs_2_), calls=%async_computation.4 | async-start | bytes 2621440 | tf_op jit(solution)/shard_map/all_to_all | solution.py:749
  160.8 8.1 %collective-permute-done.15.refs_1_ = bf16[128,2048]{1,0:T(8,128)(2,1)S(1)} collective-permute-done((bf16[128,2048]{1,0:T(8,128)(2,1)S(1)}, bf16[128,2048]{1,0:T(8,128)(2,1)S(1)}, u32[]{:S(2)}, u32[]{:S(2)}) %collective-permute-start.15) | collective-permute-done | bytes 524320 | tf_op jit(solution)/shard_map/ppermute | solution.py:34
  168.9 4.0 %combine.5 = (f32[128,2048]{1,0:T(8,128)}, bf16[128,2048]{1,0:T(8,128)(2,1)}) custom-call(s32[6]{0:T(128)S(1)} %pad_add_fusion.place_ref.place, bf16[4,80,2048]{2,1,0:T(8,128)(2,1)} %all-to-all-done.4.refs_0_, f32[2,4,256]{2,1,0:T(4,128)S(1)} %pad_maximum_fusion.9.refs_2_.refs_1_, bf16[128,2048]{1,0:T(8,128)(2,1)} %get-tuple-element.101.refs_2_), custom_call_target="tpu_custom_call" | custom-call | bytes 4500000 | tf_op jit(solution)/shard_map/combine/pallas_call | solution.py:63
  172.9 6.4 %collective-permute-done.18 = bf16[128,2048]{1,0:T(8,128)(2,1)} collective-permute-done((bf16[128,2048]{1,0:T(8,128)(2,1)}, bf16[128,2048]{1,0:T(8,128)(2,1)}, u32[]{:S(2)}, u32[]{:S(2)}) %collective-permute-start.18) | collective-permute-done | bytes 524320 | tf_op jit(solution)/shard_map/ppermute | solution.py:34
  182.1 4.8 %adapter_gradients.1 = (f32[64,768]{1,0:T(8,128)}, f32[64,2048]{1,0:T(8,128)}) custom-call(s32[6]{0:T(128)S(1)} %pad_add_fusion.place_ref.place, bf16[4,80,2048]{2,1,0:T(8,128)(2,1)S(1)} %copy-done.3, bf16[320,768]{1,0:T(8,128)(2,1)S(1)} %copy-done.11, bf16[320,64]{1,0:T(8,128)(2,1)S(1)} %copy-done.14, ...), custom_call_target="tpu_custom_call" | custom-call | bytes 6000000 | tf_op jit(solution)/shard_map/adapter_gradients/pallas_call | solution.py:63
  187.0 7.6 %collective-permute-done.19.refs_2_ = bf16[128,2048]{1,0:T(8,128)(2,1)S(1)} collective-permute-done((bf16[128,2048]{1,0:T(8,128)(2,1)S(1)}, bf16[128,2048]{1,0:T(8,128)(2,1)S(1)}, u32[]{:S(2)}, u32[]{:S(2)}) %collective-permute-start.19) | collective-permute-done | bytes 524320 | tf_op jit(solution)/shard_map/ppermute | solution.py:34
  203.3 9.1 %collective-permute-done.22.refs_0_ = bf16[144,2048]{1,0:T(8,128)(2,1)S(1)} collective-permute-done((bf16[144,2048]{1,0:T(8,128)(2,1)S(1)}, bf16[144,2048]{1,0:T(8,128)(2,1)S(1)}, u32[]{:S(2)}, u32[]{:S(2)}) %collective-permute-start.22) | collective-permute-done | bytes 589856 | tf_op jit(solution)/shard_map/ppermute | solution.py:29
  212.4 13.6 %collective-permute-done.23.refs_1_ = bf16[144,2048]{1,0:T(8,128)(2,1)S(1)} collective-permute-done((bf16[144,2048]{1,0:T(8,128)(2,1)S(1)}, bf16[144,2048]{1,0:T(8,128)(2,1)S(1)}, u32[]{:S(2)}, u32[]{:S(2)}) %collective-permute-start.23) | collective-permute-done | bytes 589856 | tf_op jit(solution)/shard_map/ppermute | solution.py:29
  229.7 6.4 %head_gradients.3 = (bf16[256,512]{1,0:T(8,128)(2,1)S(1)}, bf16[256,512]{1,0:T(8,128)(2,1)S(1)}, bf16[256,512]{1,0:T(8,128)(2,1)S(1)}, f32[64,512]{1,0:T(8,128)S(1)}, f32[64,512]{1,0:T(8,128)S(1)}) custom-call(s32[6]{0:T(128)S(1)} %pad_add_fusion.place_ref.place, bf16[144,2048]{1,0:T(8,128)(2,1)S(1)} %collective-permute-done.22.refs_0_, ...), custom_call_target="tpu_custom_call" | custom-call | bytes 9100000 | tf_op jit(solution)/shard_map/head_gradients/pallas_call | solution.py:63
  239.2 11.1 %attention_backward.1 = (f32[1024,512]{1,0:T(8,128)}, f32[4,128,256]{2,1,0:T(8,128)S(1)}, bf16[4,128,256]{2,1,0:T(8,128)(2,1)S(1)}) custom-call(s32[6]{0:T(128)S(1)} %pad_add_fusion.place_ref.place, bf16[1024,512]{1,0:T(8,128)(2,1)} %q_ref.5, bf16[1024,512]{1,0:T(8,128)(2,1)} %k_ref.5, bf16[1024,512]{1,0:T(8,128)(2,1)} %v_ref.5, ...), custom_call_target="tpu_custom_call" | custom-call | bytes 11800000 | tf_op jit(solution)/shard_map/attention_backward/pallas_call | solution.py:617
  (197 shorter events, 82.4 us)
Async XLA Ops:
  3.3 29.3 %collective-permute-start.2 = (bf16[128,2048]{1,0:T(8,128)(2,1)}, bf16[128,2048]{1,0:T(8,128)(2,1)}, u32[]{:S(2)}, u32[]{:S(2)}) collective-permute-start(bf16[128,2048]{1,0:T(8,128)(2,1)} %refs_0_.1), channel_id=1, source_target_pairs={{0,8},{8,16},{16,24},{24,0},{1,9},{9,17},{17,25},{25,1},{2,10},{10... | collective-permute-start | bytes 1572872 | tf_op jit(solution)/shard_map/ppermute | solution.py:34
  6.2 26.4 %collective-permute-start.3 = (bf16[128,2048]{1,0:T(8,128)(2,1)}, bf16[128,2048]{1,0:T(8,128)(2,1)}, u32[]{:S(2)}, u32[]{:S(2)}) collective-permute-start(bf16[128,2048]{1,0:T(8,128)(2,1)} %refs_0_.1), channel_id=1, source_target_pairs={{0,24},{8,0},{16,8},{24,16},{1,25},{9,1},{17,9},{25,17},{2,26},{10... | collective-permute-start | bytes 1572872 | tf_op jit(solution)/shard_map/ppermute | solution.py:34
  8.3 24.3 %collective-permute-start.4 = (f32[2,16,128]{2,1,0:T(8,128)S(1)}, f32[2,16,128]{2,1,0:T(8,128)S(1)}, u32[]{:S(2)}, u32[]{:S(2)}) collective-permute-start(f32[2,16,128]{2,1,0:T(8,128)S(1)} %pad_maximum_fusion.7), channel_id=1, source_target_pairs={{0,8},{8,16},{16,24},{24,0},{1,9},{9,17},{17,25},{25,1},{2,10},{10... | collective-permute-start | bytes 49160 | tf_op jit(solution)/shard_map/ppermute | solution.py:34
  8.3 24.3 %collective-permute-start.5 = (f32[2,16,128]{2,1,0:T(8,128)S(1)}, f32[2,16,128]{2,1,0:T(8,128)S(1)}, u32[]{:S(2)}, u32[]{:S(2)}) collective-permute-start(f32[2,16,128]{2,1,0:T(8,128)S(1)} %pad_maximum_fusion.7), channel_id=1, source_target_pairs={{0,24},{8,0},{16,8},{24,16},{1,25},{9,1},{17,9},{25,17},{2,26},{10... | collective-permute-start | bytes 49160 | tf_op jit(solution)/shard_map/ppermute | solution.py:34
  15.7 24.1 %all-to-all-start = ((bf16[4,80,2048]{2,1,0:T(8,128)(2,1)}), bf16[4,80,2048]{2,1,0:T(8,128)(2,1)S(1)}, u32[]{:S(2)}, u32[]{:S(2)}) async-start(bf16[4,80,2048]{2,1,0:T(8,128)(2,1)} %dispatch.3.refs_0_), calls=%async_computation | async-start | bytes 2621440 | tf_op jit(solution)/shard_map/all_to_all | solution.py:749
  33.7 34.3 %collective-permute-start.8 = (bf16[128,2048]{1,0:T(8,128)(2,1)S(1)}, bf16[128,2048]{1,0:T(8,128)(2,1)}, u32[]{:S(2)}, u32[]{:S(2)}) collective-permute-start(bf16[128,2048]{1,0:T(8,128)(2,1)S(1)} %copy-done.6), channel_id=1, source_target_pairs={{0,16},{8,24},{16,0},{24,8},{1,17},{9,25},{17,1},{25,9},{2,18},{10... | collective-permute-start | bytes 1572872 | tf_op jit(solution)/shard_map/ppermute | solution.py:34
  40.9 35.2 %all-to-all-start.1 = ((bf16[4,160,2048]{2,1,0:T(8,128)(2,1)}), bf16[4,160,2048]{2,1,0:T(8,128)(2,1)S(1)}, u32[]{:S(2)}, u32[]{:S(2)}) async-start(bf16[4,160,2048]{2,1,0:T(8,128)(2,1)} %dispatch.4.refs_8_), calls=%async_computation.1 | async-start | bytes 5242880 | tf_op jit(solution)/shard_map/all_to_all | solution.py:749
  45.1 22.8 %collective-permute-start.9 = (f32[2,16,128]{2,1,0:T(8,128)S(1)}, f32[2,16,128]{2,1,0:T(8,128)S(1)}, u32[]{:S(2)}, u32[]{:S(2)}) collective-permute-start(f32[2,16,128]{2,1,0:T(8,128)S(1)} %pad_maximum_fusion.7), channel_id=1, source_target_pairs={{0,16},{8,24},{16,0},{24,8},{1,17},{9,25},{17,1},{25,9},{2,18},{10... | collective-permute-start | bytes 49160 | tf_op jit(solution)/shard_map/ppermute | solution.py:34
  76.1 22.8 %all-to-all-start.2 = ((bf16[4,88,2048]{2,1,0:T(8,128)(2,1)}), bf16[4,88,2048]{2,1,0:T(8,128)(2,1)}, u32[]{:S(2)}, u32[]{:S(2)}) async-start(bf16[4,88,2048]{2,1,0:T(8,128)(2,1)} %dispatch.5.refs_10_), calls=%async_computation.2 | async-start | bytes 2883584 | tf_op jit(solution)/shard_map/all_to_all | solution.py:749
  95.2 18.6 %collective-permute-start.11 = (bf16[160,2048]{1,0:T(8,128)(2,1)}, bf16[160,2048]{1,0:T(8,128)(2,1)}, u32[]{:S(2)}, u32[]{:S(2)}) collective-permute-start(bf16[160,2048]{1,0:T(8,128)(2,1)} %get-tuple-element.94), channel_id=1, source_target_pairs={{0,2},{1,3},{2,0},{3,1},{4,6},{5,7},{6,4},{7,5},{8,10},{9,11},{10,... | collective-permute-start | bytes 1966088 | tf_op jit(solution)/shard_map/ppermute | solution.py:29
  97.3 35.7 %collective-permute-start.12 = (bf16[160,2048]{1,0:T(8,128)(2,1)}, bf16[160,2048]{1,0:T(8,128)(2,1)}, u32[]{:S(2)}, u32[]{:S(2)}) collective-permute-start(bf16[160,2048]{1,0:T(8,128)(2,1)} %get-tuple-element.95), channel_id=1, source_target_pairs={{0,4},{1,5},{2,6},{3,7},{4,0},{5,1},{6,2},{7,3},{8,12},{9,13},{10,... | collective-permute-start | bytes 1966088 | tf_op jit(solution)/shard_map/ppermute | solution.py:29
  98.7 34.2 %collective-permute-start.13 = (bf16[160,2048]{1,0:T(8,128)(2,1)}, bf16[160,2048]{1,0:T(8,128)(2,1)}, u32[]{:S(2)}, u32[]{:S(2)}) collective-permute-start(bf16[160,2048]{1,0:T(8,128)(2,1)} %get-tuple-element.96), channel_id=1, source_target_pairs={{0,6},{1,7},{2,4},{3,5},{4,2},{5,3},{6,0},{7,1},{8,14},{9,15},{10,... | collective-permute-start | bytes 1966088 | tf_op jit(solution)/shard_map/ppermute | solution.py:29
  109.1 32.1 %all-to-all-start.3 = ((bf16[4,80,2048]{2,1,0:T(8,128)(2,1)}), bf16[4,80,2048]{2,1,0:T(8,128)(2,1)}, u32[]{:S(2)}, u32[]{:S(2)}) async-start(bf16[4,80,2048]{2,1,0:T(8,128)(2,1)} %get-tuple-element.92.refs_6_), calls=%async_computation.3 | async-start | bytes 2621440 | tf_op jit(solution)/shard_map/all_to_all | solution.py:749
  137.4 13.3 %collective-permute-start.14 = (bf16[128,2048]{1,0:T(8,128)(2,1)}, bf16[128,2048]{1,0:T(8,128)(2,1)S(1)}, u32[]{:S(2)}, u32[]{:S(2)}) collective-permute-start(bf16[128,2048]{1,0:T(8,128)(2,1)} %get-tuple-element.98), channel_id=1, source_target_pairs={{0,1},{1,0},{2,3},{3,2},{4,5},{5,4},{6,7},{7,6},{8,9},{9,8},{10,11... | collective-permute-start | bytes 1572872 | tf_op jit(solution)/shard_map/ppermute | solution.py:29
  146.4 22.5 %all-to-all-start.4 = ((bf16[4,80,2048]{2,1,0:T(8,128)(2,1)}), bf16[4,80,2048]{2,1,0:T(8,128)(2,1)}, u32[]{:S(2)}, u32[]{:S(2)}) async-start(bf16[4,80,2048]{2,1,0:T(8,128)(2,1)} %get-tuple-element.93.refs_2_), calls=%async_computation.4 | async-start | bytes 2621440 | tf_op jit(solution)/shard_map/all_to_all | solution.py:749
  152.2 16.7 %collective-permute-start.15 = (bf16[128,2048]{1,0:T(8,128)(2,1)S(1)}, bf16[128,2048]{1,0:T(8,128)(2,1)S(1)}, u32[]{:S(2)}, u32[]{:S(2)}) collective-permute-start(bf16[128,2048]{1,0:T(8,128)(2,1)S(1)} %add_convert_fusion.2), channel_id=1, source_target_pairs={{0,8},{8,16},{16,24},{24,0},{1,9},{9,17},{17,25},{25,1},{2,10},{10... | collective-permute-start | bytes 1572872 | tf_op jit(solution)/shard_map/ppermute | solution.py:34
  154.7 24.6 %collective-permute-start.18 = (bf16[128,2048]{1,0:T(8,128)(2,1)}, bf16[128,2048]{1,0:T(8,128)(2,1)}, u32[]{:S(2)}, u32[]{:S(2)}) collective-permute-start(bf16[128,2048]{1,0:T(8,128)(2,1)} %add_convert_fusion.1), channel_id=1, source_target_pairs={{0,24},{8,0},{16,8},{24,16},{1,25},{9,1},{17,9},{25,17},{2,26},{10... | collective-permute-start | bytes 1572872 | tf_op jit(solution)/shard_map/ppermute | solution.py:34
  158.7 22.6 %collective-permute-start.21 = (bf16[64,128]{1,0:T(8,128)(2,1)}, bf16[64,128]{1,0:T(8,128)(2,1)}, u32[]{:S(2)}, u32[]{:S(2)}) collective-permute-start(bf16[64,128]{1,0:T(8,128)(2,1)} %fusion.47), channel_id=1, source_target_pairs={{0,1},{1,0},{2,3},{3,2},{4,5},{5,4},{6,7},{7,6},{8,9},{9,8},{10,11... | collective-permute-start | bytes 49160 | tf_op jit(solution)/shard_map/ppermute | solution.py:29
  172.9 13.9 %collective-permute-start.20 = (bf16[128,2048]{1,0:T(8,128)(2,1)}, bf16[128,2048]{1,0:T(8,128)(2,1)S(1)}, u32[]{:S(2)}, u32[]{:S(2)}) collective-permute-start(bf16[128,2048]{1,0:T(8,128)(2,1)} %get-tuple-element.106.refs_10_), channel_id=1, source_target_pairs={{0,1},{1,0},{2,3},{3,2},{4,5},{5,4},{6,7},{7,6},{8,9},{9,8},{10,11... | collective-permute-start | bytes 1572872 | tf_op jit(solution)/shard_map/ppermute | solution.py:29
  180.7 13.9 %collective-permute-start.19 = (bf16[128,2048]{1,0:T(8,128)(2,1)S(1)}, bf16[128,2048]{1,0:T(8,128)(2,1)S(1)}, u32[]{:S(2)}, u32[]{:S(2)}) collective-permute-start(bf16[128,2048]{1,0:T(8,128)(2,1)S(1)} %add_convert_fusion), channel_id=1, source_target_pairs={{0,24},{8,0},{16,8},{24,16},{1,25},{9,1},{17,9},{25,17},{2,26},{10... | collective-permute-start | bytes 1572872 | tf_op jit(solution)/shard_map/ppermute | solution.py:34
  196.2 16.1 %collective-permute-start.22 = (bf16[144,2048]{1,0:T(8,128)(2,1)S(1)}, bf16[144,2048]{1,0:T(8,128)(2,1)S(1)}, u32[]{:S(2)}, u32[]{:S(2)}) collective-permute-start(bf16[144,2048]{1,0:T(8,128)(2,1)S(1)} %get-tuple-element.112), channel_id=1, source_target_pairs={{0,2},{1,3},{2,0},{3,1},{4,6},{5,7},{6,4},{7,5},{8,10},{9,11},{10,... | collective-permute-start | bytes 1769480 | tf_op jit(solution)/shard_map/ppermute | solution.py:29
  197.9 28.1 %collective-permute-start.23 = (bf16[144,2048]{1,0:T(8,128)(2,1)S(1)}, bf16[144,2048]{1,0:T(8,128)(2,1)S(1)}, u32[]{:S(2)}, u32[]{:S(2)}) collective-permute-start(bf16[144,2048]{1,0:T(8,128)(2,1)S(1)} %get-tuple-element.113), channel_id=1, source_target_pairs={{0,4},{1,5},{2,6},{3,7},{4,0},{5,1},{6,2},{7,3},{8,12},{9,13},{10,... | collective-permute-start | bytes 1769480 | tf_op jit(solution)/shard_map/ppermute | solution.py:29
  199.4 26.6 %collective-permute-start.24 = (bf16[144,2048]{1,0:T(8,128)(2,1)S(1)}, bf16[144,2048]{1,0:T(8,128)(2,1)S(1)}, u32[]{:S(2)}, u32[]{:S(2)}) collective-permute-start(bf16[144,2048]{1,0:T(8,128)(2,1)S(1)} %get-tuple-element.114), channel_id=1, source_target_pairs={{0,6},{1,7},{2,4},{3,5},{4,2},{5,3},{6,0},{7,1},{8,14},{9,15},{10,... | collective-permute-start | bytes 1769480 | tf_op jit(solution)/shard_map/ppermute | solution.py:29
  236.2 14.1 %collective-permute-start.29 = (bf16[128,512]{1,0:T(8,128)(2,1)S(1)}, bf16[128,512]{1,0:T(8,128)(2,1)S(1)}, u32[]{:S(2)}, u32[]{:S(2)}) collective-permute-start(bf16[128,512]{1,0:T(8,128)(2,1)S(1)} %pad_maximum_fusion.6), channel_id=1, source_target_pairs={{0,24},{8,0},{16,8},{24,16},{1,25},{9,1},{17,9},{25,17},{2,26},{10... | collective-permute-start | bytes 393224 | tf_op jit(solution)/shard_map/ppermute | solution.py:34
  (36 other events, 304.0 us)
